TPU v7x, 32 devices: a whole 2x2x4 slice. The times are simulated.
32 devices in a mesh: dp: 4 (over z), tensor: 4 (over y, x), ctx: 2 (over core).
Axes of the slice: x: 2, y: 2, z: 4, core: 2. Of those that a mesh axis runs over, the one named last changes fastest.
Arguments:
- tokens: bfloat16 [4, 1024, 768], P('dp', ('ctx', 'tensor')), may hold values from -6 to 6
- lengths: int32 [4, 4], P('dp'), may hold values from 32 to 768, as said below
- norm1_gain: float32 [768], replicated, may hold values from 0.25 to 1.75
- norm1_shift: float32 [768], replicated, may hold values from -1.75 to 1.75
- qkv_weight: bfloat16 [768, 3, 768], P(None, None, 'tensor'), may hold values from -0.3125 to 0.3125
- query_bias: float32 [768], P('tensor'), may hold values from -3 to 3
- value_bias: float32 [768], P('tensor'), may hold values from -3 to 3
- output_projection_weight: bfloat16 [768, 768], P('tensor'), may hold values from -1.25 to 1.25
- out_bias: float32 [768], replicated, may hold values from -1.75 to 1.75
- norm2_gain: float32 [768], replicated, may hold values from 0.25 to 1.75
- norm2_shift: float32 [768], replicated, may hold values from -1.75 to 1.75
- up_projection_weight: bfloat16 [768, 3072], P(None, 'tensor'), may hold values from -0.21875 to 0.21875
- up_projection_bias: float32 [3072], P('tensor'), may hold values from -3 to 3
- down_projection_weight: bfloat16 [3072, 768], P('tensor'), may hold values from -0.15625 to 0.15625
- down_bias: float32 [768], replicated, may hold values from -1.75 to 1.75
- cotangent: bfloat16 [4, 1024, 768], P('dp', ('ctx', 'tensor')), may hold values from -6 to 6
Outputs:
- output: bfloat16 [4, 1024, 768], P('dp', ('ctx', 'tensor'))
- input_grad: bfloat16 [4, 1024, 768], P('dp', ('ctx', 'tensor'))
- norm1_gain_grad: float32 [768], replicated
- norm1_shift_grad: float32 [768], replicated
- qkv_weight_grad: float32 [768, 3, 768], P(None, None, 'tensor')
- query_bias_grad: float32 [768], P('tensor')
- value_bias_grad: float32 [768], P('tensor')
- out_weight_grad: float32 [768, 768], P('tensor')
- out_bias_grad: float32 [768], replicated
- norm2_gain_grad: float32 [768], replicated
- norm2_shift_grad: float32 [768], replicated
- up_weight_grad: float32 [768, 3072], P(None, 'tensor')
- up_bias_grad: float32 [3072], P('tensor')
- down_weight_grad: float32 [3072, 768], P('tensor')
- down_bias_grad: float32 [768], replicated
Inputs may be any that keep to these rules, and one draw needn't show every extreme that they name: In each sequence the 4 documents lie in order and their lengths sum to 1024; the second document holds exactly 768 tokens and begins at a position from 64 to 128.
All inputs are finite; a program needn't handle non-finite values.
Results may differ from a plain program's by a relative error of at most 0.013.
The roundings to bfloat16 on the way count: a program that leaves them out, or rounds other values in their place, can miss the bound.
Values may be sent and summed in bfloat16 or wider, within the bound.
No kernel may reach another device: no remote copies, remote signals or barrier semaphores. Data moves between devices by JAX's collectives and lax.ppermute only.
A program may use at most 128 MiB of HBM per device.

v0:
```python
import jax
import jax.numpy as jnp
from jax import lax
from jax.sharding import PartitionSpec as P

HEAD_DIM = 64


norm_epsilon = 1e-05
masked_fill = -1e30


def layer_norm(values, norm_gain, offset):
    center = values - jnp.mean(values, axis=-1, keepdims=True)
    spread = jnp.mean(center * center, axis=-1, keepdims=True)
    return center * lax.rsqrt(spread + norm_epsilon) * norm_gain + offset


def gelu_tanh(values):
    inner = 0.7978845608028654 * (values + 0.044715 * values * values * values)
    return 0.5 * values * (1.0 + jnp.tanh(inner))


def segment_ids(lengths, length_all):
    bounds = jnp.cumsum(lengths, axis=-1)[..., :-1]
    places = jnp.arange(length_all, dtype=jnp.int32)
    return jnp.sum((places[:, None] >= bounds[..., None, :]).astype(jnp.int32), axis=-1)


def score_block(queries, key_heads, allowed):
    dot_raw = jnp.einsum("sqhe,skhe->shqk", queries, key_heads, preferred_element_type=jnp.float32)
    return jnp.where(allowed[:, None], dot_raw * HEAD_DIM ** (-0.5), masked_fill)


def per_device(
    tokens,
    lengths,
    norm1_gain,
    norm1_shift,
    qkv_weight,
    query_bias,
    value_bias,
    output_projection_weight,
    out_bias,
    norm2_gain,
    norm2_shift,
    up_projection_weight,
    up_projection_bias,
    down_projection_weight,
    down_bias,
    cotangent,
):
    seq_count, own_rows, model_width = tokens.shape
    local_width = qkv_weight.shape[2]
    local_heads = local_width // HEAD_DIM
    half_rows = own_rows * lax.axis_size("tensor")
    full_rows = half_rows * lax.axis_size("ctx")
    head_shape = (seq_count, half_rows, local_heads, HEAD_DIM)
    key_shape = (seq_count, full_rows, local_heads, HEAD_DIM)
    flat_shape = (seq_count, half_rows, local_width)
    row_axes = (0, 1)
    score_scale = HEAD_DIM ** (-0.5)
    inputs = tokens.astype(jnp.float32)
    normed_one = layer_norm(inputs, norm1_gain, norm1_shift).astype(jnp.bfloat16)
    first_rows = lax.all_gather(normed_one, "tensor", axis=1, tiled=True)
    flat_query_key_value = qkv_weight.reshape(model_width, 3 * local_width)
    projected_rows = jnp.einsum(
        "fug,gk->fuk", first_rows, flat_query_key_value, preferred_element_type=jnp.float32
    )
    projected_rows = projected_rows.reshape(seq_count, half_rows, 3, local_width)
    queries = (projected_rows[:, :, 0] + query_bias).astype(jnp.bfloat16)
    key_rows = projected_rows[:, :, 1].astype(jnp.bfloat16)
    value_rows = (projected_rows[:, :, 2] + value_bias).astype(jnp.bfloat16)
    all_keys, all_values = (
        lax.all_gather(key_rows, "ctx", axis=1, tiled=True),
        lax.all_gather(value_rows, "ctx", axis=1, tiled=True),
    )
    query_heads = queries.reshape(head_shape)
    key_heads = all_keys.reshape(key_shape)
    value_heads = all_values.reshape(key_shape)
    segment = segment_ids(lengths, full_rows)
    first_row = lax.axis_index("ctx") * half_rows
    query_place = first_row + jnp.arange(half_rows, dtype=jnp.int32)
    key_place = jnp.arange(full_rows, dtype=jnp.int32)
    query_segment = lax.dynamic_slice_in_dim(segment, first_row, half_rows, 1)
    allowed = (key_place[None, None, :] <= query_place[None, :, None]) & (
        query_segment[:, :, None] == segment[:, None, :]
    )
    scores = score_block(query_heads, key_heads, allowed)
    row_max = jnp.max(scores, axis=-1, keepdims=True)
    powers = jnp.exp(scores - row_max)
    row_total = jnp.sum(powers, axis=-1, keepdims=True)
    weights = powers / row_total
    log_total = row_max + jnp.log(row_total)
    attention_mixture = jnp.einsum(
        "shqk,skhe->sqhe",
        weights.astype(jnp.bfloat16),
        value_heads,
        preferred_element_type=jnp.float32,
    )
    mixture_reduced = attention_mixture.astype(jnp.bfloat16).reshape(flat_shape)
    branch_part = jnp.einsum(
        "tfb,bu->tfu", mixture_reduced, output_projection_weight, preferred_element_type=jnp.float32
    )
    branch_output = (
        lax.psum_scatter(branch_part, "tensor", scatter_dimension=1, tiled=True) + out_bias
    )
    hidden_state = inputs + branch_output
    second_normalized = layer_norm(hidden_state, norm2_gain, norm2_shift).astype(jnp.bfloat16)
    second_rows = lax.all_gather(second_normalized, "tensor", axis=1, tiled=True)
    up_projected = (
        jnp.einsum(
            "mvg,gw->mvw", second_rows, up_projection_weight, preferred_element_type=jnp.float32
        )
        + up_projection_bias
    )
    activated_reduced = gelu_tanh(up_projected).astype(jnp.bfloat16)
    down_part = jnp.einsum(
        "rcn,nu->rcu", activated_reduced, down_projection_weight, preferred_element_type=jnp.float32
    )
    output = (
        hidden_state
        + lax.psum_scatter(down_part, "tensor", scatter_dimension=1, tiled=True)
        + down_bias
    ).astype(jnp.bfloat16)
    seed_grad = cotangent.astype(jnp.float32)
    down_bias_grad = jnp.sum(seed_grad, axis=row_axes)
    starting_rows = lax.all_gather(cotangent, "tensor", axis=1, tiled=True)
    down_weight_grad = jnp.einsum(
        "vuy,vuw->yw", activated_reduced, starting_rows, preferred_element_type=jnp.float32
    )
    active_grad = jnp.einsum(
        "pqi,ri->pqr", starting_rows, down_projection_weight, preferred_element_type=jnp.float32
    )
    _, gelu_pull = jax.vjp(gelu_tanh, up_projected)
    up_gradient_rows = gelu_pull(active_grad)[0].astype(jnp.bfloat16)
    up_bias_grad = jnp.sum(up_gradient_rows, axis=row_axes, dtype=jnp.float32)
    up_weight_grad = jnp.einsum(
        "upy,upt->yt", second_rows, up_gradient_rows, preferred_element_type=jnp.float32
    )
    normed_two_part = jnp.einsum(
        "rzo,ao->rza", up_gradient_rows, up_projection_weight, preferred_element_type=jnp.float32
    )
    normed_two_grad = lax.psum_scatter(normed_two_part, "tensor", scatter_dimension=1, tiled=True)
    _, norm_two_pull = jax.vjp(layer_norm, hidden_state, norm2_gain, norm2_shift)
    hidden_part, norm2_gain_grad, norm2_shift_grad = norm_two_pull(normed_two_grad)
    hidden_grad = seed_grad + hidden_part
    branch_grad = hidden_grad.astype(jnp.bfloat16)
    out_bias_grad = jnp.sum(branch_grad, axis=row_axes, dtype=jnp.float32)
    branch_output_rows = lax.all_gather(branch_grad, "tensor", axis=1, tiled=True)
    out_weight_grad = jnp.einsum(
        "ixy,ixb->yb", mixture_reduced, branch_output_rows, preferred_element_type=jnp.float32
    )
    mixture_grad = jnp.einsum(
        "mao,io->mai",
        branch_output_rows,
        output_projection_weight,
        preferred_element_type=jnp.float32,
    )
    mixture_grad = mixture_grad.astype(jnp.bfloat16).reshape(head_shape)
    weights_back = jnp.exp(score_block(query_heads, key_heads, allowed) - log_total)
    weight_grad = jnp.einsum(
        "sqhe,skhe->shqk", mixture_grad, value_heads, preferred_element_type=jnp.float32
    )
    value_part = jnp.einsum(
        "shqk,sqhe->skhe",
        weights_back.astype(jnp.bfloat16),
        mixture_grad,
        preferred_element_type=jnp.float32,
    )
    center = jnp.sum(weights_back * weight_grad, axis=-1, keepdims=True)
    score_grad = (weights_back * (weight_grad - center)).astype(jnp.bfloat16)
    query_grad = jnp.einsum(
        "shqk,skhe->sqhe", score_grad, key_heads, preferred_element_type=jnp.float32
    )
    query_grad = (query_grad * score_scale).astype(jnp.bfloat16).reshape(flat_shape)
    key_part = (
        jnp.einsum("shqk,sqhe->skhe", score_grad, query_heads, preferred_element_type=jnp.float32)
        * score_scale
    )
    key_sum, value_sum = (
        lax.psum_scatter(key_part, "ctx", scatter_dimension=1, tiled=True),
        lax.psum_scatter(value_part, "ctx", scatter_dimension=1, tiled=True),
    )
    key_grad = key_sum.astype(jnp.bfloat16).reshape(flat_shape)
    value_grad = value_sum.astype(jnp.bfloat16).reshape(flat_shape)
    query_bias_grad = jnp.sum(query_grad, axis=row_axes, dtype=jnp.float32)
    value_bias_grad = jnp.sum(value_grad, axis=row_axes, dtype=jnp.float32)
    stacked_rows = jnp.stack([query_grad, key_grad, value_grad], axis=2).reshape(
        seq_count, half_rows, 3 * local_width
    )
    qkv_weight_grad = jnp.einsum(
        "kfz,kfm->zm", first_rows, stacked_rows, preferred_element_type=jnp.float32
    )
    qkv_weight_grad = qkv_weight_grad.reshape(model_width, 3, local_width)
    normed_one_part = jnp.einsum(
        "orj,aj->ora", stacked_rows, flat_query_key_value, preferred_element_type=jnp.float32
    )
    normed_one_grad = lax.psum_scatter(normed_one_part, "tensor", scatter_dimension=1, tiled=True)
    _, norm_one_pull = jax.vjp(layer_norm, inputs, norm1_gain, norm1_shift)
    input_part, norm1_gain_grad, norm1_shift_grad = norm_one_pull(normed_one_grad)
    input_grad = (hidden_grad + input_part).astype(jnp.bfloat16)
    (
        qkv_weight_grad,
        query_bias_grad,
        value_bias_grad,
        out_weight_grad,
        up_weight_grad,
        up_bias_grad,
        down_weight_grad,
    ) = lax.psum(
        (
            qkv_weight_grad,
            query_bias_grad,
            value_bias_grad,
            out_weight_grad,
            up_weight_grad,
            up_bias_grad,
            down_weight_grad,
        ),
        ("dp", "ctx"),
    )
    (
        norm1_gain_grad,
        norm1_shift_grad,
        out_bias_grad,
        norm2_gain_grad,
        norm2_shift_grad,
        down_bias_grad,
    ) = lax.psum(
        (
            norm1_gain_grad,
            norm1_shift_grad,
            out_bias_grad,
            norm2_gain_grad,
            norm2_shift_grad,
            down_bias_grad,
        ),
        ("dp", "tensor", "ctx"),
    )
    return (
        output,
        input_grad,
        norm1_gain_grad,
        norm1_shift_grad,
        qkv_weight_grad,
        query_bias_grad,
        value_bias_grad,
        out_weight_grad,
        out_bias_grad,
        norm2_gain_grad,
        norm2_shift_grad,
        up_weight_grad,
        up_bias_grad,
        down_weight_grad,
        down_bias_grad,
    )


def solution(mesh):
    return jax.shard_map(
        per_device,
        mesh=mesh,
        in_specs=(
            P("dp", ("ctx", "tensor"), None),
            P("dp", None),
            P(),
            P(),
            P(None, None, "tensor"),
            P("tensor"),
            P("tensor"),
            P("tensor", None),
            P(),
            P(),
            P(),
            P(None, "tensor"),
            P("tensor"),
            P("tensor", None),
            P(),
            P("dp", ("ctx", "tensor"), None),
        ),
        out_specs=(
            P("dp", ("ctx", "tensor"), None),
            P("dp", ("ctx", "tensor"), None),
            P(),
            P(),
            P(None, None, "tensor"),
            P("tensor"),
            P("tensor"),
            P("tensor", None),
            P(),
            P(),
            P(),
            P(None, "tensor"),
            P("tensor"),
            P("tensor", None),
            P(),
        ),
        check_vma=False,
    )
```

profile of v0, /device:TPU:0, one launch (start us, length us, event | category | flops | bytes accessed | tf_op | source)
XLA Modules:
  0.0 406.1 jit_solution(14586138814971938736)
XLA Ops:
  7.3 1.2 convert_reduce_fusion.1
  8.5 1.1 fusion.47
  9.6 0.5 copy-done.50
  10.1 1.1 fusion.45
  11.2 12.7 %all_gather.18 = bf16[1,512,768]{2,1,0:T(8,128)(2,1)S(1)} all-gather(bf16[1,128,768]{2,1,0:T(8,128)(2,1)S(1)} %fusion.45), channel_id=1, replica_groups=mesh['dp'=4,'tensor'=4,'ctx'=2] {'tensor'}, dimensions={1}, use_global_device_ids=true | all-gather | bytes 983040 | tf_op jit(solution)/shard_map/all_gather | solution.py:65
  23.9 0.7 convolution_bitcast_fusion.4
  24.6 0.2 copy-done.12
  24.9 2.1 all-gather
  27.5 2.1 all_gather.19
  29.6 0.5 fusion.7
  30.2 1.5 fusion.62
  31.7 1.5 fusion
  33.2 1.1 copy-done.1
  34.3 1.7 fusion.20
  36.0 0.7 copy-done.26
  36.7 1.6 convolution_bitcast_fusion.1
  38.4 16.4 %all_gather.22 = bf16[1,512,768]{2,1,0:T(8,128)(2,1)S(1)} all-gather(bf16[1,128,768]{2,1,0:T(8,128)(2,1)S(1)} %copy-done.16), channel_id=1, replica_groups=mesh['dp'=4,'tensor'=4,'ctx'=2] {'tensor'}, dimensions={1}, use_global_device_ids=true | all-gather | bytes 983040 | tf_op jit(solution)/shard_map/all_gather | solution.py:128
  54.7 18.3 %reduce-scatter.7.cloned.1.call-done = f32[1,128,768]{2,1,0:T(8,128)} async-done(((f32[1,512,768]{2,1,0:T(8,128)}), f32[1,128,768]{2,1,0:T(8,128)}) %reduce-scatter.7.cloned.1.call-update) | async-done | bytes 393232 | tf_op jit(solution)/shard_map/reduce_scatter | solution.py:106
  73.1 1.2 fusion.61
  74.5 0.3 copy-done.36
  74.8 0.2 copy-done.52
  75.2 0.4 copy-done.40
  75.6 11.1 %all_gather.21 = bf16[1,512,768]{2,1,0:T(8,128)(2,1)S(1)} all-gather(bf16[1,128,768]{2,1,0:T(8,128)(2,1)S(1)} %add_convert_fusion.2), channel_id=1, replica_groups=mesh['dp'=4,'tensor'=4,'ctx'=2] {'tensor'}, dimensions={1}, use_global_device_ids=true | all-gather | bytes 983040 | tf_op jit(solution)/shard_map/all_gather | solution.py:110
  86.7 0.8 convolution_add_fusion
  87.5 2.4 convert_reduce_fusion
  90.0 0.9 copy-done.25
  90.8 2.0 convolution_bitcast_fusion.2
  92.9 3.6 convolution_bitcast_fusion.3
  96.6 0.6 copy-done.32
  97.2 26.7 %reduce-scatter.11.cloned.1.call-done = f32[1,128,768]{2,1,0:T(8,128)} async-done(((f32[1,512,768]{2,1,0:T(8,128)}), f32[1,128,768]{2,1,0:T(8,128)}) %reduce-scatter.11.cloned.1.call-update) | async-done | bytes 393232 | tf_op jit(solution)/shard_map/reduce_scatter | solution.py:144
  123.9 1.2 multiply_reduce_fusion.1
  125.2 33.2 %reduce-scatter.9.cloned.1.call-done = f32[1,128,768]{2,1,0:T(8,128)} async-done(((f32[1,512,768]{2,1,0:T(8,128)}), f32[1,128,768]{2,1,0:T(8,128)}) %reduce-scatter.9.cloned.1.call-update) | async-done | bytes 393232 | tf_op jit(solution)/shard_map/reduce_scatter | solution.py:123
  158.4 2.0 fusion.60
  160.6 0.6 copy-done.10
  161.2 11.3 %all_gather.23 = bf16[1,512,768]{2,1,0:T(8,128)(2,1)S(1)} all-gather(bf16[1,128,768]{2,1,0:T(8,128)(2,1)S(1)} %get-tuple-element.38), channel_id=1, replica_groups=mesh['dp'=4,'tensor'=4,'ctx'=2] {'tensor'}, dimensions={1}, use_global_device_ids=true | all-gather | bytes 983040 | tf_op jit(solution)/shard_map/all_gather | solution.py:150
  172.5 0.4 convolution_convert_fusion
  172.9 4.8 %fusion.15 = f32[1,1024,3,64]{1,3,2,0:T(8,128)} fusion(bf16[512,3,64]{0,2,1:T(8,128)(2,1)S(1)} %bitcast.108, f32[3,512,1024]{2,1,0:T(8,128)} %copy-done.1, f32[3,512]{1,0:T(4,128)S(1)} %log_add_fusion), kind=kOutput, calls=%fused_computation.32 | convolution fusion | flops 204472320 | bytes 7280640 | tf_op jit(solution)/shard_map/shqk,sqhe->skhe/dot_general | solution.py:165
  177.8 3.9 multiply_reduce_fusion
  181.8 3.9 multiply_convert_fusion
  185.6 1.6 copy-done.2
  187.3 1.6 fusion.18
  189.0 3.6 convert_reduce_fusion.5
  192.6 1.7 convert_reduce_fusion.4
  194.3 4.1 reduce-scatter.13.cloned.1.call-done
  198.4 1.1 convert_element_type.151
  199.5 1.1 pad_maximum_fusion
  200.5 2.0 convolution_bitcast_fusion
  202.6 3.5 fusion.31
  206.1 2.3 fusion.25
  208.5 1.1 fusion.22
  209.7 1.8 fusion.34
  211.7 0.5 copy-done.35
  212.3 17.9 %all-reduce.1 = (f32[192]{0:T(256)}, f32[192]{0:T(256)}, f32[768]{0:T(1024)}) all-reduce(f32[192]{0:T(256)S(1)} %reduce_sum.205, f32[192]{0:T(256)S(1)} %reduce_sum.210, f32[768]{0:T(1024)S(1)} %copy-done.45), channel_id=1, replica_groups=mesh['dp'=4,'tensor'=4,'ctx'=2] {'dp','ctx'}, use_global_device_ids=true, to_apply=%region_25.26 | all-reduce | flops 1152 | bytes 9216 | tf_op jit(solution)/shard_map/psum | solution.py:211
  230.2 4.6 %reduce-scatter.17.cloned.1.call-done = f32[1,128,768]{2,1,0:T(8,128)} async-done(((f32[1,512,768]{2,1,0:T(8,128)}), f32[1,128,768]{2,1,0:T(8,128)}) %reduce-scatter.17.cloned.1.call-update) | async-done | bytes 393232 | tf_op jit(solution)/shard_map/reduce_scatter | solution.py:199
  234.8 1.2 fusion.58
  236.0 1.3 fusion.46
  237.3 1.9 convert_reduce_fusion.2
  239.2 41.5 %all-reduce = (f32[768]{0:T(1024)}, f32[768]{0:T(1024)}, f32[768]{0:T(1024)}, f32[768]{0:T(1024)}, f32[768]{0:T(1024)}, /*index=5*/f32[768]{0:T(1024)}) all-reduce(f32[768]{0:T(1024)S(1)} %get-tuple-element.17, f32[768]{0:T(1024)S(1)} %get-tuple-element.20, ...), channel_id=1, replica_groups=mesh['dp'=4,'tensor'=4,'ctx'=2] {'dp','tensor','ctx'}, use_global_device_ids=true, to_apply=%region_20.21 | all-reduce | flops 4608 | bytes 36864 | tf_op jit(solution)/shard_map/psum | solution.py:230
  280.8 110.8 %all-reduce.5.cloned.1.call-done = (f32[768,3,192]{0,2,1:T(8,128)}, f32[192,768]{1,0:T(8,128)}, f32[768,768]{1,0:T(8,128)}, f32[768,768]{1,0:T(8,128)}) async-done(((f32[768,3,192]{0,2,1:T(8,128)}, f32[192,768]{1,0:T(8,128)}, f32[768,768]{1,0:T(8,128)}, f32[768,768]{1,0:T(8,128)}), (f32[768,3,192]{0,2,1:T(8,128)}, f32[192,768]{1,0:T(8,128)}, f32[768,768]{1,0:T(8,128)}, ...) | async-done | bytes 7077904 | tf_op jit(solution)/shard_map/psum | solution.py:211
  391.6 2.9 copy.35
  394.6 0.8 copy.36
  395.4 1.4 copy.37
  396.8 1.1 copy-done.14
  397.9 1.4 copy.38
  (143 shorter events, 2.0 us)
Async XLA Ops:
  7.2 80.3 %copy-start = (bf16[768,768]{1,0:T(8,128)(2,1)S(1)}, bf16[768,768]{1,0:T(8,128)(2,1)}, u32[]{:S(2)}) copy-start(bf16[768,768]{1,0:T(8,128)(2,1)} %param.29) | copy-start | bytes 3538948
  7.2 16.7 %copy-start.8 = (bf16[768,3,192]{0,2,1:T(8,128)(2,1)S(1)}, bf16[768,3,192]{0,2,1:T(8,128)(2,1)}, u32[]{:S(2)}) copy-start(bf16[768,3,192]{0,2,1:T(8,128)(2,1)} %param.20) | copy-start | bytes 2654212
  7.2 65.9 %reduce-scatter.7.cloned.1.call-start = ((), (), s32[]{:S(2)}) async-start(), calls=%async_computation.6 | async-start | bytes 1966080 | tf_op jit(solution)/shard_map/reduce_scatter | solution.py:106
  8.4 2.8 copy-start.33
  9.6 0.5 copy-start.50
  10.1 1.1 copy-start.38
  23.9 1.0 copy-start.12
  24.6 2.4 copy-start.56
  24.6 2.7 copy-start.49
  24.6 2.8 copy-start.48
  24.9 6.8 %copy-start.6 = (f32[1,512,1,192]{1,3,2,0:T(8,128)}, f32[1,512,1,192]{1,3,2,0:T(8,128)S(1)}, u32[]{:S(2)}) copy-start(f32[1,512,1,192]{1,3,2,0:T(8,128)S(1)} %slice.18) | copy-start | bytes 1179652
  27.0 4.7 %copy-start.4 = (bf16[1,1024,1,192]{1,3,2,0:T(8,128)(2,1)}, bf16[1,1024,1,192]{1,3,2,0:T(8,128)(2,1)S(1)}, u32[]{:S(2)}) copy-start(bf16[1,1024,1,192]{1,3,2,0:T(8,128)(2,1)S(1)} %all-gather) | copy-start | bytes 1179652
  29.6 3.6 copy-start.17
  31.7 2.6 copy-start.1
  33.2 2.8 copy-start.31
  34.3 2.4 copy-start.18
  36.0 0.7 copy-start.26
  36.7 1.7 copy-start.16
  38.2 34.8 %copy-start.3 = (bf16[1,128,768]{2,1,0:T(8,128)(2,1)S(1)}, bf16[1,128,768]{2,1,0:T(8,128)(2,1)}, u32[]{:S(2)}) copy-start(bf16[1,128,768]{2,1,0:T(8,128)(2,1)} %param.16) | copy-start | bytes 589828
  38.2 34.8 %copy-start.42 = (f32[768]{0:T(1024)S(1)}, f32[768]{0:T(1024)}, u32[]{:S(2)}) copy-start(f32[768]{0:T(1024)} %param.24) | copy-start | bytes 9220
  38.3 36.8 %copy-start.30 = (f32[768]{0:T(1024)S(1)}, f32[768]{0:T(1024)}, u32[]{:S(2)}) copy-start(f32[768]{0:T(1024)} %param.25) | copy-start | bytes 9220
  38.3 36.8 %copy-start.43 = (f32[768]{0:T(1024)S(1)}, f32[768]{0:T(1024)}, u32[]{:S(2)}) copy-start(f32[768]{0:T(1024)} %param.26) | copy-start | bytes 9220
  38.3 85.6 %reduce-scatter.11.cloned.1.call-start = ((), (), s32[]{:S(2)}) async-start(), calls=%async_computation.8 | async-start | bytes 1966080 | tf_op jit(solution)/shard_map/reduce_scatter | solution.py:144
  54.7 32.7 %copy-start.23 = (bf16[1,512,768]{2,1,0:T(8,128)(2,1)}, bf16[1,512,768]{2,1,0:T(8,128)(2,1)S(1)}, u32[]{:S(2)}) copy-start(bf16[1,512,768]{2,1,0:T(8,128)(2,1)S(1)} %all_gather.22) | copy-start | bytes 2359300
  73.1 13.6 %copy-start.54 = (bf16[768,768]{1,0:T(8,128)(2,1)S(1)}, bf16[768,768]{1,0:T(8,128)(2,1)}, u32[]{:S(2)}) copy-start(bf16[768,768]{1,0:T(8,128)(2,1)} %param.27) | copy-start | bytes 3538948
  73.1 13.6 %copy-start.55 = (f32[768]{0:T(1024)S(1)}, f32[768]{0:T(1024)}, u32[]{:S(2)}) copy-start(f32[768]{0:T(1024)} %param.28) | copy-start | bytes 9220
  74.5 0.5 copy-start.52
  87.5 2.4 copy-start.57
  89.9 0.9 copy-start.25
  92.8 65.6 %reduce-scatter.9.cloned.1.call-start = ((), (), s32[]{:S(2)}) async-start(), calls=%async_computation.7 | async-start | bytes 1966080 | tf_op jit(solution)/shard_map/reduce_scatter | solution.py:123
  96.5 0.7 copy-start.32
  96.5 27.4 %copy-start.37 = (f32[128]{0:T(128)S(1)}, f32[128]{0:T(128)}, u32[]{:S(2)}) copy-start(f32[128]{0:T(128)} %copy-done.36) | copy-start | bytes 1540
  96.5 27.4 %copy-start.41 = (f32[128]{0:T(128)S(1)}, f32[128]{0:T(128)}, u32[]{:S(2)}) copy-start(f32[128]{0:T(128)} %copy-done.40) | copy-start | bytes 1540
  96.5 28.7 %copy-start.53 = (f32[128]{0:T(128)S(1)}, f32[128]{0:T(128)}, u32[]{:S(2)}) copy-start(f32[128]{0:T(128)} %copy-done.52) | copy-start | bytes 1540
  96.5 61.9 %copy-start.44 = (f32[768]{0:T(1024)S(1)}, f32[768]{0:T(1024)}, u32[]{:S(2)}) copy-start(f32[768]{0:T(1024)} %param.30) | copy-start | bytes 9220
  96.6 96.1 %reduce-scatter.15.cloned.1.call-start = ((), (), s32[]{:S(2)}) async-start(), calls=%async_computation.10 | async-start | bytes 1179648 | tf_op jit(solution)/shard_map/reduce_scatter | solution.py:183
  158.4 14.1 %copy-start.19 = (bf16[192,768]{1,0:T(8,128)(2,1)S(1)}, bf16[192,768]{1,0:T(8,128)(2,1)}, u32[]{:S(2)}) copy-start(bf16[192,768]{1,0:T(8,128)(2,1)} %param.23) | copy-start | bytes 884740
  160.4 0.8 copy-start.10
  160.5 17.3 %copy-start.46 = (f32[128]{0:T(128)}, f32[128]{0:T(128)S(1)}, u32[]{:S(2)}) copy-start(f32[128]{0:T(128)S(1)} %negate_multiply_fusion.1) | copy-start | bytes 1540
  177.8 20.6 %reduce-scatter.13.cloned.1.call-start = ((), (), s32[]{:S(2)}) async-start(), calls=%async_computation.9 | async-start | bytes 1179648 | tf_op jit(solution)/shard_map/reduce_scatter | solution.py:182
  181.8 5.5 %copy-start.7 = (f32[1,512,1,192]{1,3,2,0:T(8,128)S(1)}, f32[1,512,1,192]{1,3,2,0:T(8,128)}, u32[]{:S(2)}) copy-start(f32[1,512,1,192]{1,3,2,0:T(8,128)} %copy-done.6) | copy-start | bytes 1179652
  185.6 1.6 copy-start.2
  187.3 1.7 copy-start.5
  188.9 45.9 %reduce-scatter.17.cloned.1.call-start = ((), (), s32[]{:S(2)}) async-start(), calls=%async_computation.11 | async-start | bytes 1966080 | tf_op jit(solution)/shard_map/reduce_scatter | solution.py:199
  198.4 2.2 copy-start.9
  199.5 3.1 copy-start.21
  202.5 189.1 %all-reduce.5.cloned.1.call-start = ((), (), s32[]{:S(2)}) async-start(), calls=%async_computation.12 | async-start | bytes 14155776 | tf_op jit(solution)/shard_map/psum | solution.py:211
  202.6 3.5 copy-start.24
  202.6 3.5 copy-start.58
  206.1 2.4 copy-start.27
  208.5 1.2 copy-start.13
  208.5 1.2 copy-start.20
  208.5 1.2 copy-start.22
  211.5 0.7 copy-start.35
  211.5 0.8 copy-start.45
  211.5 23.3 %copy-start.29 = (f32[768]{0:T(1024)S(1)}, f32[768]{0:T(1024)}, u32[]{:S(2)}) copy-start(f32[768]{0:T(1024)} %param.18) | copy-start | bytes 9220
  211.5 23.3 %copy-start.34 = (f32[128]{0:T(128)S(1)}, f32[128]{0:T(128)}, u32[]{:S(2)}) copy-start(f32[128]{0:T(128)} %copy-done.33) | copy-start | bytes 1540
  211.5 24.4 %copy-start.51 = (f32[128]{0:T(128)S(1)}, f32[128]{0:T(128)}, u32[]{:S(2)}) copy-start(f32[128]{0:T(128)} %copy-done.50) | copy-start | bytes 1540
  211.5 24.5 %copy-start.39 = (f32[128]{0:T(128)S(1)}, f32[128]{0:T(128)}, u32[]{:S(2)}) copy-start(f32[128]{0:T(128)} %copy-done.38) | copy-start | bytes 1540
  211.6 25.7 %copy-start.11 = (f32[1,128,768]{2,1,0:T(8,128)S(1)}, f32[1,128,768]{2,1,0:T(8,128)}, u32[]{:S(2)}) copy-start(f32[1,128,768]{2,1,0:T(8,128)} %copy-done.10) | copy-start | bytes 1179652
  211.6 25.7 %copy-start.47 = (f32[128]{0:T(128)S(1)}, f32[128]{0:T(128)}, u32[]{:S(2)}) copy-start(f32[128]{0:T(128)} %copy-done.46) | copy-start | bytes 1540
  391.6 3.0 copy-start.28
  391.6 3.8 copy-start.15
  395.4 2.5 copy-start.14
  (2 other events, 1.0 us)
Sparse Core Ops, SparseCore 0:
  38.4 34.6 reduce-scatter.6
  93.0 30.9 reduce-scatter.10
  127.5 30.8 reduce-scatter.8
  177.9 8.2 reduce-scatter.14
  189.0 9.2 reduce-scatter.12
  202.7 32.0 reduce-scatter.16
  238.6 152.9 all-reduce.4
where the time goes:
time: 407 us; the launch traced here: 406 us
  waiting for transfers between devices  198 us (49%)
  blocking collectives  115 us (28%)
  matrix products  39.3 us (10%)
  other arithmetic  22.9 us (6%)
  local copies, waits for them, and re-layouts  16 us (4%)
  between operations  14.7 us (4%)
    psum x1, waiting for transfers between devices, per_device(): lax.psum((qkv_weight_grad, query_bias_grad, value_bias_grad, out_weight_g...  111 us
    psum x1, blocking collectives, per_device(): lax.psum((norm1_gain_grad, norm1_shift_grad, out_bias_grad, norm2_gain_gr...  41.5 us
    reduce_scatter x1, waiting for transfers between devices, per_device(): lax.psum_scatter(down_part, 'tensor', scatter_dimension=1, tiled=True)  33.2 us
    reduce_scatter x1, waiting for transfers between devices, per_device(): lax.psum_scatter(normed_two_part, 'tensor', scatter_dimension=1, tiled=True)  26.7 us
    reduce_scatter x1, waiting for transfers between devices, per_device(): lax.psum_scatter(branch_part, 'tensor', scatter_dimension=1, tiled=True)  18.3 us
    psum x1, blocking collectives, per_device(): lax.psum((qkv_weight_grad, query_bias_grad, value_bias_grad, out_weight_g...  17.9 us
    all_gather x1, blocking collectives, per_device(): starting_rows = lax.all_gather(cotangent, 'tensor', axis=1, tiled=True)  16.4 us
    unnamed x122, local copies, waits for them, and re-layouts  15.6 us
  transfers between devices with their start and end apart: 7, of which 6 were waited for; matrix products, arithmetic and copies ran while one was open for 8% of the time, Pallas kernels for 0%

commit v1 on v0

v1 whole, which is shorter than its diff:
```python
import jax
import jax.numpy as jnp
from jax import lax
from jax.sharding import PartitionSpec as P

HEAD_DIM = 64
EPS = 1e-05
MASKED = -1e30
BF16 = jnp.bfloat16
F32 = jnp.float32
SCALE = HEAD_DIM**-0.5


def dot(a, b, ca, cb):
    return lax.dot_general(a, b, (((ca,), (cb,)), ((), ())), preferred_element_type=F32)


def norm_parts(values):
    center = values - jnp.mean(values, axis=-1, keepdims=True)
    scale = lax.rsqrt(jnp.mean(center * center, axis=-1, keepdims=True) + EPS)
    return center * scale, scale


def norm_back(grad, gain, xhat, scale):
    g = grad * gain
    return scale * (
        g - jnp.mean(g, axis=-1, keepdims=True) - xhat * jnp.mean(g * xhat, axis=-1, keepdims=True)
    )


def gelu_tanh(values):
    inner = 0.7978845608028654 * (values + 0.044715 * values * values * values)
    return 0.5 * values * (1.0 + jnp.tanh(inner))


def xor_pairs(count, mask):
    return [(i, i ^ mask) for i in range(count)]


def pick(x, index):
    return lax.dynamic_index_in_dim(x, index, 0, keepdims=False)


def gather_rows(x, axis="tensor"):
    count = lax.axis_size(axis)
    me = lax.axis_index(axis)
    out = jnp.zeros((count,) + x.shape, x.dtype)
    out = lax.dynamic_update_slice_in_dim(out, x[None], me, 0)
    for r in range(1, count):
        got = lax.ppermute(x, axis, xor_pairs(count, r))
        out = lax.dynamic_update_slice_in_dim(out, got[None], me ^ r, 0)
    return out


def scatter_sum(x, axis="tensor"):
    count = lax.axis_size(axis)
    me = lax.axis_index(axis)
    low = x.astype(BF16)
    got = [
        lax.ppermute(pick(low, me ^ r), axis, xor_pairs(count, r)) for r in range(1, count)
    ]
    total = pick(x, me)
    for g in got:
        total = total + g.astype(F32)
    return total


def add_low(a, b):
    return (a.astype(F32) + b.astype(F32)).astype(BF16)


def sum_dp(x):
    count = lax.axis_size("dp")
    if count != 4:
        return lax.psum(x, "dp")
    bit = lax.axis_index("dp") & 1
    near, far = xor_pairs(4, 1), xor_pairs(4, 2)
    part = add_low(pick(x, bit), lax.ppermute(pick(x, 1 - bit), "dp", near))
    part = add_low(part, lax.ppermute(part, "dp", far))
    other = lax.ppermute(part, "dp", near)
    return jnp.where(bit == 0, jnp.stack([part, other]), jnp.stack([other, part]))


def sum_weights(x):
    rows, cols = x.shape
    me = lax.axis_index("ctx")
    pairs = xor_pairs(2, 1)
    x = x.reshape(2, rows // 2, cols)
    part = add_low(pick(x, me), lax.ppermute(pick(x, 1 - me), "ctx", pairs))
    part = sum_dp(part.reshape(2, rows // 4, cols)).reshape(rows // 2, cols)
    other = lax.ppermute(part, "ctx", pairs)
    out = jnp.where(me == 0, jnp.stack([part, other]), jnp.stack([other, part]))
    return out.reshape(rows, cols).astype(F32)


def sum_small(x, axis):
    count = lax.axis_size(axis)
    if count not in (2, 4):
        return lax.psum(x, axis)
    got = [lax.ppermute(x, axis, xor_pairs(count, r)) for r in range(1, count)]
    return sum(got, x)


def segment_ids(lengths, length_all):
    bounds = jnp.cumsum(lengths, axis=-1)[:-1]
    places = jnp.arange(length_all, dtype=jnp.int32)
    return jnp.sum((places[:, None] >= bounds[None, :]).astype(jnp.int32), axis=-1)


def per_device(
    tokens,
    lengths,
    norm1_gain,
    norm1_shift,
    qkv_weight,
    query_bias,
    value_bias,
    out_weight,
    out_bias,
    norm2_gain,
    norm2_shift,
    up_weight,
    up_bias,
    down_weight,
    down_bias,
    cotangent,
):
    tokens, cotangent, lengths = tokens[0], cotangent[0], lengths[0]
    own, width = tokens.shape
    ranks = lax.axis_size("tensor")
    half = own * ranks
    full = half * lax.axis_size("ctx")
    local = qkv_weight.shape[2]
    heads = local // HEAD_DIM
    rank = lax.axis_index("tensor")
    ctx = lax.axis_index("ctx")
    ctx_pairs = xor_pairs(2, 1)
    weight_t = jnp.transpose(qkv_weight, (1, 2, 0)).reshape(3 * local, width)

    rows = lax.all_gather(tokens, "tensor", axis=0, tiled=True).astype(F32)
    cot_rows = gather_rows(cotangent).reshape(half, width)
    half_weight = pick(out_weight.reshape(2, local // 2, width), ctx)
    half_weights = gather_rows(half_weight)
    other_weights = lax.ppermute(half_weights, "ctx", ctx_pairs)
    both = jnp.where(
        ctx == 0,
        jnp.stack([half_weights, other_weights], 1),
        jnp.stack([other_weights, half_weights], 1),
    )
    out_weight_all = both.reshape(ranks * local, width)

    xhat1, scale1 = norm_parts(rows)
    normed1 = (xhat1 * norm1_gain + norm1_shift).astype(BF16)
    qkv = dot(normed1, weight_t, 1, 1)
    queries = (qkv[:, :local] + query_bias).astype(BF16)
    keys = qkv[:, local : 2 * local].astype(BF16)
    values = (qkv[:, 2 * local :] + value_bias).astype(BF16)
    kv = jnp.concatenate([keys, values], 1)
    kv_other = lax.ppermute(kv, "ctx", ctx_pairs)
    kv_all = jnp.where(
        ctx == 0, jnp.concatenate([kv, kv_other], 0), jnp.concatenate([kv_other, kv], 0)
    )
    q_heads = queries.reshape(half, heads, HEAD_DIM)
    k_heads = kv_all[:, :local].reshape(full, heads, HEAD_DIM)
    v_heads = kv_all[:, local:].reshape(full, heads, HEAD_DIM)
    segment = segment_ids(lengths, full)
    q_place = ctx * half + jnp.arange(half, dtype=jnp.int32)
    k_place = jnp.arange(full, dtype=jnp.int32)
    q_segment = lax.dynamic_slice_in_dim(segment, ctx * half, half, 0)
    allowed = (k_place[None, :] <= q_place[:, None]) & (q_segment[:, None] == segment[None, :])

    def score_block():
        raw = jnp.einsum("qhe,khe->hqk", q_heads, k_heads, preferred_element_type=F32)
        return jnp.where(allowed[None], raw * SCALE, MASKED)

    scores = score_block()
    row_max = jnp.max(scores, axis=-1, keepdims=True)
    powers = jnp.exp(scores - row_max)
    row_total = jnp.sum(powers, axis=-1, keepdims=True)
    probs = powers / row_total
    log_total = row_max + jnp.log(row_total)
    mixture = (
        jnp.einsum("hqk,khe->qhe", probs.astype(BF16), v_heads, preferred_element_type=F32)
        .astype(BF16)
        .reshape(half, local)
    )
    mixtures = lax.all_gather(mixture, "tensor", axis=1, tiled=True)

    hidden = rows + dot(mixtures, out_weight_all, 1, 0) + out_bias
    xhat2, scale2 = norm_parts(hidden)
    normed2 = (xhat2 * norm2_gain + norm2_shift).astype(BF16)
    up = dot(normed2, up_weight, 1, 0) + up_bias
    active, gelu_pull = jax.vjp(gelu_tanh, up)
    active = active.astype(BF16)
    up_grad = gelu_pull(dot(cot_rows, down_weight, 1, 1))[0].astype(BF16)
    normed2_part = dot(up_grad, up_weight, 1, 1).reshape(ranks, own, width)
    normed2_grad = scatter_sum(normed2_part)

    down_part = dot(active, down_weight, 1, 0).reshape(ranks, own, width)
    down_grad = sum_weights(dot(active, cot_rows, 0, 0).astype(BF16))
    up_grad_weight = sum_weights(dot(normed2, up_grad, 0, 0).astype(BF16))

    own_hidden = pick(hidden.reshape(ranks, own, width), rank)
    own_xhat2 = pick(xhat2.reshape(ranks, own, width), rank)
    own_scale2 = pick(scale2.reshape(ranks, own, 1), rank)
    norm2_gain_part = jnp.sum(normed2_grad * own_xhat2, axis=0)
    norm2_shift_part = jnp.sum(normed2_grad, axis=0)
    hidden_grad = cotangent.astype(F32) + norm_back(normed2_grad, norm2_gain, own_xhat2, own_scale2)
    branch_grad = hidden_grad.astype(BF16)
    branch_rows = lax.all_gather(branch_grad, "tensor", axis=0, tiled=True)

    mixture_grad = dot(branch_rows, out_weight, 1, 1).astype(BF16).reshape(half, heads, HEAD_DIM)
    probs = jnp.exp(score_block() - log_total)
    prob_grad = jnp.einsum("qhe,khe->hqk", mixture_grad, v_heads, preferred_element_type=F32)
    value_part = jnp.einsum(
        "hqk,qhe->khe", probs.astype(BF16), mixture_grad, preferred_element_type=F32
    )
    center = jnp.sum(probs * prob_grad, axis=-1, keepdims=True)
    score_grad = (probs * (prob_grad - center)).astype(BF16)
    query_grad = jnp.einsum("hqk,khe->qhe", score_grad, k_heads, preferred_element_type=F32)
    query_grad = (query_grad * SCALE).astype(BF16).reshape(half, local)
    key_part = jnp.einsum("hqk,qhe->khe", score_grad, q_heads, preferred_element_type=F32) * SCALE
    kv_part = jnp.concatenate([key_part.reshape(full, local), value_part.reshape(full, local)], 1)
    kv_part = kv_part.reshape(2, half, 2 * local)
    kv_got = lax.ppermute(pick(kv_part, 1 - ctx).astype(BF16), "ctx", ctx_pairs)
    kv_grad = (pick(kv_part, ctx) + kv_got.astype(F32)).astype(BF16)
    grads = jnp.concatenate([query_grad, kv_grad], 1)
    qkv_grad = dot(grads, normed1, 0, 0).astype(BF16)
    out_grad = dot(mixture, branch_rows, 0, 0).astype(BF16)
    attn_grad = sum_weights(jnp.concatenate([qkv_grad, out_grad], 0))
    qkv_weight_grad = jnp.transpose(
        attn_grad[: 3 * local].reshape(3, local, width), (2, 0, 1)
    )
    out_weight_grad = attn_grad[3 * local :]

    normed1_part = dot(grads, weight_t, 1, 0)
    norm1_gain_part = jnp.sum(normed1_part * xhat1, axis=0)
    norm1_shift_part = jnp.sum(normed1_part, axis=0)
    normed1_grad = scatter_sum(normed1_part.reshape(ranks, own, width))
    own_xhat1 = pick(xhat1.reshape(ranks, own, width), rank)
    own_scale1 = pick(scale1.reshape(ranks, own, 1), rank)
    input_grad = hidden_grad + norm_back(normed1_grad, norm1_gain, own_xhat1, own_scale1)
    output = own_hidden + scatter_sum(down_part) + down_bias

    by_rank = sum_small(
        jnp.stack([norm1_gain_part, norm1_shift_part, norm2_gain_part, norm2_shift_part]), "tensor"
    )
    grads_sum = jnp.sum(grads.astype(F32), axis=0)
    bias_row = jnp.concatenate([grads_sum[:local], grads_sum[2 * local :]])
    bias_row = jnp.pad(bias_row, (0, width - 2 * local))
    up_bias_part = jnp.sum(up_grad.astype(F32), axis=0)
    small = jnp.concatenate(
        [
            by_rank,
            jnp.stack(
                [
                    jnp.sum(branch_rows.astype(F32), axis=0),
                    jnp.sum(cot_rows.astype(F32), axis=0),
                    up_bias_part,
                    bias_row,
                ]
            ),
        ],
        0,
    )
    small = sum_small(sum_small(small, "ctx"), "dp")
    return (
        output.astype(BF16)[None],
        input_grad.astype(BF16)[None],
        small[0],
        small[1],
        qkv_weight_grad,
        small[7, :local],
        small[7, local : 2 * local],
        out_weight_grad,
        small[4],
        small[2],
        small[3],
        up_grad_weight,
        small[6],
        down_grad,
        small[5],
    )


def solution(mesh):
    row_spec = P("dp", ("ctx", "tensor"), None)
    return jax.shard_map(
        per_device,
        mesh=mesh,
        in_specs=(
            row_spec,
            P("dp", None),
            P(),
            P(),
            P(None, None, "tensor"),
            P("tensor"),
            P("tensor"),
            P("tensor", None),
            P(),
            P(),
            P(),
            P(None, "tensor"),
            P("tensor"),
            P("tensor", None),
            P(),
            row_spec,
        ),
        out_specs=(
            row_spec,
            row_spec,
            P(),
            P(),
            P(None, None, "tensor"),
            P("tensor"),
            P("tensor"),
            P("tensor", None),
            P(),
            P(),
            P(),
            P(None, "tensor"),
            P("tensor"),
            P("tensor", None),
            P(),
        ),
        check_vma=False,
    )
```

time: 407 us -> 224 us (0.55)
  waiting for transfers between devices: 198 us -> 64.6 us
  blocking collectives: 115 us -> 38.8 us
  starting transfers between devices: 0.29 us -> 39 us
  matrix products: 39.3 us -> 22.1 us
  local copies, waits for them, and re-layouts: 16 us -> 31.1 us
  between operations: 14.7 us -> 1.63 us
    psum x1 -> x0, waiting for transfers between devices: 111 us -> none  [per_device(): lax.psum((qkv_weight_grad, query_bias_grad, value_bias_grad, out_weight_g...]
    reduce_scatter x6 -> x0, waiting for transfers between devices: 87 us -> none  [the longest x1 33.2 us: per_device(): lax.psum_scatter(down_part, 'tensor', scatter_dimension=1, tiled=True)]
    ppermute x0 -> x40, waiting for transfers between devices: none -> 64.6 us  [the longest x3 23.4 us: sum_dp(): other = lax.ppermute(part, 'dp', near)]
    psum x2 -> x0, blocking collectives: 59.4 us -> none  [the longest x1 41.5 us: per_device(): lax.psum((norm1_gain_grad, norm1_shift_grad, out_bias_grad, norm2_gain_gr...]
    ppermute x0 -> x40, starting transfers between devices: none -> 39 us  [the longest x9 10.5 us: scatter_sum(): lax.ppermute(pick(low, me ^ r), axis, xor_pairs(count, r))]
    dot_general x18, matrix products: 39.3 us -> 22.1 us  [the longest x12 13.1 us: dot(): lax.dot_general(a, b, (((ca,), (cb,)), ((), ())), preferred_element_type=...]
    all_gather x6 -> x3, blocking collectives: 55.6 us -> 38.8 us  [the longest x1 15.4 us: per_device(): rows = lax.all_gather(tokens, 'tensor', axis=0, tiled=True).astype(F32)]
    unnamed x122 -> x68, local copies, waits for them, and re-layouts: 15.6 us -> 3.04 us
  transfers between devices with their start and end apart: 7 -> 40, of which waited for: 6 -> 12; matrix products, arithmetic and copies ran while one was open for 8% -> 28% of each run, Pallas kernels for 0% -> 0%
where the time goes in v1:
time: 224 us; the launch traced here: 223 us
  waiting for transfers between devices  64.6 us (29%)
  starting transfers between devices  39 us (17%)
  blocking collectives  38.8 us (17%)
  local copies, waits for them, and re-layouts  31.1 us (14%)
  other arithmetic  25.7 us (11%)
  matrix products  22.1 us (10%)
    ppermute x3, waiting for transfers between devices, sum_dp(): other = lax.ppermute(part, 'dp', near)  23.4 us
    ppermute x3, waiting for transfers between devices, sum_dp(): part = add_low(part, lax.ppermute(part, 'dp', far))  16.2 us
    all_gather x1, blocking collectives, per_device(): rows = lax.all_gather(tokens, 'tensor', axis=0, tiled=True).astype(F32)  15.4 us
    dot_general x12, matrix products, dot(): lax.dot_general(a, b, (((ca,), (cb,)), ((), ())), preferred_element_type=...  13.1 us
    ppermute x3, waiting for transfers between devices, sum_dp(): part = add_low(pick(x, bit), lax.ppermute(pick(x, 1 - bit), 'dp', near))  12 us
    all_gather x1, blocking collectives, per_device(): branch_rows = lax.all_gather(branch_grad, 'tensor', axis=0, tiled=True)  11.7 us
    all_gather x1, blocking collectives, per_device(): mixtures = lax.all_gather(mixture, 'tensor', axis=1, tiled=True)  11.7 us
    ppermute x9, starting transfers between devices, scatter_sum(): lax.ppermute(pick(low, me ^ r), axis, xor_pairs(count, r))  10.5 us
  transfers between devices with their start and end apart: 40, of which 12 were waited for; matrix products, arithmetic and copies ran while one was open for 28% of the time, Pallas kernels for 0%

profile of v1, /device:TPU:0, one launch (start us, length us, event | category | flops | bytes accessed | tf_op | source)
XLA Modules:
  0.0 222.8 jit_solution(442013292502491455)
XLA Ops:
  0.7 1.7 dynamic-slice_bitcast_fusion.15
  2.4 2.9 %collective-permute-start.1 = (bf16[96,768]{1,0:T(8,128)(2,1)}, bf16[96,768]{1,0:T(8,128)(2,1)}, u32[]{:S(2)}, u32[]{:S(2)}) collective-permute-start(bf16[96,768]{1,0:T(8,128)(2,1)} %get-tuple-element.50), channel_id=1, source_target_pairs={{0,2},{2,0},{4,6},{6,4},{1,3},{3,1},{5,7},{7,5},{8,10},{10,8},{12,... | collective-permute-start | bytes 442376 | tf_op jit(solution)/shard_map/ppermute | solution.py:50
  5.3 1.5 collective-permute-start.2
  6.9 2.0 collective-permute-start.8
  8.8 1.5 collective-permute-start.9
  10.4 15.4 %all-gather = bf16[1,512,768]{2,1,0:T(8,128)(2,1)S(1)} all-gather(bf16[1,128,768]{2,1,0:T(8,128)(2,1)} %param.16), channel_id=2, replica_groups=mesh['dp'=4,'tensor'=4,'ctx'=2] {'tensor'}, dimensions={1}, use_global_device_ids=true | all-gather | bytes 983040 | tf_op jit(solution)/shard_map/all_gather | solution.py:140
  26.8 1.3 fusion.7
  28.1 2.1 fusion.62
  32.2 1.0 pad_maximum_fusion.2
  33.3 1.5 collective-permute-start.10
  41.4 1.5 fusion.84
  42.9 1.5 fusion
  44.4 1.7 fusion.29
  46.1 11.7 %all_gather.10 = bf16[512,768]{0,1:T(8,128)(2,1)S(1)} all-gather(bf16[512,192]{0,1:T(8,128)(2,1)S(1)} %bitcast.316), channel_id=1, replica_groups=mesh['dp'=4,'tensor'=4,'ctx'=2] {'tensor'}, dimensions={1}, use_global_device_ids=true | all-gather | bytes 983040 | tf_op jit(solution)/shard_map/all_gather | solution.py:187
  61.5 1.1 fusion.71
  62.6 1.8 convert_reduce_fusion.1
  67.2 1.0 dynamic-slice_bitcast_fusion.14
  68.2 1.5 collective-permute-start.7
  70.8 1.5 collective-permute-start.13
  72.3 1.0 collective-permute-start.12
  76.6 4.7 %collective-permute-done.13 = bf16[128,768]{1,0:T(8,128)(2,1)S(1)} collective-permute-done((bf16[128,768]{1,0:T(8,128)(2,1)S(1)}, bf16[128,768]{1,0:T(8,128)(2,1)S(1)}, u32[]{:S(2)}, u32[]{:S(2)}) %collective-permute-start.13) | collective-permute-done | bytes 196640 | tf_op jit(solution)/shard_map/ppermute | solution.py:60
  82.3 4.9 %collective-permute-done.12 = bf16[128,768]{1,0:T(8,128)(2,1)S(1)} collective-permute-done((bf16[128,768]{1,0:T(8,128)(2,1)S(1)}, bf16[128,768]{1,0:T(8,128)(2,1)S(1)}, u32[]{:S(2)}, u32[]{:S(2)}) %collective-permute-start.12) | collective-permute-done | bytes 196640 | tf_op jit(solution)/shard_map/ppermute | solution.py:60
  89.1 11.7 %all_gather.11 = bf16[512,768]{1,0:T(8,128)(2,1)S(1)} all-gather(bf16[128,768]{1,0:T(8,128)(2,1)S(1)} %get-tuple-element.33), channel_id=1, replica_groups=mesh['dp'=4,'tensor'=4,'ctx'=2] {'tensor'}, dimensions={0}, use_global_device_ids=true | all-gather | bytes 983040 | tf_op jit(solution)/shard_map/all_gather | solution.py:210
  101.2 1.9 multiply_reduce_fusion
  103.1 2.1 fusion.21
  105.2 1.4 multiply_convert_fusion
  107.3 1.1 fusion.28
  108.5 1.6 concatenate.32
  110.1 1.4 copy.34
  111.5 2.7 %concatenate.33 = f32[2,512,192]{1,0,2:T(2,128)} reshape(f32[1024,3,64]{0,2,1:T(8,128)} %fusion.21) | data formatting | bytes 1572864 | tf_op jit(solution)/shard_map/concatenate | solution.py:223
  114.2 2.3 %copy.35 = f32[2,512,192]{2,1,0:T(8,128)} copy(f32[2,512,192]{1,0,2:T(2,128)} %concatenate.33) | data formatting | bytes 1572864 | tf_op jit(solution)/shard_map/concatenate | solution.py:223
  117.2 1.2 fusion.39
  118.6 2.2 fusion.63
  122.3 2.0 multiply_reduce_fusion.1
  124.4 1.5 collective-permute-start.20
  125.9 1.0 collective-permute-start.19
  126.9 1.0 collective-permute-start.18
  128.2 1.1 convolution_convert_fusion.2
  131.1 1.5 collective-permute-start.17
  132.6 1.2 fusion.26
  133.8 1.1 collective-permute-start.16
  134.9 2.0 fusion.25
  137.7 1.3 concatenate.37
  139.0 1.4 collective-permute-done.21
  141.2 3.6 %collective-permute-start.24 = (f32[8,768]{1,0:T(8,128)S(1)}, f32[8,768]{1,0:T(8,128)S(1)}, u32[]{:S(2)}, u32[]{:S(2)}) collective-permute-start(f32[8,768]{1,0:T(8,128)S(1)} %add.318), channel_id=1, source_target_pairs={{0,24},{8,16},{16,8},{24,0},{1,25},{9,17},{17,9},{25,1},{2,26},{10... | collective-permute-start | bytes 73736 | tf_op jit(solution)/shard_map/ppermute | solution.py:100
  145.6 1.1 dynamic-slice_bitcast_fusion.3
  146.8 1.0 collective-permute-start.15
  147.8 1.7 collective-permute-done.23
  150.8 2.0 collective-permute-start.36
  152.9 1.4 fusion.75
  154.2 5.1 %collective-permute-done.31 = bf16[192,768]{1,0:T(8,128)(2,1)S(1)} collective-permute-done((bf16[192,768]{1,0:T(8,128)(2,1)S(1)}, bf16[192,768]{1,0:T(8,128)(2,1)S(1)}, u32[]{:S(2)}, u32[]{:S(2)}) %collective-permute-start.31) | collective-permute-done | bytes 294944 | tf_op jit(solution)/shard_map/ppermute | solution.py:78
  159.4 2.2 collective-permute-start.32
  161.6 6.9 %collective-permute-done.36 = bf16[192,768]{1,0:T(8,128)(2,1)S(1)} collective-permute-done((bf16[192,768]{1,0:T(8,128)(2,1)S(1)}, bf16[192,768]{1,0:T(8,128)(2,1)S(1)}, u32[]{:S(2)}, u32[]{:S(2)}) %collective-permute-start.36) | collective-permute-done | bytes 294944 | tf_op jit(solution)/shard_map/ppermute | solution.py:78
  168.9 2.5 %collective-permute-start.26 = (bf16[192,768]{1,0:T(8,128)(2,1)S(1)}, bf16[192,768]{1,0:T(8,128)(2,1)S(1)}, u32[]{:S(2)}, u32[]{:S(2)}) collective-permute-start(bf16[192,768]{1,0:T(8,128)(2,1)S(1)} %dynamic-slice_bitcast_fusion.5), channel_id=1, source_target_pairs={{0,8},{8,0},{16,24},{24,16},{1,9},{9,1},{17,25},{25,17},{2,10},{10... | collective-permute-start | bytes 884744 | tf_op jit(solution)/shard_map/ppermute | solution.py:78
  171.4 11.5 %collective-permute-done.32 = bf16[192,768]{1,0:T(8,128)(2,1)S(1)} collective-permute-done((bf16[192,768]{1,0:T(8,128)(2,1)S(1)}, bf16[192,768]{1,0:T(8,128)(2,1)S(1)}, u32[]{:S(2)}, u32[]{:S(2)}) %collective-permute-start.32) | collective-permute-done | bytes 294944 | tf_op jit(solution)/shard_map/ppermute | solution.py:79
  183.1 4.7 %collective-permute-done.37 = bf16[192,768]{1,0:T(8,128)(2,1)S(1)} collective-permute-done((bf16[192,768]{1,0:T(8,128)(2,1)S(1)}, bf16[192,768]{1,0:T(8,128)(2,1)S(1)}, u32[]{:S(2)}, u32[]{:S(2)}) %collective-permute-start.37) | collective-permute-done | bytes 294944 | tf_op jit(solution)/shard_map/ppermute | solution.py:79
  188.0 2.5 %collective-permute-start.27 = (bf16[192,768]{1,0:T(8,128)(2,1)S(1)}, bf16[192,768]{1,0:T(8,128)(2,1)S(1)}, u32[]{:S(2)}, u32[]{:S(2)}) collective-permute-start(bf16[192,768]{1,0:T(8,128)(2,1)S(1)} %fusion.38), channel_id=1, source_target_pairs={{0,16},{8,24},{16,0},{24,8},{1,17},{9,25},{17,1},{25,9},{2,18},{10... | collective-permute-start | bytes 884744 | tf_op jit(solution)/shard_map/ppermute | solution.py:79
  190.5 9.8 %collective-permute-done.33 = bf16[192,768]{1,0:T(8,128)(2,1)S(1)} collective-permute-done((bf16[192,768]{1,0:T(8,128)(2,1)S(1)}, bf16[192,768]{1,0:T(8,128)(2,1)S(1)}, u32[]{:S(2)}, u32[]{:S(2)}) %collective-permute-start.33) | collective-permute-done | bytes 294944 | tf_op jit(solution)/shard_map/ppermute | solution.py:80
  200.5 6.0 %collective-permute-done.38 = bf16[192,768]{1,0:T(8,128)(2,1)S(1)} collective-permute-done((bf16[192,768]{1,0:T(8,128)(2,1)S(1)}, bf16[192,768]{1,0:T(8,128)(2,1)S(1)}, u32[]{:S(2)}, u32[]{:S(2)}) %collective-permute-start.38) | collective-permute-done | bytes 294944 | tf_op jit(solution)/shard_map/ppermute | solution.py:80
  206.9 1.8 fusion.64
  208.8 7.5 %collective-permute-done.28 = bf16[192,768]{1,0:T(8,128)(2,1)S(1)} collective-permute-done((bf16[192,768]{1,0:T(8,128)(2,1)S(1)}, bf16[192,768]{1,0:T(8,128)(2,1)S(1)}, u32[]{:S(2)}, u32[]{:S(2)}) %collective-permute-start.28) | collective-permute-done | bytes 294944 | tf_op jit(solution)/shard_map/ppermute | solution.py:80
  216.9 1.7 bitcast_convert_fusion.1
  218.5 1.7 bitcast_convert_fusion
  220.7 1.3 slice.85
  (208 shorter events, 35.6 us)
Async XLA Ops:
  0.6 60.9 %copy-start = (bf16[768,768]{1,0:T(8,128)(2,1)S(1)}, bf16[768,768]{1,0:T(8,128)(2,1)}, u32[]{:S(2)}) copy-start(bf16[768,768]{1,0:T(8,128)(2,1)} %param.29) | copy-start | bytes 3538948
  0.7 25.6 %copy-start.33 = (s32[1,4]{1,0:T(1,128)S(1)}, s32[1,4]{1,0:T(1,128)}, u32[]{:S(2)}) copy-start(s32[1,4]{1,0:T(1,128)} %param.17) | copy-start | bytes 52
  2.4 30.9 %collective-permute-start.1 = (bf16[96,768]{1,0:T(8,128)(2,1)}, bf16[96,768]{1,0:T(8,128)(2,1)}, u32[]{:S(2)}, u32[]{:S(2)}) collective-permute-start(bf16[96,768]{1,0:T(8,128)(2,1)} %get-tuple-element.50), channel_id=1, source_target_pairs={{0,2},{2,0},{4,6},{6,4},{1,3},{3,1},{5,7},{7,5},{8,10},{10,8},{12,... | collective-permute-start | bytes 442376 | tf_op jit(solution)/shard_map/ppermute | solution.py:50
  5.3 30.4 %collective-permute-start.2 = (bf16[96,768]{1,0:T(8,128)(2,1)}, bf16[96,768]{1,0:T(8,128)(2,1)}, u32[]{:S(2)}, u32[]{:S(2)}) collective-permute-start(bf16[96,768]{1,0:T(8,128)(2,1)} %get-tuple-element.50), channel_id=1, source_target_pairs={{0,4},{2,6},{4,0},{6,2},{1,5},{3,7},{5,1},{7,3},{8,12},{10,14},{12... | collective-permute-start | bytes 442376 | tf_op jit(solution)/shard_map/ppermute | solution.py:50
  6.9 29.9 %collective-permute-start.3 = (bf16[96,768]{1,0:T(8,128)(2,1)}, bf16[96,768]{1,0:T(8,128)(2,1)}, u32[]{:S(2)}, u32[]{:S(2)}) collective-permute-start(bf16[96,768]{1,0:T(8,128)(2,1)} %get-tuple-element.50), channel_id=1, source_target_pairs={{0,6},{2,4},{4,2},{6,0},{1,7},{3,5},{5,3},{7,1},{8,14},{10,12},{12... | collective-permute-start | bytes 442376 | tf_op jit(solution)/shard_map/ppermute | solution.py:50
  6.9 31.4 %collective-permute-start.8 = (bf16[128,768]{1,0:T(8,128)(2,1)}, bf16[128,768]{1,0:T(8,128)(2,1)}, u32[]{:S(2)}, u32[]{:S(2)}) collective-permute-start(bf16[128,768]{1,0:T(8,128)(2,1)} %bitcast.313), channel_id=1, source_target_pairs={{0,2},{2,0},{4,6},{6,4},{1,3},{3,1},{5,7},{7,5},{8,10},{10,8},{12,... | collective-permute-start | bytes 589832 | tf_op jit(solution)/shard_map/ppermute | solution.py:50
  8.8 30.4 %collective-permute-start.9 = (bf16[128,768]{1,0:T(8,128)(2,1)}, bf16[128,768]{1,0:T(8,128)(2,1)}, u32[]{:S(2)}, u32[]{:S(2)}) collective-permute-start(bf16[128,768]{1,0:T(8,128)(2,1)} %bitcast.314), channel_id=1, source_target_pairs={{0,4},{2,6},{4,0},{6,2},{1,5},{3,7},{5,1},{7,3},{8,12},{10,14},{12... | collective-permute-start | bytes 589832 | tf_op jit(solution)/shard_map/ppermute | solution.py:50
  10.4 16.3 %copy-start.15 = (bf16[1,128,768]{2,1,0:T(8,128)(2,1)S(1)}, bf16[1,128,768]{2,1,0:T(8,128)(2,1)}, u32[]{:S(2)}) copy-start(bf16[1,128,768]{2,1,0:T(8,128)(2,1)} %param.31) | copy-start | bytes 589828
  26.4 4.7 %copy-start.21 = (f32[512]{0:T(512)}, f32[512]{0:T(512)S(1)}, u32[]{:S(2)}) copy-start(f32[512]{0:T(512)S(1)} %add_rsqrt_fusion.1) | copy-start | bytes 6148
  33.3 7.1 %copy-start.7 = (bf16[512,192]{0,1:T(8,128)(2,1)S(1)}, bf16[512,192]{0,1:T(8,128)(2,1)}, u32[]{:S(2)}) copy-start(bf16[512,192]{0,1:T(8,128)(2,1)} %get-tuple-element.37) | copy-start | bytes 589828
  33.3 7.1 %copy-start.8 = (bf16[512,192]{0,1:T(8,128)(2,1)S(1)}, bf16[512,192]{0,1:T(8,128)(2,1)}, u32[]{:S(2)}) copy-start(bf16[512,192]{0,1:T(8,128)(2,1)} %slice.109) | copy-start | bytes 589828
  33.3 6.9 %collective-permute-start.10 = (bf16[128,768]{1,0:T(8,128)(2,1)}, bf16[128,768]{1,0:T(8,128)(2,1)S(1)}, u32[]{:S(2)}, u32[]{:S(2)}) collective-permute-start(bf16[128,768]{1,0:T(8,128)(2,1)} %bitcast.315), channel_id=1, source_target_pairs={{0,6},{2,4},{4,2},{6,0},{1,7},{3,5},{5,3},{7,1},{8,14},{10,12},{12... | collective-permute-start | bytes 589832 | tf_op jit(solution)/shard_map/ppermute | solution.py:50
  35.8 4.6 %collective-permute-start = (bf16[512,384]{0,1:T(8,128)(2,1)S(1)}, bf16[512,384]{0,1:T(8,128)(2,1)S(1)}, u32[]{:S(2)}, u32[]{:S(2)}) collective-permute-start(bf16[512,384]{0,1:T(8,128)(2,1)S(1)} %pad_maximum_fusion.2), channel_id=1, source_target_pairs={{0,1},{1,0},{2,3},{3,2},{4,5},{5,4},{6,7},{7,6},{8,9},{9,8},{10,11... | collective-permute-start | bytes 1179656 | tf_op jit(solution)/shard_map/ppermute | solution.py:159
  37.7 20.0 %collective-permute-start.4 = (bf16[4,96,768]{2,1,0:T(8,128)(2,1)S(1)}, bf16[4,96,768]{2,1,0:T(8,128)(2,1)S(1)}, u32[]{:S(2)}, u32[]{:S(2)}) collective-permute-start(bf16[4,96,768]{2,1,0:T(8,128)(2,1)S(1)} %bitcast_dynamic-update-slice_fusion.3), channel_id=1, source_target_pairs={{0,1},{1,0},{2,3},{3,2},{4,5},{5,4},{6,7},{7,6},{8,9},{9,8},{10,11... | collective-permute-start | bytes 1769480 | tf_op jit(solution)/shard_map/ppermute | solution.py:144
  46.1 11.7 %copy-start.17 = (bf16[3,64,512]{2,1,0:T(8,128)(2,1)}, bf16[3,64,512]{2,1,0:T(8,128)(2,1)S(1)}, u32[]{:S(2)}) copy-start(bf16[3,64,512]{2,1,0:T(8,128)(2,1)S(1)} %fusion.29) | copy-start | bytes 589828
  46.1 11.8 %copy-start.29 = (f32[768]{0:T(1024)S(1)}, f32[768]{0:T(1024)}, u32[]{:S(2)}) copy-start(f32[768]{0:T(1024)} %param.24) | copy-start | bytes 9220
  62.6 4.5 %copy-start.4 = (f32[512,768]{1,0:T(8,128)}, f32[512,768]{1,0:T(8,128)S(1)}, u32[]{:S(2)}) copy-start(f32[512,768]{1,0:T(8,128)S(1)} %fusion.71) | copy-start | bytes 4718596
  66.1 8.8 %copy-start.12 = (bf16[768,768]{1,0:T(8,128)(2,1)}, bf16[768,768]{1,0:T(8,128)(2,1)S(1)}, u32[]{:S(2)}) copy-start(bf16[768,768]{1,0:T(8,128)(2,1)S(1)} %convolution_convert_fusion.1) | copy-start | bytes 3538948
  67.1 8.7 %copy-start.10 = (bf16[768,768]{1,0:T(8,128)(2,1)}, bf16[768,768]{1,0:T(8,128)(2,1)S(1)}, u32[]{:S(2)}) copy-start(bf16[768,768]{1,0:T(8,128)(2,1)S(1)} %convolution_convert_fusion) | copy-start | bytes 3538948
  68.2 50.3 %collective-permute-start.7 = (bf16[128,768]{1,0:T(8,128)(2,1)}, bf16[128,768]{1,0:T(8,128)(2,1)}, u32[]{:S(2)}, u32[]{:S(2)}) collective-permute-start(bf16[128,768]{1,0:T(8,128)(2,1)} %get-tuple-element.46), channel_id=1, source_target_pairs={{0,6},{2,4},{4,2},{6,0},{1,7},{3,5},{5,3},{7,1},{8,14},{10,12},{12... | collective-permute-start | bytes 589832 | tf_op jit(solution)/shard_map/ppermute | solution.py:60
  69.7 48.9 %collective-permute-start.6 = (bf16[128,768]{1,0:T(8,128)(2,1)}, bf16[128,768]{1,0:T(8,128)(2,1)}, u32[]{:S(2)}, u32[]{:S(2)}) collective-permute-start(bf16[128,768]{1,0:T(8,128)(2,1)} %get-tuple-element.47), channel_id=1, source_target_pairs={{0,4},{2,6},{4,0},{6,2},{1,5},{3,7},{5,1},{7,3},{8,12},{10,14},{12... | collective-permute-start | bytes 589832 | tf_op jit(solution)/shard_map/ppermute | solution.py:60
  70.8 10.6 %collective-permute-start.13 = (bf16[128,768]{1,0:T(8,128)(2,1)S(1)}, bf16[128,768]{1,0:T(8,128)(2,1)S(1)}, u32[]{:S(2)}, u32[]{:S(2)}) collective-permute-start(bf16[128,768]{1,0:T(8,128)(2,1)S(1)} %get-tuple-element.43), channel_id=1, source_target_pairs={{0,6},{2,4},{4,2},{6,0},{1,7},{3,5},{5,3},{7,1},{8,14},{10,12},{12... | collective-permute-start | bytes 589832 | tf_op jit(solution)/shard_map/ppermute | solution.py:60
  72.3 15.0 %collective-permute-start.12 = (bf16[128,768]{1,0:T(8,128)(2,1)S(1)}, bf16[128,768]{1,0:T(8,128)(2,1)S(1)}, u32[]{:S(2)}, u32[]{:S(2)}) collective-permute-start(bf16[128,768]{1,0:T(8,128)(2,1)S(1)} %get-tuple-element.44), channel_id=1, source_target_pairs={{0,4},{2,6},{4,0},{6,2},{1,5},{3,7},{5,1},{7,3},{8,12},{10,14},{12... | collective-permute-start | bytes 589832 | tf_op jit(solution)/shard_map/ppermute | solution.py:60
  73.3 14.1 %collective-permute-start.11 = (bf16[128,768]{1,0:T(8,128)(2,1)S(1)}, bf16[128,768]{1,0:T(8,128)(2,1)S(1)}, u32[]{:S(2)}, u32[]{:S(2)}) collective-permute-start(bf16[128,768]{1,0:T(8,128)(2,1)S(1)} %get-tuple-element.42), channel_id=1, source_target_pairs={{0,2},{2,0},{4,6},{6,4},{1,3},{3,1},{5,7},{7,5},{8,10},{10,8},{12,... | collective-permute-start | bytes 589832 | tf_op jit(solution)/shard_map/ppermute | solution.py:60
  75.8 12.3 %copy-start.16 = (bf16[1,128,768]{2,1,0:T(8,128)(2,1)S(1)}, bf16[1,128,768]{2,1,0:T(8,128)(2,1)}, u32[]{:S(2)}) copy-start(bf16[1,128,768]{2,1,0:T(8,128)(2,1)} %param.31) | copy-start | bytes 589828
  81.4 37.2 %collective-permute-start.5 = (bf16[128,768]{1,0:T(8,128)(2,1)}, bf16[128,768]{1,0:T(8,128)(2,1)}, u32[]{:S(2)}, u32[]{:S(2)}) collective-permute-start(bf16[128,768]{1,0:T(8,128)(2,1)} %get-tuple-element.45), channel_id=1, source_target_pairs={{0,2},{2,0},{4,6},{6,4},{1,3},{3,1},{5,7},{7,5},{8,10},{10,8},{12,... | collective-permute-start | bytes 589832 | tf_op jit(solution)/shard_map/ppermute | solution.py:60
  87.3 43.9 %collective-permute-start.30 = (bf16[384,768]{1,0:T(8,128)(2,1)}, bf16[384,768]{1,0:T(8,128)(2,1)}, u32[]{:S(2)}, u32[]{:S(2)}) collective-permute-start(bf16[384,768]{1,0:T(8,128)(2,1)} %dynamic-slice_bitcast_fusion.1), channel_id=1, source_target_pairs={{0,1},{1,0},{2,3},{3,2},{4,5},{5,4},{6,7},{7,6},{8,9},{9,8},{10,11... | collective-permute-start | bytes 1769480 | tf_op jit(solution)/shard_map/ppermute | solution.py:89
  87.4 46.4 %collective-permute-start.35 = (bf16[384,768]{1,0:T(8,128)(2,1)}, bf16[384,768]{1,0:T(8,128)(2,1)}, u32[]{:S(2)}, u32[]{:S(2)}) collective-permute-start(bf16[384,768]{1,0:T(8,128)(2,1)} %dynamic-slice_bitcast_fusion), channel_id=1, source_target_pairs={{0,1},{1,0},{2,3},{3,2},{4,5},{5,4},{6,7},{7,6},{8,9},{9,8},{10,11... | collective-permute-start | bytes 1769480 | tf_op jit(solution)/shard_map/ppermute | solution.py:89
  88.1 12.7 %copy-start.19 = (bf16[192,768]{1,0:T(8,128)(2,1)S(1)}, bf16[192,768]{1,0:T(8,128)(2,1)}, u32[]{:S(2)}) copy-start(bf16[192,768]{1,0:T(8,128)(2,1)} %param.23) | copy-start | bytes 884740
  116.5 2.1 copy-start.23
  117.2 3.6 %copy-start.18 = (bf16[3,64,512]{2,1,0:T(8,128)(2,1)S(1)}, bf16[3,64,512]{2,1,0:T(8,128)(2,1)}, u32[]{:S(2)}) copy-start(bf16[3,64,512]{2,1,0:T(8,128)(2,1)} %copy-done.17) | copy-start | bytes 589828
  118.5 2.7 %copy-start.2 = (f32[2,512,192]{2,1,0:T(8,128)S(1)}, f32[2,512,192]{2,1,0:T(8,128)}, u32[]{:S(2)}) copy-start(f32[2,512,192]{2,1,0:T(8,128)} %copy.35) | copy-start | bytes 2359300
  118.5 2.7 %collective-permute-start.14 = (bf16[512,384]{1,0:T(8,128)(2,1)S(1)}, bf16[512,384]{1,0:T(8,128)(2,1)S(1)}, u32[]{:S(2)}, u32[]{:S(2)}) collective-permute-start(bf16[512,384]{1,0:T(8,128)(2,1)S(1)} %fusion.39), channel_id=1, source_target_pairs={{0,1},{1,0},{2,3},{3,2},{4,5},{5,4},{6,7},{7,6},{8,9},{9,8},{10,11... | collective-permute-start | bytes 1179656 | tf_op jit(solution)/shard_map/ppermute | solution.py:225
  122.3 5.9 %copy-start.24 = (f32[768]{0:T(1024)S(1)}, f32[768]{0:T(1024)}, u32[]{:S(2)}) copy-start(f32[768]{0:T(1024)} %param.18) | copy-start | bytes 9220
  122.3 5.9 %copy-start.32 = (f32[768]{0:T(1024)S(1)}, f32[768]{0:T(1024)}, u32[]{:S(2)}) copy-start(f32[768]{0:T(1024)} %param.19) | copy-start | bytes 9220
  124.4 13.3 %collective-permute-start.20 = (f32[4,768]{1,0:T(4,128)S(1)}, f32[4,768]{1,0:T(4,128)S(1)}, u32[]{:S(2)}, u32[]{:S(2)}) collective-permute-start(f32[4,768]{1,0:T(4,128)S(1)} %pad_maximum_fusion.5), channel_id=1, source_target_pairs={{0,6},{2,4},{4,2},{6,0},{1,7},{3,5},{5,3},{7,1},{8,14},{10,12},{12... | collective-permute-start | bytes 36872 | tf_op jit(solution)/shard_map/ppermute | solution.py:100
  125.9 11.7 %collective-permute-start.19 = (f32[4,768]{1,0:T(4,128)S(1)}, f32[4,768]{1,0:T(4,128)S(1)}, u32[]{:S(2)}, u32[]{:S(2)}) collective-permute-start(f32[4,768]{1,0:T(4,128)S(1)} %pad_maximum_fusion.5), channel_id=1, source_target_pairs={{0,4},{2,6},{4,0},{6,2},{1,5},{3,7},{5,1},{7,3},{8,12},{10,14},{12... | collective-permute-start | bytes 36872 | tf_op jit(solution)/shard_map/ppermute | solution.py:100
  126.9 10.7 %collective-permute-start.18 = (f32[4,768]{1,0:T(4,128)S(1)}, f32[4,768]{1,0:T(4,128)S(1)}, u32[]{:S(2)}, u32[]{:S(2)}) collective-permute-start(f32[4,768]{1,0:T(4,128)S(1)} %pad_maximum_fusion.5), channel_id=1, source_target_pairs={{0,2},{2,0},{4,6},{6,4},{1,3},{3,1},{5,7},{7,5},{8,10},{10,8},{12,... | collective-permute-start | bytes 36872 | tf_op jit(solution)/shard_map/ppermute | solution.py:100
  130.2 2.4 %copy-start.13 = (bf16[768,768]{1,0:T(8,128)(2,1)S(1)}, bf16[768,768]{1,0:T(8,128)(2,1)}, u32[]{:S(2)}) copy-start(bf16[768,768]{1,0:T(8,128)(2,1)} %copy-done.12) | copy-start | bytes 3538948
  130.3 4.7 %copy-start.11 = (bf16[768,768]{1,0:T(8,128)(2,1)S(1)}, bf16[768,768]{1,0:T(8,128)(2,1)}, u32[]{:S(2)}) copy-start(bf16[768,768]{1,0:T(8,128)(2,1)} %copy-done.10) | copy-start | bytes 3538948
  131.1 19.7 %collective-permute-start.17 = (bf16[128,768]{1,0:T(8,128)(2,1)}, bf16[128,768]{1,0:T(8,128)(2,1)}, u32[]{:S(2)}, u32[]{:S(2)}) collective-permute-start(bf16[128,768]{1,0:T(8,128)(2,1)} %get-tuple-element.40), channel_id=1, source_target_pairs={{0,6},{2,4},{4,2},{6,0},{1,7},{3,5},{5,3},{7,1},{8,14},{10,12},{12... | collective-permute-start | bytes 589832 | tf_op jit(solution)/shard_map/ppermute | solution.py:60
  133.8 19.0 %collective-permute-start.16 = (bf16[128,768]{1,0:T(8,128)(2,1)}, bf16[128,768]{1,0:T(8,128)(2,1)}, u32[]{:S(2)}, u32[]{:S(2)}) collective-permute-start(bf16[128,768]{1,0:T(8,128)(2,1)} %get-tuple-element.41), channel_id=1, source_target_pairs={{0,4},{2,6},{4,0},{6,2},{1,5},{3,7},{5,1},{7,3},{8,12},{10,14},{12... | collective-permute-start | bytes 589832 | tf_op jit(solution)/shard_map/ppermute | solution.py:60
  139.0 1.4 collective-permute-start.21
  141.2 5.6 %collective-permute-start.24 = (f32[8,768]{1,0:T(8,128)S(1)}, f32[8,768]{1,0:T(8,128)S(1)}, u32[]{:S(2)}, u32[]{:S(2)}) collective-permute-start(f32[8,768]{1,0:T(8,128)S(1)} %add.318), channel_id=1, source_target_pairs={{0,24},{8,16},{16,8},{24,0},{1,25},{9,17},{17,9},{25,1},{2,26},{10... | collective-permute-start | bytes 73736 | tf_op jit(solution)/shard_map/ppermute | solution.py:100
  144.8 4.7 %collective-permute-start.23 = (f32[8,768]{1,0:T(8,128)S(1)}, f32[8,768]{1,0:T(8,128)S(1)}, u32[]{:S(2)}, u32[]{:S(2)}) collective-permute-start(f32[8,768]{1,0:T(8,128)S(1)} %add.318), channel_id=1, source_target_pairs={{0,16},{8,24},{16,0},{24,8},{1,17},{9,25},{17,1},{25,9},{2,18},{10... | collective-permute-start | bytes 73736 | tf_op jit(solution)/shard_map/ppermute | solution.py:100
  144.8 4.7 %collective-permute-start.22 = (f32[8,768]{1,0:T(8,128)S(1)}, f32[8,768]{1,0:T(8,128)S(1)}, u32[]{:S(2)}, u32[]{:S(2)}) collective-permute-start(f32[8,768]{1,0:T(8,128)S(1)} %add.318), channel_id=1, source_target_pairs={{0,8},{8,0},{16,24},{24,16},{1,9},{9,1},{17,25},{25,17},{2,10},{10... | collective-permute-start | bytes 73736 | tf_op jit(solution)/shard_map/ppermute | solution.py:100
  145.5 23.0 %copy-start.5 = (bf16[384,768]{1,0:T(8,128)(2,1)S(1)}, bf16[384,768]{1,0:T(8,128)(2,1)}, u32[]{:S(2)}) copy-start(bf16[384,768]{1,0:T(8,128)(2,1)} %fusion.25) | copy-start | bytes 1769476
  146.8 6.1 %collective-permute-start.15 = (bf16[128,768]{1,0:T(8,128)(2,1)S(1)}, bf16[128,768]{1,0:T(8,128)(2,1)S(1)}, u32[]{:S(2)}, u32[]{:S(2)}) collective-permute-start(bf16[128,768]{1,0:T(8,128)(2,1)S(1)} %get-tuple-element.39), channel_id=1, source_target_pairs={{0,2},{2,0},{4,6},{6,4},{1,3},{3,1},{5,7},{7,5},{8,10},{10,8},{12,... | collective-permute-start | bytes 589832 | tf_op jit(solution)/shard_map/ppermute | solution.py:60
  149.5 19.2 %collective-permute-start.25 = (bf16[384,768]{1,0:T(8,128)(2,1)}, bf16[384,768]{1,0:T(8,128)(2,1)S(1)}, u32[]{:S(2)}, u32[]{:S(2)}) collective-permute-start(bf16[384,768]{1,0:T(8,128)(2,1)} %dynamic-slice_bitcast_fusion.2), channel_id=1, source_target_pairs={{0,1},{1,0},{2,3},{3,2},{4,5},{5,4},{6,7},{7,6},{8,9},{9,8},{10,11... | collective-permute-start | bytes 1769480 | tf_op jit(solution)/shard_map/ppermute | solution.py:89
  149.5 9.8 %collective-permute-start.31 = (bf16[192,768]{1,0:T(8,128)(2,1)S(1)}, bf16[192,768]{1,0:T(8,128)(2,1)S(1)}, u32[]{:S(2)}, u32[]{:S(2)}) collective-permute-start(bf16[192,768]{1,0:T(8,128)(2,1)S(1)} %dynamic-slice_bitcast_fusion.4), channel_id=1, source_target_pairs={{0,8},{8,0},{16,24},{24,16},{1,9},{9,1},{17,25},{25,17},{2,10},{10... | collective-permute-start | bytes 884744 | tf_op jit(solution)/shard_map/ppermute | solution.py:78
  150.8 17.7 %collective-permute-start.36 = (bf16[192,768]{1,0:T(8,128)(2,1)S(1)}, bf16[192,768]{1,0:T(8,128)(2,1)S(1)}, u32[]{:S(2)}, u32[]{:S(2)}) collective-permute-start(bf16[192,768]{1,0:T(8,128)(2,1)S(1)} %dynamic-slice_bitcast_fusion.3), channel_id=1, source_target_pairs={{0,8},{8,0},{16,24},{24,16},{1,9},{9,1},{17,25},{25,17},{2,10},{10... | collective-permute-start | bytes 884744 | tf_op jit(solution)/shard_map/ppermute | solution.py:78
  159.4 23.5 %collective-permute-start.32 = (bf16[192,768]{1,0:T(8,128)(2,1)S(1)}, bf16[192,768]{1,0:T(8,128)(2,1)S(1)}, u32[]{:S(2)}, u32[]{:S(2)}) collective-permute-start(bf16[192,768]{1,0:T(8,128)(2,1)S(1)} %fusion.37), channel_id=1, source_target_pairs={{0,16},{8,24},{16,0},{24,8},{1,17},{9,25},{17,1},{25,9},{2,18},{10... | collective-permute-start | bytes 884744 | tf_op jit(solution)/shard_map/ppermute | solution.py:79
  168.6 19.1 %collective-permute-start.37 = (bf16[192,768]{1,0:T(8,128)(2,1)S(1)}, bf16[192,768]{1,0:T(8,128)(2,1)S(1)}, u32[]{:S(2)}, u32[]{:S(2)}) collective-permute-start(bf16[192,768]{1,0:T(8,128)(2,1)S(1)} %fusion.36), channel_id=1, source_target_pairs={{0,16},{8,24},{16,0},{24,8},{1,17},{9,25},{17,1},{25,9},{2,18},{10... | collective-permute-start | bytes 884744 | tf_op jit(solution)/shard_map/ppermute | solution.py:79
  168.9 19.0 %collective-permute-start.26 = (bf16[192,768]{1,0:T(8,128)(2,1)S(1)}, bf16[192,768]{1,0:T(8,128)(2,1)S(1)}, u32[]{:S(2)}, u32[]{:S(2)}) collective-permute-start(bf16[192,768]{1,0:T(8,128)(2,1)S(1)} %dynamic-slice_bitcast_fusion.5), channel_id=1, source_target_pairs={{0,8},{8,0},{16,24},{24,16},{1,9},{9,1},{17,25},{25,17},{2,10},{10... | collective-permute-start | bytes 884744 | tf_op jit(solution)/shard_map/ppermute | solution.py:78
  183.0 17.4 %collective-permute-start.33 = (bf16[192,768]{1,0:T(8,128)(2,1)S(1)}, bf16[192,768]{1,0:T(8,128)(2,1)S(1)}, u32[]{:S(2)}, u32[]{:S(2)}) collective-permute-start(bf16[192,768]{1,0:T(8,128)(2,1)S(1)} %add_convert_fusion.3), channel_id=1, source_target_pairs={{0,8},{8,0},{16,24},{24,16},{1,9},{9,1},{17,25},{25,17},{2,10},{10... | collective-permute-start | bytes 884744 | tf_op jit(solution)/shard_map/ppermute | solution.py:80
  187.8 18.8 %collective-permute-start.38 = (bf16[192,768]{1,0:T(8,128)(2,1)S(1)}, bf16[192,768]{1,0:T(8,128)(2,1)S(1)}, u32[]{:S(2)}, u32[]{:S(2)}) collective-permute-start(bf16[192,768]{1,0:T(8,128)(2,1)S(1)} %add_convert_fusion.2), channel_id=1, source_target_pairs={{0,8},{8,0},{16,24},{24,16},{1,9},{9,1},{17,25},{25,17},{2,10},{10... | collective-permute-start | bytes 884744 | tf_op jit(solution)/shard_map/ppermute | solution.py:80
  188.0 18.8 %collective-permute-start.27 = (bf16[192,768]{1,0:T(8,128)(2,1)S(1)}, bf16[192,768]{1,0:T(8,128)(2,1)S(1)}, u32[]{:S(2)}, u32[]{:S(2)}) collective-permute-start(bf16[192,768]{1,0:T(8,128)(2,1)S(1)} %fusion.38), channel_id=1, source_target_pairs={{0,16},{8,24},{16,0},{24,8},{1,17},{9,25},{17,1},{25,9},{2,18},{10... | collective-permute-start | bytes 884744 | tf_op jit(solution)/shard_map/ppermute | solution.py:79
  200.3 6.6 %copy-start.9 = (f32[128,768]{1,0:T(8,128)S(1)}, f32[128,768]{1,0:T(8,128)}, u32[]{:S(2)}) copy-start(f32[128,768]{1,0:T(8,128)} %get-tuple-element.34) | copy-start | bytes 1179652
  200.3 6.6 %copy-start.27 = (f32[128]{0:T(128)S(1)}, f32[128]{0:T(128)}, u32[]{:S(2)}) copy-start(f32[128]{0:T(128)} %fusion.67) | copy-start | bytes 1540
  200.4 16.0 %collective-permute-start.34 = (bf16[384,768]{1,0:T(8,128)(2,1)S(1)}, bf16[384,768]{1,0:T(8,128)(2,1)S(1)}, u32[]{:S(2)}, u32[]{:S(2)}) collective-permute-start(bf16[384,768]{1,0:T(8,128)(2,1)S(1)} %bitcast.282), channel_id=1, source_target_pairs={{0,1},{1,0},{2,3},{3,2},{4,5},{5,4},{6,7},{7,6},{8,9},{9,8},{10,11... | collective-permute-start | bytes 1769480 | tf_op jit(solution)/shard_map/ppermute | solution.py:91
  206.7 10.0 %collective-permute-start.39 = (bf16[384,768]{1,0:T(8,128)(2,1)S(1)}, bf16[384,768]{1,0:T(8,128)(2,1)S(1)}, u32[]{:S(2)}, u32[]{:S(2)}) collective-permute-start(bf16[384,768]{1,0:T(8,128)(2,1)S(1)} %bitcast.284), channel_id=1, source_target_pairs={{0,1},{1,0},{2,3},{3,2},{4,5},{5,4},{6,7},{7,6},{8,9},{9,8},{10,11... | collective-permute-start | bytes 1769480 | tf_op jit(solution)/shard_map/ppermute | solution.py:91
  206.8 9.5 %collective-permute-start.28 = (bf16[192,768]{1,0:T(8,128)(2,1)S(1)}, bf16[192,768]{1,0:T(8,128)(2,1)S(1)}, u32[]{:S(2)}, u32[]{:S(2)}) collective-permute-start(bf16[192,768]{1,0:T(8,128)(2,1)S(1)} %add_convert_fusion.4), channel_id=1, source_target_pairs={{0,8},{8,0},{16,24},{24,16},{1,9},{9,1},{17,25},{25,17},{2,10},{10... | collective-permute-start | bytes 884744 | tf_op jit(solution)/shard_map/ppermute | solution.py:80
  216.4 3.8 %collective-permute-start.29 = (bf16[384,768]{1,0:T(8,128)(2,1)S(1)}, bf16[384,768]{1,0:T(8,128)(2,1)S(1)}, u32[]{:S(2)}, u32[]{:S(2)}) collective-permute-start(bf16[384,768]{1,0:T(8,128)(2,1)S(1)} %bitcast.286), channel_id=1, source_target_pairs={{0,1},{1,0},{2,3},{3,2},{4,5},{5,4},{6,7},{7,6},{8,9},{9,8},{10,11... | collective-permute-start | bytes 1769480 | tf_op jit(solution)/shard_map/ppermute | solution.py:91
  220.4 2.4 %copy-start.1 = (bf16[768,768]{1,0:T(8,128)(2,1)S(1)}, bf16[768,768]{1,0:T(8,128)(2,1)}, u32[]{:S(2)}) copy-start(bf16[768,768]{1,0:T(8,128)(2,1)} %param.29) | copy-start | bytes 3538948
  (10 other events, 14.0 us)

commit v2 on v1

v2 whole, which is shorter than its diff:
```python
import functools

import jax
import jax.numpy as jnp
from jax import lax
from jax.experimental import pallas as pl
from jax.experimental.pallas import tpu as pltpu
from jax.sharding import PartitionSpec as P

HEAD_DIM = 64
EPS = 1e-05
MASKED = -1e30
BF16 = jnp.bfloat16
F32 = jnp.float32
SCALE = HEAD_DIM**-0.5
LOG2_SCALE = SCALE * 1.4426950408889634
LONG_START_MAX = 128
LONG_END_MIN = 64 + 768
LONG_END_MAX = 128 + 768
MIB = 1024 * 1024


def dot(a, b, ca, cb):
    return lax.dot_general(a, b, (((ca,), (cb,)), ((), ())), preferred_element_type=F32)


def norm_parts(values):
    center = values - jnp.mean(values, axis=-1, keepdims=True)
    scale = lax.rsqrt(jnp.mean(center * center, axis=-1, keepdims=True) + EPS)
    return center * scale, scale


def norm_back(grad, gain, xhat, scale):
    g = grad * gain
    return scale * (
        g - jnp.mean(g, axis=-1, keepdims=True) - xhat * jnp.mean(g * xhat, axis=-1, keepdims=True)
    )


def xor_pairs(count, mask):
    return [(i, i ^ mask) for i in range(count)]


def pick(x, index):
    return lax.dynamic_index_in_dim(x, index, 0, keepdims=False)


def after(x, *deps):
    return lax.optimization_barrier((x,) + deps)[0]


def rows_at(index, size):
    return pl.ds(pl.multiple_of(index * size, size), size)


def call(kernel, out_shape, args, vmem=16, scratch=(), smem=0):
    spaces = [pltpu.SMEM] * smem + [pltpu.VMEM] * (len(args) - smem)
    return pl.pallas_call(
        kernel,
        out_shape=out_shape,
        in_specs=[pl.BlockSpec(memory_space=s) for s in spaces],
        out_specs=[pl.BlockSpec(memory_space=pltpu.VMEM)] * len(out_shape),
        scratch_shapes=list(scratch),
        compiler_params=pltpu.CompilerParams(vmem_limit_bytes=vmem * MIB),
    )(*args)


def vec(ref):
    return ref[...].reshape(1, ref.shape[0])


def shape(dims, dtype):
    return jax.ShapeDtypeStruct(dims, dtype)


def qkv_kernel(
    meta_ref, x0, x1, x2, x3, gain_ref, shift_ref, w_ref, qb_ref, vb_ref, rows_ref, normed_ref, q_ref, kv_ref
):
    local = q_ref.shape[1]
    own = x0.shape[0]
    rank = meta_ref[0]
    gain, shift = vec(gain_ref), vec(shift_ref)
    for r, x in enumerate((x0, x1, x2, x3)):
        at = rows_at(rank ^ r, own)
        rows_ref[at] = x[...]
        xhat, _ = norm_parts(x[...].astype(F32))
        normed_ref[at] = (xhat * gain + shift).astype(BF16)
    normed = normed_ref[...]
    q_ref[...] = (dot(normed, w_ref[:local], 1, 1) + vec(qb_ref)).astype(BF16)
    kv_ref[:, :local] = dot(normed, w_ref[local : 2 * local], 1, 1).astype(BF16)
    kv_ref[:, local:] = (dot(normed, w_ref[2 * local :], 1, 1) + vec(vb_ref)).astype(BF16)


def blocks_of(ctx, half, size):
    out = []
    for i in range(half // size):
        first = ctx * half + i * size
        low = LONG_END_MIN // 128 * 128 if first >= LONG_END_MAX else 0
        out.append((i * size, first, low, first + size))
    return out


def allowed_of(meta_ref, first, low, end, size):
    query = first + lax.broadcasted_iota(jnp.int32, (1, size), 1)
    start = jnp.zeros_like(query)
    bound = jnp.int32(0)
    for j in range(3):
        bound = bound + meta_ref[2 + j]
        start = jnp.where(query >= bound, bound, start)
    key = low + lax.broadcasted_iota(jnp.int32, (end - low, size), 0)
    return (key >= start) & (key <= query)


def head_mask(head, width):
    lane = lax.broadcasted_iota(jnp.int32, (1, width), 1)
    inside = (lane >= head * HEAD_DIM) & (lane < (head + 1) * HEAD_DIM)
    return jnp.where(inside, 1.0, 0.0).astype(BF16)


def attend_body(ctx, size, meta_ref, q_ref, k_ref, vt_ref, mix_ref, lse_ref):
    half, local = q_ref.shape
    for at, first, low, end in blocks_of(ctx, half, size):
        allowed = allowed_of(meta_ref, first, low, end, size)
        cols = slice(at, at + size)
        for h in range(local // HEAD_DIM):
            feats = slice(h * HEAD_DIM, (h + 1) * HEAD_DIM)
            q = q_ref[cols] * head_mask(h, local)
            s = dot(k_ref[low:end], q, 1, 1)
            s = jnp.where(allowed, s * LOG2_SCALE, MASKED)
            top = jnp.max(s, axis=0, keepdims=True)
            p = jnp.exp2(s - top)
            total = jnp.sum(p, axis=0, keepdims=True)
            p = p * (1.0 / total)
            lse_ref[h : h + 1, cols] = top + jnp.log2(total)
            mix = dot(vt_ref[feats, low:end], p.astype(BF16), 1, 0)
            mix_ref[feats, cols] = mix.astype(BF16)


def attend_kernel(size, meta_ref, q_ref, kv_ref, mix_ref, lse_ref, k_all, vt_all):
    half, local = q_ref.shape
    ctx = meta_ref[1]

    @pl.when(ctx == 0)
    def _():
        k_all[:half] = kv_ref[:half, :local]
        kvt = kv_ref[:half].T
        vt_all[:, :half] = kvt[local:]
        attend_body(0, size, meta_ref, q_ref, k_all, vt_all, mix_ref, lse_ref)

    @pl.when(ctx != 0)
    def _():
        k_all[...] = kv_ref[:, :local]
        kvt = kv_ref[...].T
        vt_all[...] = kvt[local:]
        attend_body(1, size, meta_ref, q_ref, k_all, vt_all, mix_ref, lse_ref)


def back_body(ctx, size, meta_ref, q_ref, d_ref, lse_ref, k_ref, kt_ref, v_ref, dq_ref, dk, dv, p_all, s_all):
    half, local = q_ref.shape
    heads = local // HEAD_DIM
    for at, first, low, end in blocks_of(ctx, half, size):
        allowed = allowed_of(meta_ref, first, low, end, size)
        cols = slice(at, at + size)
        keys = slice(low, end)
        qs, ds = [], []
        for h in range(heads):
            feats = slice(h * HEAD_DIM, (h + 1) * HEAD_DIM)
            mask = head_mask(h, local)
            q = q_ref[cols] * mask
            d = d_ref[cols] * mask
            qs.append(q)
            ds.append(d)
            s = dot(k_ref[keys], q, 1, 1)
            p = jnp.exp2(jnp.where(allowed, s * LOG2_SCALE - lse_ref[h : h + 1, cols], MASKED))
            dp = dot(v_ref[keys], d, 1, 1)
            center = jnp.sum(p * dp, axis=0, keepdims=True)
            score = (p * (dp - center)).astype(BF16)
            lanes = slice(h * size, (h + 1) * size)
            p_all[keys, lanes] = p.astype(BF16)
            s_all[keys, lanes] = score
            dq_ref[feats, cols] = (dot(kt_ref[feats, keys], score, 1, 0) * SCALE).astype(BF16)
        dk[keys] += dot(s_all[keys], jnp.concatenate(qs, 0), 1, 0)
        dv[keys] += dot(p_all[keys], jnp.concatenate(ds, 0), 1, 0)


def back_kernel(
    size, meta_ref, q_ref, kv_ref, lse_ref, b0, b1, b2, b3, w_ref,
    dq_ref, keep_ref, send_ref, rows_ref, k_all, kt_all, v_all, d_all, dk, dv, p_all, s_all,
):
    half, local = q_ref.shape
    own = b0.shape[0]
    rank, ctx = meta_ref[0], meta_ref[1]
    for r, b in enumerate((b0, b1, b2, b3)):
        rows_ref[rows_at(rank ^ r, own)] = b[...]
    d_all[...] = dot(rows_ref[...], w_ref[...], 1, 1).astype(BF16)
    rest = (dq_ref, dk, dv, p_all, s_all)

    @pl.when(ctx == 0)
    def _():
        k_all[:half] = kv_ref[:half, :local]
        v_all[:half] = kv_ref[:half, local:]
        kt_all[:, :half] = k_all[:half].T
        dk[:half] = jnp.zeros((half, local), F32)
        dv[:half] = jnp.zeros((half, local), F32)
        back_body(0, size, meta_ref, q_ref, d_all, lse_ref, k_all, kt_all, v_all, *rest)
        keep_ref[:, :local] = dk[:half] * SCALE
        keep_ref[:, local:] = dv[:half]
        send_ref[...] = jnp.zeros(send_ref.shape, BF16)

    @pl.when(ctx != 0)
    def _():
        k_all[...] = kv_ref[:, :local]
        v_all[...] = kv_ref[:, local:]
        kt_all[...] = k_all[...].T
        dk[...] = jnp.zeros(dk.shape, F32)
        dv[...] = jnp.zeros(dv.shape, F32)
        back_body(1, size, meta_ref, q_ref, d_all, lse_ref, k_all, kt_all, v_all, *rest)
        send_ref[:, :local] = (dk[:half] * SCALE).astype(BF16)
        send_ref[:, local:] = dv[:half].astype(BF16)
        keep_ref[:, :local] = dk[half:] * SCALE
        keep_ref[:, local:] = dv[half:]


def ff_kernel(
    meta_ref, m0, m1, m2, m3, x_ref, w_ref, wa_ref, wb_ref, ob_ref, gain_ref, shift_ref, up_ref, ub_ref, down_ref, c0, c1, c2, c3,
    normed_ref, active_ref, upg_ref, cot_ref, hidden_ref, s0, s1, s2, s3, ub_out, db_out, w_all, mix_all, part,
):
    own = c0.shape[0]
    half = x_ref.shape[0]
    local = w_ref.shape[0]
    rank, ctx = meta_ref[0], meta_ref[1]
    piece = local // 2
    w_all[:local] = w_ref[...]
    for r in range(wa_ref.shape[0] // piece):
        w_all[rows_at(2 * (r + 1) + ctx, piece)] = wa_ref[r * piece : (r + 1) * piece]
        w_all[rows_at(2 * (r + 1) + 1 - ctx, piece)] = wb_ref[rows_at((1 - ctx) * 3 + r, piece)]
    for r, m in enumerate((m0, m1, m2, m3)):
        mix_all[r * local : (r + 1) * local] = m[...]
    for r, c in enumerate((c0, c1, c2, c3)):
        cot_ref[rows_at(rank ^ r, own)] = c[...]
    chunk = 256
    ob, gain, shift, ub = vec(ob_ref), vec(gain_ref), vec(shift_ref), vec(ub_ref)
    ub_total = jnp.zeros(ub_out.shape, F32)
    db_total = jnp.zeros(db_out.shape, F32)
    for i in range(half // chunk):
        at = slice(i * chunk, (i + 1) * chunk)
        hidden = dot(mix_all[:, at], w_all[...], 0, 0) + x_ref[at].astype(F32) + ob
        part[at] = hidden
        xhat, _ = norm_parts(hidden)
        normed_ref[at] = (xhat * gain + shift).astype(BF16)
    hidden_ref[...] = part[rows_at(rank, own)]
    for i in range(half // chunk):
        at = slice(i * chunk, (i + 1) * chunk)
        v = dot(normed_ref[at], up_ref[...], 1, 0) + ub
        d = dot(cot_ref[at], down_ref[...], 1, 1)
        square = v * v
        t = jnp.tanh(0.7978845608028654 * v * (1.0 + 0.044715 * square))
        active_ref[at] = (0.5 * v * (1.0 + t)).astype(BF16)
        slope = 0.5 * (1.0 + t) + (0.5 * 0.7978845608028654) * v * (1.0 - t * t) * (
            1.0 + 3.0 * 0.044715 * square
        )
        g = (d * slope).astype(BF16)
        upg_ref[at] = g
        ub_total += jnp.sum(g.astype(F32), axis=0, keepdims=True)
        db_total += jnp.sum(cot_ref[at].astype(F32), axis=0, keepdims=True)
        part[at] = dot(g, up_ref[...], 1, 1)
    ub_out[...] = ub_total
    db_out[...] = db_total
    s0[...] = part[rows_at(rank, own)]
    for r, s in enumerate((s1, s2, s3), 1):
        s[...] = part[rows_at(rank ^ r, own)].astype(BF16)


def quarters_out(meta_ref, total, quarters):
    ctx, bit = meta_ref[1], meta_ref[6]
    size = quarters[0].shape[0]
    own, near, far_near, far_own = quarters
    own[...] = total[rows_at(2 * ctx + bit, size)]
    near[...] = total[rows_at(2 * ctx + 1 - bit, size)]
    far_near[...] = total[rows_at(3 - 2 * ctx - bit, size)]
    far_own[...] = total[rows_at(2 - 2 * ctx + bit, size)]


def weight_grad_kernel(meta_ref, a_ref, b_ref, *refs):
    total = refs[4]
    total[...] = dot(a_ref[...], b_ref[...], 0, 0).astype(BF16)
    quarters_out(meta_ref, total, refs[:4])


def out_part_kernel(meta_ref, active_ref, down_ref, s0, s1, s2, s3, part):
    rank = meta_ref[0]
    own = s0.shape[0]
    part[...] = dot(active_ref[...], down_ref[...], 1, 0)
    s0[...] = part[rows_at(rank, own)]
    for r, s in enumerate((s1, s2, s3), 1):
        s[...] = part[rows_at(rank ^ r, own)].astype(BF16)


def sum4(refs):
    total = refs[0][...]
    for ref in refs[1:]:
        total = total + ref[...].astype(F32)
    return total


def norm2_back_kernel(s0, g1, g2, g3, hidden_ref, cot_ref, gain_ref, grad_ref, low_ref, small_ref):
    grad = sum4((s0, g1, g2, g3))
    xhat, scale = norm_parts(hidden_ref[...])
    hidden_grad = cot_ref[...].astype(F32) + norm_back(grad, vec(gain_ref), xhat, scale)
    grad_ref[...] = hidden_grad
    low_ref[...] = hidden_grad.astype(BF16)
    small_ref[0:1] = jnp.sum(grad * xhat, axis=0, keepdims=True)
    small_ref[1:2] = jnp.sum(grad, axis=0, keepdims=True)


def q_back_kernel(
    meta_ref, dq_ref, normed_ref, mix_ref, rows_ref, w_ref, t0, t1, t2, t3, part_ref, qb_ref, ob_ref, total
):
    local = dq_ref.shape[0]
    dq = dq_ref[...]
    total[:local] = dot(dq, normed_ref[...], 1, 0).astype(BF16)
    total[local:] = dot(mix_ref[...], rows_ref[...], 1, 0).astype(BF16)
    quarters_out(meta_ref, total, (t0, t1, t2, t3))
    part_ref[...] = dot(dq, w_ref[:local], 0, 0)
    qb_ref[...] = dot(jnp.ones((8, dq.shape[1]), BF16), dq, 1, 1)[0:1]
    ob_ref[...] = jnp.sum(rows_ref[...].astype(F32), axis=0, keepdims=True)


def kv_back_kernel(
    meta_ref, keep_kv, got_kv, normed_ref, w_ref, x_ref, norm2_ref, qpart_ref,
    t0, t1, t2, t3, s0, s1, s2, s3, norm_ref, vb_ref, total, part,
):
    rank, ctx = meta_ref[0], meta_ref[1]
    own, width = s0.shape
    half, local = keep_kv.shape[0], keep_kv.shape[1] // 2
    normed = normed_ref[...]
    dkv = (keep_kv[...] + got_kv[rows_at(1 - ctx, half)].astype(F32)).astype(BF16)
    total[...] = dot(dkv, normed, 0, 0).astype(BF16)
    quarters_out(meta_ref, total, (t0, t1, t2, t3))
    part[...] = qpart_ref[...] + dot(dkv, w_ref[local:], 1, 0)
    gain_total = jnp.zeros((1, width), F32)
    shift_total = jnp.zeros((1, width), F32)
    chunk = 128
    for c in range(half // chunk):
        at = slice(c * chunk, (c + 1) * chunk)
        xhat, _ = norm_parts(x_ref[at].astype(F32))
        gain_total += jnp.sum(part[at] * xhat, axis=0, keepdims=True)
        shift_total += jnp.sum(part[at], axis=0, keepdims=True)
    norms = jnp.concatenate(
        [gain_total, shift_total, norm2_ref[...], jnp.zeros((4, width), F32)], 0
    )
    norm_ref[...] = norms
    high = norms.astype(BF16)
    tail = jnp.concatenate([high.astype(F32), norms - high.astype(F32)], 0).astype(BF16)
    s0[...] = part[rows_at(rank, own)]
    for r, s in enumerate((s1, s2, s3), 1):
        s[:own] = part[rows_at(rank ^ r, own)].astype(BF16)
        s[own:] = tail
    vb_ref[...] = jnp.sum(dkv.astype(F32), axis=0, keepdims=True)[:, local:]


def norm1_back_kernel(
    s0, g1, g2, g3, x_ref, gain_ref, hidden_ref, norm_ref, ob_ref, db_ref, ub_ref, qb_ref, vb_ref, out_ref, small_ref
):
    own = s0.shape[0]
    grad = s0[...]
    norms = norm_ref[...]
    for g in (g1, g2, g3):
        grad = grad + g[:own].astype(F32)
        tail = g[own:].astype(F32)
        norms = norms + (tail[:8] + tail[8:])
    xhat, scale = norm_parts(x_ref[...].astype(F32))
    out = hidden_ref[...] + norm_back(grad, vec(gain_ref), xhat, scale)
    out_ref[...] = out.astype(BF16)
    local = qb_ref.shape[1]
    small_ref[0:4] = norms[:4]
    small_ref[4:5] = ob_ref[...]
    small_ref[5:6] = db_ref[...]
    small_ref[6:7] = ub_ref[...]
    small_ref[7:8] = jnp.zeros_like(ob_ref)
    small_ref[7:8, :local] = qb_ref[...]
    lanes = small_ref.shape[1] // 2
    small_ref[7:8, lanes : lanes + local] = vb_ref[...]


def output_kernel(s0, g1, g2, g3, hidden_ref, bias_ref, out_ref):
    out_ref[...] = (hidden_ref[...] + sum4((s0, g1, g2, g3)) + vec(bias_ref)).astype(BF16)


def place(meta_ref, own_ref, other_ref, own_all, other_all, out_ref):
    ctx, bit = meta_ref[1], meta_ref[6]
    size = own_ref.shape[0]
    out_ref[rows_at(2 * ctx + bit, size)] = own_ref[...].astype(F32)
    out_ref[rows_at(2 * ctx + 1 - bit, size)] = other_ref[...].astype(F32)
    peer = rows_at(1 - ctx, size)
    out_ref[rows_at(2 - 2 * ctx + bit, size)] = own_all[peer].astype(F32)
    out_ref[rows_at(3 - 2 * ctx - bit, size)] = other_all[peer].astype(F32)


def whole_kernel(meta_ref, own_ref, other_ref, own_all, other_all, out_ref):
    place(meta_ref, own_ref, other_ref, own_all, other_all, out_ref)


def attn_whole_kernel(meta_ref, *refs):
    qkv_out, out_out, total = refs[8:]
    local = out_out.shape[0]
    place(meta_ref, *refs[:4], total)
    qkv_out[:local] = total[:local]
    out_out[...] = total[local:]
    place(meta_ref, *refs[4:8], total)
    qkv_out[local:] = total[...]


def small_kernel(a, b, c, d, *outs):
    total = a[...] + b[...] + c[...] + d[...]
    for i, out in enumerate(outs[:7]):
        out[...] = total[i]
    local = outs[7].shape[0]
    lanes = total.shape[1] // 2
    outs[7][...] = total[7, :local]
    outs[8][...] = total[7, lanes : lanes + local]


def to_peers(blocks):
    return [
        lax.ppermute(b, "tensor", xor_pairs(lax.axis_size("tensor"), r))
        for r, b in enumerate(blocks, 1)
    ]


NEAR, FAR = xor_pairs(4, 1), xor_pairs(4, 2)


def peer_add_kernel(meta_ref, a_ref, pair_ref, out_ref):
    size = a_ref.shape[0]
    got = pair_ref[rows_at(1 - meta_ref[1], size)].astype(F32)
    out_ref[...] = (a_ref[...].astype(F32) + got).astype(BF16)


def peer_add2_kernel(meta_ref, a_ref, pair_ref, b_ref, out_ref):
    size = a_ref.shape[0]
    got = pair_ref[rows_at(1 - meta_ref[1], size)].astype(F32)
    out_ref[...] = (a_ref[...].astype(F32) + got + b_ref[...].astype(F32)).astype(BF16)


def add_kernel(a_ref, b_ref, out_ref):
    out_ref[...] = (a_ref[...].astype(F32) + b_ref[...].astype(F32)).astype(BF16)


class Order:
    def __init__(self):
        self.last = None

    def first(self, x):
        return x if self.last is None else after(x, self.last)

    def call(self, kernel, out_shape, args, at=-1, **kw):
        args = list(args)
        args[at] = self.first(args[at])
        out = call(kernel, out_shape, args, **kw)
        self.last = out[0]
        return out

    def pair(self, x):
        self.last = lax.all_gather(self.first(x), "ctx", axis=0, tiled=True)
        return self.last


class WeightSum:
    def __init__(self, order, meta, quarters):
        self.order, self.meta = order, meta
        self.own, self.near, self.far_near, self.far_own = quarters
        self.shape = [shape(self.own.shape, BF16)]
        self.short = lax.axis_size("dp") == 4

    def one(self):
        got = self.order.pair(self.far_near)
        (send,) = self.order.call(
            peer_add_kernel, self.shape, [self.meta, self.near, got], smem=1
        )
        self.got = lax.ppermute(send, "dp", NEAR) if self.short else lax.psum(send, "dp")

    def two(self):
        self.pairs = self.order.pair(self.far_own)

    def three(self):
        other = self.got if self.short else jnp.zeros_like(self.got)
        (self.own,) = self.order.call(
            peer_add2_kernel, self.shape, [self.meta, self.own, self.pairs, other], smem=1
        )
        if self.short:
            self.got = lax.ppermute(self.own, "dp", FAR)
        else:
            self.own = lax.psum(self.own, "dp")

    def four(self):
        if self.short:
            (self.own,) = self.order.call(add_kernel, self.shape, [self.own, self.got])
            self.got = lax.ppermute(self.own, "dp", NEAR)

    def five(self):
        self.own_all = self.order.pair(self.own)

    def six(self):
        self.got_all = self.order.pair(self.got)

    def parts(self):
        return [self.own, self.got, self.own_all, self.got_all]

    def whole(self):
        rows, cols = self.own.shape
        return self.order.call(
            whole_kernel, [shape((4 * rows, cols), F32)], [self.meta, *self.parts()], smem=1
        )[0]


def per_device(
    tokens,
    lengths,
    norm1_gain,
    norm1_shift,
    qkv_weight,
    query_bias,
    value_bias,
    out_weight,
    out_bias,
    norm2_gain,
    norm2_shift,
    up_weight,
    up_bias,
    down_weight,
    down_bias,
    cotangent,
):
    tokens, cotangent = tokens[0], cotangent[0]
    own, width = tokens.shape
    ranks = lax.axis_size("tensor")
    half = own * ranks
    full = half * lax.axis_size("ctx")
    local = qkv_weight.shape[2]
    hidden_units = up_weight.shape[1]
    rank = lax.axis_index("tensor")
    ctx = lax.axis_index("ctx")
    bit = lax.axis_index("dp") & 1
    meta = jnp.concatenate(
        [jnp.stack([rank, ctx]).astype(jnp.int32), lengths[0], bit.astype(jnp.int32)[None]]
    )
    weight_t = jnp.transpose(qkv_weight, (1, 2, 0)).reshape(3 * local, width)
    size = 128
    block = shape((own, width), F32)
    block_low = shape((own, width), BF16)
    row_out = shape((1, width), F32)

    def quarters(rows_all, cols):
        return [shape((rows_all // 4, cols), BF16)] * 4

    order = Order()
    xs = to_peers([tokens] * 3)
    out_half = pick(out_weight.reshape(2, local // 2, width), ctx)
    out_halves = to_peers([out_half] * 3)
    rows, normed1, q, kv = order.call(
        qkv_kernel,
        [shape((half, width), BF16)] * 2
        + [shape((half, local), BF16), shape((half, 2 * local), BF16)],
        [meta, tokens, *xs, norm1_gain, norm1_shift, weight_t, query_bias, value_bias],
        smem=1,
    )
    cots = to_peers([after(cotangent, kv)] * 3)
    kv_all = order.pair(kv)
    mix, lse = order.call(
        functools.partial(attend_kernel, size),
        [shape((local, half), BF16), shape((8, half), F32)],
        [meta, q, kv_all],
        smem=1,
        scratch=[pltpu.VMEM((full, local), BF16), pltpu.VMEM((local, full), BF16)],
    )
    mixes = to_peers([mix] * 3)
    out_half = jnp.concatenate([after(out_halves[0], mix, *cots), *out_halves[1:]], 0)
    out_both = order.pair(out_half)
    (normed2, active, up_grad, cot_rows, hidden, *normed2_parts, up_bias_part, down_bias_part) = order.call(
        ff_kernel,
        [
            shape((half, width), BF16),
            shape((half, hidden_units), BF16),
            shape((half, hidden_units), BF16),
            shape((half, width), BF16),
            block,
            block,
            block_low,
            block_low,
            block_low,
            shape((1, hidden_units), F32),
            row_out,
        ],
        [meta, mix, *mixes, rows, out_weight, out_half, out_both, out_bias, norm2_gain, norm2_shift]
        + [up_weight, up_bias, down_weight, cotangent, *cots],
        smem=1,
        vmem=28,
        scratch=[
            pltpu.VMEM((ranks * local, width), BF16),
            pltpu.VMEM((ranks * local, half), BF16),
            pltpu.VMEM((half, width), F32),
        ],
    )
    normed2_got = to_peers(normed2_parts[1:])

    def weight_grad(a, b):
        rows_all, cols = a.shape[1], b.shape[1]
        out = order.call(
            weight_grad_kernel,
            quarters(rows_all, cols),
            [meta, a, b],
            smem=1,
            scratch=[pltpu.VMEM((rows_all, cols), BF16)],
        )
        return WeightSum(order, meta, out)

    down_sum = weight_grad(active, cot_rows)
    down_sum.one()
    up_sum = weight_grad(normed2, up_grad)
    hidden_grad, branch_grad, norm2_part = order.call(
        norm2_back_kernel,
        [block, block_low, shape((2, width), F32)],
        [normed2_parts[0], *normed2_got, hidden, cotangent, norm2_gain],
        at=0,
    )
    branches = to_peers([branch_grad] * 3)
    down_sum.two()
    up_sum.one()
    out_parts = order.call(
        out_part_kernel,
        [block, block_low, block_low, block_low],
        [meta, active, down_weight],
        at=1,
        smem=1,
        scratch=[pltpu.VMEM((half, width), F32)],
    )
    down_sum.three()
    up_sum.two()
    dq, kv_keep, kv_send, branch_rows = order.call(
        functools.partial(back_kernel, size),
        [
            shape((local, half), BF16),
            shape((half, 2 * local), F32),
            shape((half, 2 * local), BF16),
            shape((half, width), BF16),
        ],
        [meta, q, kv_all, lse, branch_grad, *branches, out_weight],
        at=1,
        smem=1,
        vmem=24,
        scratch=[
            pltpu.VMEM((full, local), BF16),
            pltpu.VMEM((local, full), BF16),
            pltpu.VMEM((full, local), BF16),
            pltpu.VMEM((half, local), BF16),
            pltpu.VMEM((full, local), F32),
            pltpu.VMEM((full, local), F32),
            pltpu.VMEM((full, local // HEAD_DIM * size), BF16),
            pltpu.VMEM((full, local // HEAD_DIM * size), BF16),
        ],
    )
    up_sum.three()
    kv_got = order.pair(kv_send)
    *qo_quarters, q_part, q_bias_part, out_bias_part = order.call(
        q_back_kernel,
        quarters(2 * local, width) + [shape((half, width), F32), shape((1, local), F32), row_out],
        [meta, dq, normed1, mix, branch_rows, weight_t],
        at=1,
        smem=1,
        scratch=[pltpu.VMEM((2 * local, width), BF16)],
    )
    qo_sum = WeightSum(order, meta, qo_quarters)
    qo_sum.one()
    tail_low = shape((own + 16, width), BF16)
    *kv_quarters, n0, n1, n2, n3, norm_part, v_bias_part = order.call(
        kv_back_kernel,
        quarters(2 * local, width)
        + [block, tail_low, tail_low, tail_low, shape((8, width), F32), shape((1, local), F32)],
        [meta, kv_keep, kv_got, normed1, weight_t, rows, norm2_part, q_part],
        smem=1,
        scratch=[pltpu.VMEM((2 * local, width), BF16), pltpu.VMEM((half, width), F32)],
    )
    normed1_got = to_peers([n1, n2, n3])
    kv_sum = WeightSum(order, meta, kv_quarters)
    kv_sum.one()
    down_sum.four()
    qo_sum.two()
    down_sum.five()
    qo_sum.three()
    input_grad, small = order.call(
        norm1_back_kernel,
        [block_low, shape((8, width), F32)],
        [n0, *normed1_got, tokens, norm1_gain, hidden_grad, norm_part, out_bias_part]
        + [down_bias_part, up_bias_part, q_bias_part, v_bias_part],
        at=0,
    )
    out_got = to_peers([after(b, input_grad) for b in out_parts[1:]])
    kv_sum.two()
    kv_sum.three()
    small = order.pair(small)
    small = small[:8] + small[8:]
    down_sum.six()
    up_sum.four()
    up_sum.five()
    if lax.axis_size("dp") == 4:
        smalls = [small] + [lax.ppermute(small, "dp", xor_pairs(4, r)) for r in (1, 2, 3)]
    else:
        small = lax.psum(small, "dp")
        smalls = [small] + [jnp.zeros_like(small)] * 3
    (output,) = order.call(
        output_kernel, [block_low], [out_parts[0], *out_got, hidden, down_bias], at=0
    )
    down_grad = down_sum.whole()
    qo_sum.four()
    qo_sum.five()
    kv_sum.four()
    kv_sum.five()
    up_sum.six()
    up_weight_grad = up_sum.whole()
    outs = order.call(
        small_kernel,
        [shape((width,), F32)] * 7 + [shape((local,), F32)] * 2,
        smalls,
        at=0,
    )
    qo_sum.six()
    kv_sum.six()
    attn_grad, out_weight_grad = order.call(
        attn_whole_kernel,
        [shape((3 * local, width), F32), shape((local, width), F32)],
        [meta, *qo_sum.parts(), *kv_sum.parts()],
        smem=1,
        scratch=[pltpu.VMEM((2 * local, width), F32)],
    )
    n1g, n1s, n2g, n2s, out_bias_grad, down_bias_grad, up_bias_grad, q_bias_grad, v_bias_grad = outs
    return (
        output[None],
        input_grad[None],
        n1g,
        n1s,
        jnp.transpose(attn_grad.reshape(3, local, width), (2, 0, 1)),
        q_bias_grad,
        v_bias_grad,
        out_weight_grad,
        out_bias_grad,
        n2g,
        n2s,
        up_weight_grad,
        up_bias_grad,
        down_grad,
        down_bias_grad,
    )


def solution(mesh):
    row_spec = P("dp", ("ctx", "tensor"), None)
    return jax.shard_map(
        per_device,
        mesh=mesh,
        in_specs=(
            row_spec,
            P("dp", None),
            P(),
            P(),
            P(None, None, "tensor"),
            P("tensor"),
            P("tensor"),
            P("tensor", None),
            P(),
            P(),
            P(),
            P(None, "tensor"),
            P("tensor"),
            P("tensor", None),
            P(),
            row_spec,
        ),
        out_specs=(
            row_spec,
            row_spec,
            P(),
            P(),
            P(None, None, "tensor"),
            P("tensor"),
            P("tensor"),
            P("tensor", None),
            P(),
            P(),
            P(),
            P(None, "tensor"),
            P("tensor"),
            P("tensor", None),
            P(),
        ),
        check_vma=False,
    )
```

time: 224 us -> 164 us (0.73)
  waiting for transfers between devices: 64.6 us -> 19.4 us
  Pallas kernels: 0 us -> 38.4 us
  local copies, waits for them, and re-layouts: 31.1 us -> 5.83 us
  other arithmetic: 25.7 us -> 0.74 us
  matrix products: 22.1 us -> 0 us
  starting transfers between devices: 39 us -> 51.2 us
  blocking collectives: 38.8 us -> 46.7 us
    ppermute x40 -> x39, waiting for transfers between devices: 64.6 us -> 19.4 us  [the longest x24 15.6 us: to_peers(): lax.ppermute(b, 'tensor', xor_pairs(lax.axis_size('tensor'), r))]
    pallas_call x0 -> x28, Pallas kernels: none -> 38.4 us  [call(): pl.pallas_call(kernel, out_shape=out_shape, in_specs=[pl.BlockSpec(memory...]
    dot_general x18 -> x0, matrix products: 22.1 us -> none  [the longest x12 13.1 us: dot(): lax.dot_general(a, b, (((ca,), (cb,)), ((), ())), preferred_element_type=...]
    ppermute x40 -> x39, starting transfers between devices: 39 us -> 51.2 us  [the longest x24 30.5 us: to_peers(): lax.ppermute(b, 'tensor', xor_pairs(lax.axis_size('tensor'), r))]
    convert_element_type x20 -> x0, other arithmetic: 12.2 us -> none  [the longest x9 3.84 us: add_low(): return (a.astype(F32) + b.astype(F32)).astype(BF16)]
    concatenate x5 -> x1, local copies, waits for them, and re-layouts: 9.32 us -> 0.01 us  [per_device(): jnp.concatenate([after(out_halves[0], mix, *cots), *out_halves[1:]], 0)]
    all_gather x3 -> x20, blocking collectives: 38.8 us -> 46.7 us  [pair(): self.last = lax.all_gather(self.first(x), 'ctx', axis=0, tiled=True)]
    squeeze x10 -> x1, local copies, waits for them, and re-layouts: 7.2 us -> 0.92 us  [pick(): return lax.dynamic_index_in_dim(x, index, 0, keepdims=False)]
  transfers between devices with their start and end apart: 40 -> 39, of which waited for: 12 -> 10; matrix products, arithmetic and copies ran while one was open for 28% -> 1% of each run, Pallas kernels for 0% -> 20%
where the time goes in v2:
time: 164 us; the launch traced here: 163 us
  starting transfers between devices  51.2 us (31%)
  blocking collectives  46.7 us (28%)
  Pallas kernels  38.4 us (23%)
  waiting for transfers between devices  19.4 us (12%)
  local copies, waits for them, and re-layouts  5.83 us (4%)
    all_gather x20, blocking collectives, pair(): self.last = lax.all_gather(self.first(x), 'ctx', axis=0, tiled=True)  46.7 us
    pallas_call x28, Pallas kernels, call(): pl.pallas_call(kernel, out_shape=out_shape, in_specs=[pl.BlockSpec(memory...  38.4 us
    ppermute x24, starting transfers between devices, to_peers(): lax.ppermute(b, 'tensor', xor_pairs(lax.axis_size('tensor'), r))  30.5 us
    ppermute x24, waiting for transfers between devices, to_peers(): lax.ppermute(b, 'tensor', xor_pairs(lax.axis_size('tensor'), r))  15.6 us
    ppermute x4, starting transfers between devices, three(): self.got = lax.ppermute(self.own, 'dp', FAR)  7.83 us
    ppermute x4, starting transfers between devices, one(): lax.ppermute(send, 'dp', NEAR)  5.45 us
    unnamed x38, local copies, waits for them, and re-layouts  4.9 us
    ppermute x3, starting transfers between devices, per_device(): lax.ppermute(small, 'dp', xor_pairs(4, r))  4.38 us
  transfers between devices with their start and end apart: 39, of which 10 were waited for; matrix products, arithmetic and copies ran while one was open for 1% of the time, Pallas kernels for 20%

profile of v2, /device:TPU:0, one launch (start us, length us, event | category | flops | bytes accessed | tf_op | source)
XLA Modules:
  0.0 163.3 jit_solution(14868080852249778950)
XLA Ops:
  0.7 4.0 %collective-permute-start.2 = (bf16[128,768]{1,0:T(8,128)(2,1)}, bf16[128,768]{1,0:T(8,128)(2,1)S(1)}, u32[]{:S(2)}, u32[]{:S(2)}) collective-permute-start(bf16[128,768]{1,0:T(8,128)(2,1)} %bitcast.26), channel_id=1, source_target_pairs={{0,6},{2,4},{4,2},{6,0},{1,7},{3,5},{5,3},{7,1},{8,14},{10,12},{12... | collective-permute-start | bytes 589832 | tf_op jit(solution)/shard_map/ppermute | solution.py:426
  6.2 2.0 %collective-permute-start.10 = (bf16[96,768]{1,0:T(8,128)(2,1)S(1)}, bf16[96,768]{1,0:T(8,128)(2,1)S(1)}, u32[]{:S(2)}, u32[]{:S(2)}) collective-permute-start(bf16[96,768]{1,0:T(8,128)(2,1)S(1)} %dynamic-slice_bitcast_fusion), channel_id=1, source_target_pairs={{0,4},{2,6},{4,0},{6,2},{1,5},{3,7},{5,1},{7,3},{8,12},{10,14},{12... | collective-permute-start | bytes 442376 | tf_op jit(solution)/shard_map/ppermute | solution.py:426
  8.2 1.5 collective-permute-start.6
  10.6 3.4 %collective-permute-done.1.x2 = bf16[128,768]{1,0:T(8,128)(2,1)S(1)} collective-permute-done((bf16[128,768]{1,0:T(8,128)(2,1)}, bf16[128,768]{1,0:T(8,128)(2,1)S(1)}, u32[]{:S(2)}, u32[]{:S(2)}) %collective-permute-start.1) | collective-permute-done | bytes 196640 | tf_op jit(solution)/shard_map/ppermute | solution.py:426
  14.0 1.3 collective-permute-done.x1
  15.4 1.2 copy-done
  20.2 2.1 %shard_map.271 = (bf16[512,768]{1,0:T(8,128)(2,1)S(1)}, bf16[512,768]{1,0:T(8,128)(2,1)S(1)}, bf16[512,192]{1,0:T(8,128)(2,1)S(1)}, bf16[512,384]{1,0:T(8,128)(2,1)S(1)}) custom-call(s32[7]{0:T(128)S(1)} %pad_add_fusion.meta_ref, bf16[128,768]{1,0:T(8,128)(2,1)S(1)} %bitcast.29, bf16[128,768]{1,0:T(8,128)(2,1)S(1)} %collective-permute-done.x1, ...), custom_call_target="tpu_custom_call" | custom-call | tf_op jit(solution)/shard_map/pallas_call | solution.py:58
  22.3 1.5 collective-permute-start.9
  23.8 1.5 collective-permute-start.8
  25.8 2.4 %all_gather.60.kv_ref = bf16[1024,384]{1,0:T(8,128)(2,1)S(1)} all-gather(bf16[512,384]{1,0:T(8,128)(2,1)S(1)} %get-tuple-element.130), channel_id=1, replica_groups=mesh['dp'=4,'tensor'=4,'ctx'=2] {'ctx'}, dimensions={0}, use_global_device_ids=true | all-gather | bytes 1179648 | tf_op jit(solution)/shard_map/all_gather | solution.py:465
  28.2 4.5 %shard_map.272 = (bf16[192,512]{1,0:T(8,128)(2,1)S(1)}, f32[8,512]{1,0:T(8,128)S(1)}) custom-call(s32[7]{0:T(128)S(1)} %pad_add_fusion.meta_ref, bf16[512,192]{1,0:T(8,128)(2,1)S(1)} %get-tuple-element.165.q_ref, bf16[1024,384]{1,0:T(8,128)(2,1)S(1)} %all_gather.60.kv_ref), custom_call_target="tpu_custom_call" | custom-call | tf_op jit(solution)/shard_map/pallas_call | solution.py:58
  32.7 1.5 collective-permute-start.11
  34.2 1.5 collective-permute-start.5
  36.1 1.6 collective-permute-start.3
  37.8 1.6 collective-permute-done.11
  39.4 4.5 %all_gather.61.wb_ref = bf16[576,768]{1,0:T(8,128)(2,1)S(1)} all-gather(bf16[288,768]{1,0:T(8,128)(2,1)S(1)} %constant_dynamic-update-slice_fusion.wa_ref), channel_id=1, replica_groups=mesh['dp'=4,'tensor'=4,'ctx'=2] {'ctx'}, dimensions={0}, use_global_device_ids=true | all-gather | bytes 1327104 | tf_op jit(solution)/shard_map/all_gather | solution.py:465
  43.9 4.9 %collective-permute-done.4.m2 = bf16[192,512]{1,0:T(8,128)(2,1)S(1)} collective-permute-done((bf16[192,512]{1,0:T(8,128)(2,1)S(1)}, bf16[192,512]{1,0:T(8,128)(2,1)S(1)}, u32[]{:S(2)}, u32[]{:S(2)}) %collective-permute-start.4) | collective-permute-done | bytes 196640 | tf_op jit(solution)/shard_map/ppermute | solution.py:426
  48.9 4.3 %shard_map.273 = (bf16[512,768]{1,0:T(8,128)(2,1)S(1)}, bf16[512,768]{1,0:T(8,128)(2,1)S(1)}, bf16[512,768]{1,0:T(8,128)(2,1)S(1)}, bf16[512,768]{1,0:T(8,128)(2...) custom-call(s32[7]{0:T(128)S(1)} %pad_add_fusion.meta_ref, ...), custom_call_target="tpu_custom_call" | custom-call | tf_op jit(solution)/shard_map/pallas_call | solution.py:58
  53.2 1.5 collective-permute-start.12
  55.2 1.5 collective-permute-start.14
  56.7 1.4 shard_map.274
  58.2 2.2 %all_gather.62.pair_ref = bf16[384,768]{1,0:T(8,128)(2,1)S(1)} all-gather(bf16[192,768]{1,0:T(8,128)(2,1)S(1)} %get-tuple-element.145), channel_id=1, replica_groups=mesh['dp'=4,'tensor'=4,'ctx'=2] {'ctx'}, dimensions={0}, use_global_device_ids=true | all-gather | bytes 884736 | tf_op jit(solution)/shard_map/all_gather | solution.py:465
  61.0 1.6 %collective-permute-start.15 = (bf16[192,768]{1,0:T(8,128)(2,1)S(1)}, bf16[192,768]{1,0:T(8,128)(2,1)S(1)}, u32[]{:S(2)}, u32[]{:S(2)}) collective-permute-start(bf16[192,768]{1,0:T(8,128)(2,1)S(1)} %shard_map.275), channel_id=1, source_target_pairs={{0,8},{8,0},{16,24},{24,16},{1,9},{9,1},{17,25},{25,17},{2,10},{10... | collective-permute-start | bytes 884744 | tf_op jit(solution)/shard_map/ppermute | solution.py:481
  62.7 1.4 shard_map.276
  64.1 1.4 collective-permute-done.13.g2
  66.0 2.2 %all_gather.63.pair_ref = bf16[384,768]{1,0:T(8,128)(2,1)S(1)} all-gather(bf16[192,768]{1,0:T(8,128)(2,1)S(1)} %get-tuple-element.158), channel_id=1, replica_groups=mesh['dp'=4,'tensor'=4,'ctx'=2] {'ctx'}, dimensions={0}, use_global_device_ids=true | all-gather | bytes 884736 | tf_op jit(solution)/shard_map/all_gather | solution.py:465
  68.2 2.2 %all_gather.64.pair_ref = bf16[384,768]{1,0:T(8,128)(2,1)S(1)} all-gather(bf16[192,768]{1,0:T(8,128)(2,1)S(1)} %get-tuple-element.159), channel_id=1, replica_groups=mesh['dp'=4,'tensor'=4,'ctx'=2] {'ctx'}, dimensions={0}, use_global_device_ids=true | all-gather | bytes 884736 | tf_op jit(solution)/shard_map/all_gather | solution.py:465
  71.0 1.6 %collective-permute-start.16 = (bf16[192,768]{1,0:T(8,128)(2,1)S(1)}, bf16[192,768]{1,0:T(8,128)(2,1)S(1)}, u32[]{:S(2)}, u32[]{:S(2)}) collective-permute-start(bf16[192,768]{1,0:T(8,128)(2,1)S(1)} %shard_map.278), channel_id=1, source_target_pairs={{0,8},{8,0},{16,24},{24,16},{1,9},{9,1},{17,25},{25,17},{2,10},{10... | collective-permute-start | bytes 884744 | tf_op jit(solution)/shard_map/ppermute | solution.py:481
  72.7 1.2 collective-permute-start.19
  74.7 1.4 collective-permute-start.17
  76.2 1.4 shard_map.279
  78.2 2.7 %collective-permute-start.21 = (bf16[192,768]{1,0:T(8,128)(2,1)S(1)}, bf16[192,768]{1,0:T(8,128)(2,1)S(1)}, u32[]{:S(2)}, u32[]{:S(2)}) collective-permute-start(bf16[192,768]{1,0:T(8,128)(2,1)S(1)} %shard_map.280.a_ref), channel_id=1, source_target_pairs={{0,16},{8,24},{16,0},{24,8},{1,17},{9,25},{17,1},{25,9},{2,18},{10... | collective-permute-start | bytes 884744 | tf_op jit(solution)/shard_map/ppermute | solution.py:492
  80.9 2.2 %all_gather.65.pair_ref = bf16[384,768]{1,0:T(8,128)(2,1)S(1)} all-gather(bf16[192,768]{1,0:T(8,128)(2,1)S(1)} %get-tuple-element.164), channel_id=1, replica_groups=mesh['dp'=4,'tensor'=4,'ctx'=2] {'ctx'}, dimensions={0}, use_global_device_ids=true | all-gather | bytes 884736 | tf_op jit(solution)/shard_map/all_gather | solution.py:465
  83.1 1.3 collective-permute-done.18.b2
  84.4 5.7 %shard_map.281 = (bf16[192,512]{1,0:T(8,128)(2,1)S(1)}, f32[512,384]{1,0:T(8,128)S(1)}, bf16[512,384]{1,0:T(8,128)(2,1)S(1)}, bf16[512,768]{1,0:T(8,128)(2,1)S(1)}) custom-call(s32[7]{0:T(128)S(1)} %pad_add_fusion.meta_ref, bf16[512,192]{1,0:T(8,128)(2,1)S(1)} %get-tuple-element.165.q_ref, bf16[1024,384]{1,0:T(8,128)(2,1)S(1)} %all_gather.60.kv_ref, ...), custom_call_target="tpu_custom_call" | custom-call | tf_op jit(solution)/shard_map/pallas_call | solution.py:58
  90.8 4.2 %all_gather.66.got_kv = bf16[1024,384]{1,0:T(8,128)(2,1)S(1)} all-gather(bf16[512,384]{1,0:T(8,128)(2,1)S(1)} %get-tuple-element.172), channel_id=1, replica_groups=mesh['dp'=4,'tensor'=4,'ctx'=2] {'ctx'}, dimensions={0}, use_global_device_ids=true | all-gather | bytes 1179648 | tf_op jit(solution)/shard_map/all_gather | solution.py:465
  95.0 1.3 shard_map.283
  96.3 2.0 %all_gather.67.pair_ref = bf16[192,768]{1,0:T(8,128)(2,1)S(1)} all-gather(bf16[96,768]{1,0:T(8,128)(2,1)S(1)} %get-tuple-element.181), channel_id=1, replica_groups=mesh['dp'=4,'tensor'=4,'ctx'=2] {'ctx'}, dimensions={0}, use_global_device_ids=true | all-gather | bytes 442368 | tf_op jit(solution)/shard_map/all_gather | solution.py:465
  99.5 1.9 %shard_map.285 = (bf16[96,768]{1,0:T(8,128)(2,1)S(1)}, bf16[96,768]{1,0:T(8,128)(2,1)S(1)}, bf16[96,768]{1,0:T(8,128)(2,1)S(1)}, bf16[96,768]{1,0:T(8,128)(2,1)S...) custom-call(s32[7]{0:T(128)S(1)} %pad_add_fusion.meta_ref, ...), custom_call_target="tpu_custom_call" | custom-call | tf_op jit(solution)/shard_map/pallas_call | solution.py:58
  101.3 2.0 %all_gather.68.pair_ref = bf16[192,768]{1,0:T(8,128)(2,1)S(1)} all-gather(bf16[96,768]{1,0:T(8,128)(2,1)S(1)} %get-tuple-element.186), channel_id=1, replica_groups=mesh['dp'=4,'tensor'=4,'ctx'=2] {'ctx'}, dimensions={0}, use_global_device_ids=true | all-gather | bytes 442368 | tf_op jit(solution)/shard_map/all_gather | solution.py:465
  103.9 1.6 %collective-permute-start.27 = (bf16[96,768]{1,0:T(8,128)(2,1)S(1)}, bf16[96,768]{1,0:T(8,128)(2,1)S(1)}, u32[]{:S(2)}, u32[]{:S(2)}) collective-permute-start(bf16[96,768]{1,0:T(8,128)(2,1)S(1)} %shard_map.286), channel_id=1, source_target_pairs={{0,8},{8,0},{16,24},{24,16},{1,9},{9,1},{17,25},{25,17},{2,10},{10... | collective-permute-start | bytes 442376 | tf_op jit(solution)/shard_map/ppermute | solution.py:481
  106.2 1.2 collective-permute-start.25
  107.3 1.7 %collective-permute-start.26 = (bf16[144,768]{1,0:T(8,128)(2,1)S(1)}, bf16[144,768]{1,0:T(8,128)(2,1)S(1)}, u32[]{:S(2)}, u32[]{:S(2)}) collective-permute-start(bf16[144,768]{1,0:T(8,128)(2,1)S(1)} %get-tuple-element.196), channel_id=1, source_target_pairs={{0,6},{2,4},{4,2},{6,0},{1,7},{3,5},{5,3},{7,1},{8,14},{10,12},{12... | collective-permute-start | bytes 663560 | tf_op jit(solution)/shard_map/ppermute | solution.py:426
  109.1 2.0 %all_gather.69.pair_ref = bf16[192,768]{1,0:T(8,128)(2,1)S(1)} all-gather(bf16[96,768]{1,0:T(8,128)(2,1)S(1)} %get-tuple-element.190), channel_id=1, replica_groups=mesh['dp'=4,'tensor'=4,'ctx'=2] {'ctx'}, dimensions={0}, use_global_device_ids=true | all-gather | bytes 442368 | tf_op jit(solution)/shard_map/all_gather | solution.py:465
  111.2 2.2 %all_gather.70.own_all = bf16[384,768]{1,0:T(8,128)(2,1)S(1)} all-gather(bf16[192,768]{1,0:T(8,128)(2,1)S(1)} %shard_map.287.own_ref), channel_id=1, replica_groups=mesh['dp'=4,'tensor'=4,'ctx'=2] {'ctx'}, dimensions={0}, use_global_device_ids=true | all-gather | bytes 884736 | tf_op jit(solution)/shard_map/all_gather | solution.py:465
  113.4 2.6 %collective-permute-start.20 = (bf16[192,768]{1,0:T(8,128)(2,1)S(1)}, bf16[192,768]{1,0:T(8,128)(2,1)S(1)}, u32[]{:S(2)}, u32[]{:S(2)}) collective-permute-start(bf16[192,768]{1,0:T(8,128)(2,1)S(1)} %shard_map.282.a_ref), channel_id=1, source_target_pairs={{0,16},{8,24},{16,0},{24,8},{1,17},{9,25},{17,1},{25,9},{2,18},{10... | collective-permute-start | bytes 884744 | tf_op jit(solution)/shard_map/ppermute | solution.py:492
  117.8 2.6 %collective-permute-start.33 = (bf16[96,768]{1,0:T(8,128)(2,1)S(1)}, bf16[96,768]{1,0:T(8,128)(2,1)S(1)}, u32[]{:S(2)}, u32[]{:S(2)}) collective-permute-start(bf16[96,768]{1,0:T(8,128)(2,1)S(1)} %shard_map.288.a_ref), channel_id=1, source_target_pairs={{0,16},{8,24},{16,0},{24,8},{1,17},{9,25},{17,1},{25,9},{2,18},{10... | collective-permute-start | bytes 442376 | tf_op jit(solution)/shard_map/ppermute | solution.py:492
  121.5 2.0 %all_gather.71.pair_ref = bf16[192,768]{1,0:T(8,128)(2,1)S(1)} all-gather(bf16[96,768]{1,0:T(8,128)(2,1)S(1)} %get-tuple-element.206), channel_id=1, replica_groups=mesh['dp'=4,'tensor'=4,'ctx'=2] {'ctx'}, dimensions={0}, use_global_device_ids=true | all-gather | bytes 442368 | tf_op jit(solution)/shard_map/all_gather | solution.py:465
  124.1 1.5 collective-permute-start.28
  125.6 1.8 %all_gather.72 = f32[16,768]{1,0:T(8,128)S(1)} all-gather(f32[8,768]{1,0:T(8,128)S(1)} %get-tuple-element.208), channel_id=1, replica_groups=mesh['dp'=4,'tensor'=4,'ctx'=2] {'ctx'}, dimensions={0}, use_global_device_ids=true | all-gather | bytes 73728 | tf_op jit(solution)/shard_map/all_gather | solution.py:465
  128.1 3.7 %collective-permute-done.22.other_ref = bf16[192,768]{1,0:T(8,128)(2,1)S(1)} collective-permute-done((bf16[192,768]{1,0:T(8,128)(2,1)S(1)}, bf16[192,768]{1,0:T(8,128)(2,1)S(1)}, u32[]{:S(2)}, u32[]{:S(2)}) %collective-permute-start.22) | collective-permute-done | bytes 294944 | tf_op jit(solution)/shard_map/ppermute | solution.py:499
  131.7 1.2 collective-permute-start.30
  132.9 2.2 %all_gather.73.other_all = bf16[384,768]{1,0:T(8,128)(2,1)S(1)} all-gather(bf16[192,768]{1,0:T(8,128)(2,1)S(1)} %collective-permute-done.22.other_ref), channel_id=1, replica_groups=mesh['dp'=4,'tensor'=4,'ctx'=2] {'ctx'}, dimensions={0}, use_global_device_ids=true | all-gather | bytes 884736 | tf_op jit(solution)/shard_map/all_gather | solution.py:465
  135.7 2.2 %all_gather.74.own_all = bf16[384,768]{1,0:T(8,128)(2,1)S(1)} all-gather(bf16[192,768]{1,0:T(8,128)(2,1)S(1)} %shard_map.291.own_ref), channel_id=1, replica_groups=mesh['dp'=4,'tensor'=4,'ctx'=2] {'ctx'}, dimensions={0}, use_global_device_ids=true | all-gather | bytes 884736 | tf_op jit(solution)/shard_map/all_gather | solution.py:465
  138.6 3.3 %collective-permute-start.36 = (f32[8,768]{1,0:T(8,128)S(1)}, f32[8,768]{1,0:T(8,128)S(1)}, u32[]{:S(2)}, u32[]{:S(2)}) collective-permute-start(f32[8,768]{1,0:T(8,128)S(1)} %slice_add_fusion.a), channel_id=1, source_target_pairs={{0,24},{8,16},{16,8},{24,0},{1,25},{9,17},{17,9},{25,1},{2,26},{10... | collective-permute-start | bytes 73736 | tf_op jit(solution)/shard_map/ppermute | solution.py:707
  142.7 2.1 %shard_map.293 = f32[768,768]{1,0:T(8,128)} custom-call(s32[7]{0:T(128)S(1)} %pad_add_fusion.meta_ref, bf16[192,768]{1,0:T(8,128)(2,1)S(1)} %shard_map.287.own_ref, bf16[192,768]{1,0:T(8,128)(2,1)S(1)} %collective-permute-done.22.other_ref, bf16[384,768]{1,0:T(8,128)(2,1)S(1)} %all_gather.70.own_all, bf16[384,768]{1,0:T(8,128)(2,1)S(1)} %all_gather.73.other_all), custom_call_target="tpu_custom_call" | custom-call | tf_op jit(solution)/shard_map/pallas_call | solution.py:58
  146.0 2.0 %all_gather.75.refs_2_ = bf16[192,768]{1,0:T(8,128)(2,1)S(1)} all-gather(bf16[96,768]{1,0:T(8,128)(2,1)S(1)} %shard_map.294.refs_0_), channel_id=1, replica_groups=mesh['dp'=4,'tensor'=4,'ctx'=2] {'ctx'}, dimensions={0}, use_global_device_ids=true | all-gather | bytes 442368 | tf_op jit(solution)/shard_map/all_gather | solution.py:465
  149.0 2.0 %all_gather.76.refs_6_ = bf16[192,768]{1,0:T(8,128)(2,1)S(1)} all-gather(bf16[96,768]{1,0:T(8,128)(2,1)S(1)} %shard_map.295.refs_4_), channel_id=1, replica_groups=mesh['dp'=4,'tensor'=4,'ctx'=2] {'ctx'}, dimensions={0}, use_global_device_ids=true | all-gather | bytes 442368 | tf_op jit(solution)/shard_map/all_gather | solution.py:465
  151.0 1.1 collective-permute-start.38
  152.1 2.2 %all_gather.77.other_all = bf16[384,768]{1,0:T(8,128)(2,1)S(1)} all-gather(bf16[192,768]{1,0:T(8,128)(2,1)S(1)} %collective-permute-done.31.other_ref), channel_id=1, replica_groups=mesh['dp'=4,'tensor'=4,'ctx'=2] {'ctx'}, dimensions={0}, use_global_device_ids=true | all-gather | bytes 884736 | tf_op jit(solution)/shard_map/all_gather | solution.py:465
  154.3 2.1 %shard_map.296 = f32[768,768]{1,0:T(8,128)} custom-call(s32[7]{0:T(128)S(1)} %pad_add_fusion.meta_ref, bf16[192,768]{1,0:T(8,128)(2,1)S(1)} %shard_map.291.own_ref, bf16[192,768]{1,0:T(8,128)(2,1)S(1)} %collective-permute-done.31.other_ref, bf16[384,768]{1,0:T(8,128)(2,1)S(1)} %all_gather.74.own_all, bf16[384,768]{1,0:T(8,128)(2,1)S(1)} %all_gather.77.other_all), custom_call_target="tpu_custom_call" | custom-call | tf_op jit(solution)/shard_map/pallas_call | solution.py:58
  157.1 2.0 %all_gather.78.refs_3_ = bf16[192,768]{1,0:T(8,128)(2,1)S(1)} all-gather(bf16[96,768]{1,0:T(8,128)(2,1)S(1)} %collective-permute-done.37.refs_1_), channel_id=1, replica_groups=mesh['dp'=4,'tensor'=4,'ctx'=2] {'ctx'}, dimensions={0}, use_global_device_ids=true | all-gather | bytes 442368 | tf_op jit(solution)/shard_map/all_gather | solution.py:465
  159.1 2.0 %all_gather.79.refs_7_ = bf16[192,768]{1,0:T(8,128)(2,1)S(1)} all-gather(bf16[96,768]{1,0:T(8,128)(2,1)S(1)} %collective-permute-done.38.refs_5_), channel_id=1, replica_groups=mesh['dp'=4,'tensor'=4,'ctx'=2] {'ctx'}, dimensions={0}, use_global_device_ids=true | all-gather | bytes 442368 | tf_op jit(solution)/shard_map/all_gather | solution.py:465
  161.1 2.2 %shard_map.298 = (f32[576,768]{1,0:T(8,128)}, f32[192,768]{1,0:T(8,128)}) custom-call(s32[7]{0:T(128)S(1)} %pad_add_fusion.meta_ref, bf16[96,768]{1,0:T(8,128)(2,1)S(1)} %shard_map.294.refs_0_, bf16[96,768]{1,0:T(8,128)(2,1)S(1)} %collective-permute-done.37.refs_1_, bf16[192,768]{1,0:T(8,128)(2,1)S(1)} %all_gather.75.refs_2_, ...), custom_call_target="tpu_custom_call" | custom-call | tf_op jit(solution)/shard_map/pallas_call | solution.py:58
  (104 shorter events, 22.9 us)
Async XLA Ops:
  0.6 21.6 %copy-start.5 = (bf16[1,128,768]{2,1,0:T(8,128)(2,1)S(1)}, bf16[1,128,768]{2,1,0:T(8,128)(2,1)}, u32[]{:S(2)}) copy-start(bf16[1,128,768]{2,1,0:T(8,128)(2,1)} %param.31) | copy-start | bytes 589828
  0.7 9.9 %collective-permute-start.2 = (bf16[128,768]{1,0:T(8,128)(2,1)}, bf16[128,768]{1,0:T(8,128)(2,1)S(1)}, u32[]{:S(2)}, u32[]{:S(2)}) collective-permute-start(bf16[128,768]{1,0:T(8,128)(2,1)} %bitcast.26), channel_id=1, source_target_pairs={{0,6},{2,4},{4,2},{6,0},{1,7},{3,5},{5,3},{7,1},{8,14},{10,12},{12... | collective-permute-start | bytes 589832 | tf_op jit(solution)/shard_map/ppermute | solution.py:426
  4.6 9.4 %collective-permute-start.1 = (bf16[128,768]{1,0:T(8,128)(2,1)}, bf16[128,768]{1,0:T(8,128)(2,1)S(1)}, u32[]{:S(2)}, u32[]{:S(2)}) collective-permute-start(bf16[128,768]{1,0:T(8,128)(2,1)} %bitcast.27), channel_id=1, source_target_pairs={{0,4},{2,6},{4,0},{6,2},{1,5},{3,7},{5,1},{7,3},{8,12},{10,14},{12... | collective-permute-start | bytes 589832 | tf_op jit(solution)/shard_map/ppermute | solution.py:426
  5.1 10.3 %collective-permute-start = (bf16[128,768]{1,0:T(8,128)(2,1)}, bf16[128,768]{1,0:T(8,128)(2,1)S(1)}, u32[]{:S(2)}, u32[]{:S(2)}) collective-permute-start(bf16[128,768]{1,0:T(8,128)(2,1)} %bitcast.28), channel_id=1, source_target_pairs={{0,2},{2,0},{4,6},{6,4},{1,3},{3,1},{5,7},{7,5},{8,10},{10,8},{12,... | collective-permute-start | bytes 589832 | tf_op jit(solution)/shard_map/ppermute | solution.py:426
  6.2 31.6 %collective-permute-start.10 = (bf16[96,768]{1,0:T(8,128)(2,1)S(1)}, bf16[96,768]{1,0:T(8,128)(2,1)S(1)}, u32[]{:S(2)}, u32[]{:S(2)}) collective-permute-start(bf16[96,768]{1,0:T(8,128)(2,1)S(1)} %dynamic-slice_bitcast_fusion), channel_id=1, source_target_pairs={{0,4},{2,6},{4,0},{6,2},{1,5},{3,7},{5,1},{7,3},{8,12},{10,14},{12... | collective-permute-start | bytes 442376 | tf_op jit(solution)/shard_map/ppermute | solution.py:426
  8.2 24.6 %collective-permute-start.6 = (bf16[96,768]{1,0:T(8,128)(2,1)S(1)}, bf16[96,768]{1,0:T(8,128)(2,1)S(1)}, u32[]{:S(2)}, u32[]{:S(2)}) collective-permute-start(bf16[96,768]{1,0:T(8,128)(2,1)S(1)} %dynamic-slice_bitcast_fusion), channel_id=1, source_target_pairs={{0,2},{2,0},{4,6},{6,4},{1,3},{3,1},{5,7},{7,5},{8,10},{10,8},{12,... | collective-permute-start | bytes 442376 | tf_op jit(solution)/shard_map/ppermute | solution.py:426
  15.4 1.2 copy-start
  16.5 0.9 copy-start.6
  17.5 0.7 copy-start.9
  18.2 0.7 copy-start.11
  18.8 0.7 copy-start.16
  19.5 0.7 copy-start.17
  22.3 11.9 %collective-permute-start.9 = (bf16[128,768]{1,0:T(8,128)(2,1)S(1)}, bf16[128,768]{1,0:T(8,128)(2,1)S(1)}, u32[]{:S(2)}, u32[]{:S(2)}) collective-permute-start(bf16[128,768]{1,0:T(8,128)(2,1)S(1)} %bitcast.21), channel_id=1, source_target_pairs={{0,6},{2,4},{4,2},{6,0},{1,7},{3,5},{5,3},{7,1},{8,14},{10,12},{12... | collective-permute-start | bytes 589832 | tf_op jit(solution)/shard_map/ppermute | solution.py:426
  23.8 11.9 %collective-permute-start.8 = (bf16[128,768]{1,0:T(8,128)(2,1)S(1)}, bf16[128,768]{1,0:T(8,128)(2,1)S(1)}, u32[]{:S(2)}, u32[]{:S(2)}) collective-permute-start(bf16[128,768]{1,0:T(8,128)(2,1)S(1)} %bitcast.22), channel_id=1, source_target_pairs={{0,4},{2,6},{4,0},{6,2},{1,5},{3,7},{5,1},{7,3},{8,12},{10,14},{12... | collective-permute-start | bytes 589832 | tf_op jit(solution)/shard_map/ppermute | solution.py:426
  25.3 10.8 %collective-permute-start.7 = (bf16[128,768]{1,0:T(8,128)(2,1)S(1)}, bf16[128,768]{1,0:T(8,128)(2,1)S(1)}, u32[]{:S(2)}, u32[]{:S(2)}) collective-permute-start(bf16[128,768]{1,0:T(8,128)(2,1)S(1)} %bitcast.23), channel_id=1, source_target_pairs={{0,2},{2,0},{4,6},{6,4},{1,3},{3,1},{5,7},{7,5},{8,10},{10,8},{12,... | collective-permute-start | bytes 589832 | tf_op jit(solution)/shard_map/ppermute | solution.py:426
  28.2 20.6 %copy-start.2 = (bf16[768,768]{1,0:T(8,128)(2,1)S(1)}, bf16[768,768]{1,0:T(8,128)(2,1)}, u32[]{:S(2)}) copy-start(bf16[768,768]{1,0:T(8,128)(2,1)} %down_ref.3) | copy-start | bytes 3538948
  28.2 20.6 %copy-start.3 = (bf16[192,768]{1,0:T(8,128)(2,1)S(1)}, bf16[192,768]{1,0:T(8,128)(2,1)}, u32[]{:S(2)}) copy-start(bf16[192,768]{1,0:T(8,128)(2,1)} %w_ref.3) | copy-start | bytes 884740
  28.2 20.6 %copy-start.4 = (bf16[768,768]{1,0:T(8,128)(2,1)S(1)}, bf16[768,768]{1,0:T(8,128)(2,1)}, u32[]{:S(2)}) copy-start(bf16[768,768]{1,0:T(8,128)(2,1)} %up_ref.1) | copy-start | bytes 3538948
  28.2 20.6 %copy-start.8 = (f32[768]{0:T(1024)S(1)}, f32[768]{0:T(1024)}, u32[]{:S(2)}) copy-start(f32[768]{0:T(1024)} %gain_ref.6) | copy-start | bytes 9220
  28.2 20.6 %copy-start.12 = (f32[768]{0:T(1024)S(1)}, f32[768]{0:T(1024)}, u32[]{:S(2)}) copy-start(f32[768]{0:T(1024)} %ob_ref.1) | copy-start | bytes 9220
  28.2 20.6 %copy-start.13 = (f32[768]{0:T(1024)S(1)}, f32[768]{0:T(1024)}, u32[]{:S(2)}) copy-start(f32[768]{0:T(1024)} %shift_ref.3) | copy-start | bytes 9220
  28.2 20.6 %copy-start.14 = (f32[768]{0:T(1024)S(1)}, f32[768]{0:T(1024)}, u32[]{:S(2)}) copy-start(f32[768]{0:T(1024)} %ub_ref.1) | copy-start | bytes 9220
  32.7 6.6 %collective-permute-start.11 = (bf16[96,768]{1,0:T(8,128)(2,1)S(1)}, bf16[96,768]{1,0:T(8,128)(2,1)S(1)}, u32[]{:S(2)}, u32[]{:S(2)}) collective-permute-start(bf16[96,768]{1,0:T(8,128)(2,1)S(1)} %dynamic-slice_bitcast_fusion), channel_id=1, source_target_pairs={{0,6},{2,4},{4,2},{6,0},{1,7},{3,5},{5,3},{7,1},{8,14},{10,12},{12... | collective-permute-start | bytes 442376 | tf_op jit(solution)/shard_map/ppermute | solution.py:426
  34.2 9.7 %collective-permute-start.5 = (bf16[192,512]{1,0:T(8,128)(2,1)S(1)}, bf16[192,512]{1,0:T(8,128)(2,1)S(1)}, u32[]{:S(2)}, u32[]{:S(2)}) collective-permute-start(bf16[192,512]{1,0:T(8,128)(2,1)S(1)} %get-tuple-element.132.m0.mix_ref), channel_id=1, source_target_pairs={{0,6},{2,4},{4,2},{6,0},{1,7},{3,5},{5,3},{7,1},{8,14},{10,12},{12... | collective-permute-start | bytes 589832 | tf_op jit(solution)/shard_map/ppermute | solution.py:426
  35.7 13.1 %collective-permute-start.4 = (bf16[192,512]{1,0:T(8,128)(2,1)S(1)}, bf16[192,512]{1,0:T(8,128)(2,1)S(1)}, u32[]{:S(2)}, u32[]{:S(2)}) collective-permute-start(bf16[192,512]{1,0:T(8,128)(2,1)S(1)} %get-tuple-element.132.m0.mix_ref), channel_id=1, source_target_pairs={{0,4},{2,6},{4,0},{6,2},{1,5},{3,7},{5,1},{7,3},{8,12},{10,14},{12... | collective-permute-start | bytes 589832 | tf_op jit(solution)/shard_map/ppermute | solution.py:426
  36.1 12.7 %collective-permute-start.3 = (bf16[192,512]{1,0:T(8,128)(2,1)S(1)}, bf16[192,512]{1,0:T(8,128)(2,1)S(1)}, u32[]{:S(2)}, u32[]{:S(2)}) collective-permute-start(bf16[192,512]{1,0:T(8,128)(2,1)S(1)} %get-tuple-element.132.m0.mix_ref), channel_id=1, source_target_pairs={{0,2},{2,0},{4,6},{6,4},{1,3},{3,1},{5,7},{7,5},{8,10},{10,8},{12,... | collective-permute-start | bytes 589832 | tf_op jit(solution)/shard_map/ppermute | solution.py:426
  53.2 10.9 %collective-permute-start.12 = (bf16[128,768]{1,0:T(8,128)(2,1)S(1)}, bf16[128,768]{1,0:T(8,128)(2,1)S(1)}, u32[]{:S(2)}, u32[]{:S(2)}) collective-permute-start(bf16[128,768]{1,0:T(8,128)(2,1)S(1)} %get-tuple-element.153), channel_id=1, source_target_pairs={{0,2},{2,0},{4,6},{6,4},{1,3},{3,1},{5,7},{7,5},{8,10},{10,8},{12,... | collective-permute-start | bytes 589832 | tf_op jit(solution)/shard_map/ppermute | solution.py:426
  54.7 10.8 %collective-permute-start.13 = (bf16[128,768]{1,0:T(8,128)(2,1)S(1)}, bf16[128,768]{1,0:T(8,128)(2,1)S(1)}, u32[]{:S(2)}, u32[]{:S(2)}) collective-permute-start(bf16[128,768]{1,0:T(8,128)(2,1)S(1)} %get-tuple-element.154), channel_id=1, source_target_pairs={{0,4},{2,6},{4,0},{6,2},{1,5},{3,7},{5,1},{7,3},{8,12},{10,14},{12... | collective-permute-start | bytes 589832 | tf_op jit(solution)/shard_map/ppermute | solution.py:426
  55.2 10.3 %collective-permute-start.14 = (bf16[128,768]{1,0:T(8,128)(2,1)S(1)}, bf16[128,768]{1,0:T(8,128)(2,1)S(1)}, u32[]{:S(2)}, u32[]{:S(2)}) collective-permute-start(bf16[128,768]{1,0:T(8,128)(2,1)S(1)} %get-tuple-element.155), channel_id=1, source_target_pairs={{0,6},{2,4},{4,2},{6,0},{1,7},{3,5},{5,3},{7,1},{8,14},{10,12},{12... | collective-permute-start | bytes 589832 | tf_op jit(solution)/shard_map/ppermute | solution.py:426
  61.0 16.5 %collective-permute-start.15 = (bf16[192,768]{1,0:T(8,128)(2,1)S(1)}, bf16[192,768]{1,0:T(8,128)(2,1)S(1)}, u32[]{:S(2)}, u32[]{:S(2)}) collective-permute-start(bf16[192,768]{1,0:T(8,128)(2,1)S(1)} %shard_map.275), channel_id=1, source_target_pairs={{0,8},{8,0},{16,24},{24,16},{1,9},{9,1},{17,25},{25,17},{2,10},{10... | collective-permute-start | bytes 884744 | tf_op jit(solution)/shard_map/ppermute | solution.py:481
  71.0 19.1 %collective-permute-start.16 = (bf16[192,768]{1,0:T(8,128)(2,1)S(1)}, bf16[192,768]{1,0:T(8,128)(2,1)S(1)}, u32[]{:S(2)}, u32[]{:S(2)}) collective-permute-start(bf16[192,768]{1,0:T(8,128)(2,1)S(1)} %shard_map.278), channel_id=1, source_target_pairs={{0,8},{8,0},{16,24},{24,16},{1,9},{9,1},{17,25},{25,17},{2,10},{10... | collective-permute-start | bytes 884744 | tf_op jit(solution)/shard_map/ppermute | solution.py:481
  72.7 10.4 %collective-permute-start.19 = (bf16[128,768]{1,0:T(8,128)(2,1)S(1)}, bf16[128,768]{1,0:T(8,128)(2,1)S(1)}, u32[]{:S(2)}, u32[]{:S(2)}) collective-permute-start(bf16[128,768]{1,0:T(8,128)(2,1)S(1)} %get-tuple-element.167.b0), channel_id=1, source_target_pairs={{0,6},{2,4},{4,2},{6,0},{1,7},{3,5},{5,3},{7,1},{8,14},{10,12},{12... | collective-permute-start | bytes 589832 | tf_op jit(solution)/shard_map/ppermute | solution.py:426
  73.8 10.6 %collective-permute-start.18 = (bf16[128,768]{1,0:T(8,128)(2,1)S(1)}, bf16[128,768]{1,0:T(8,128)(2,1)S(1)}, u32[]{:S(2)}, u32[]{:S(2)}) collective-permute-start(bf16[128,768]{1,0:T(8,128)(2,1)S(1)} %get-tuple-element.167.b0), channel_id=1, source_target_pairs={{0,4},{2,6},{4,0},{6,2},{1,5},{3,7},{5,1},{7,3},{8,12},{10,14},{12... | collective-permute-start | bytes 589832 | tf_op jit(solution)/shard_map/ppermute | solution.py:426
  74.7 9.7 %collective-permute-start.17 = (bf16[128,768]{1,0:T(8,128)(2,1)S(1)}, bf16[128,768]{1,0:T(8,128)(2,1)S(1)}, u32[]{:S(2)}, u32[]{:S(2)}) collective-permute-start(bf16[128,768]{1,0:T(8,128)(2,1)S(1)} %get-tuple-element.167.b0), channel_id=1, source_target_pairs={{0,2},{2,0},{4,6},{6,4},{1,3},{3,1},{5,7},{7,5},{8,10},{10,8},{12,... | collective-permute-start | bytes 589832 | tf_op jit(solution)/shard_map/ppermute | solution.py:426
  78.2 29.1 %collective-permute-start.21 = (bf16[192,768]{1,0:T(8,128)(2,1)S(1)}, bf16[192,768]{1,0:T(8,128)(2,1)S(1)}, u32[]{:S(2)}, u32[]{:S(2)}) collective-permute-start(bf16[192,768]{1,0:T(8,128)(2,1)S(1)} %shard_map.280.a_ref), channel_id=1, source_target_pairs={{0,16},{8,24},{16,0},{24,8},{1,17},{9,25},{17,1},{25,9},{2,18},{10... | collective-permute-start | bytes 884744 | tf_op jit(solution)/shard_map/ppermute | solution.py:492
  90.2 4.8 %copy-start.1 = (bf16[768,3,192]{0,2,1:T(8,128)(2,1)S(1)}, bf16[768,3,192]{0,2,1:T(8,128)(2,1)}, u32[]{:S(2)}) copy-start(bf16[768,3,192]{0,2,1:T(8,128)(2,1)} %param.20) | copy-start | bytes 2654212
  98.9 14.4 %collective-permute-start.23 = (bf16[96,768]{1,0:T(8,128)(2,1)S(1)}, bf16[96,768]{1,0:T(8,128)(2,1)S(1)}, u32[]{:S(2)}, u32[]{:S(2)}) collective-permute-start(bf16[96,768]{1,0:T(8,128)(2,1)S(1)} %shard_map.284), channel_id=1, source_target_pairs={{0,8},{8,0},{16,24},{24,16},{1,9},{9,1},{17,25},{25,17},{2,10},{10... | collective-permute-start | bytes 442376 | tf_op jit(solution)/shard_map/ppermute | solution.py:481
  103.3 17.1 %copy-start.7 = (bf16[1,128,768]{2,1,0:T(8,128)(2,1)S(1)}, bf16[1,128,768]{2,1,0:T(8,128)(2,1)}, u32[]{:S(2)}) copy-start(bf16[1,128,768]{2,1,0:T(8,128)(2,1)} %param.16) | copy-start | bytes 589828
  103.3 17.1 %copy-start.10 = (f32[768]{0:T(1024)S(1)}, f32[768]{0:T(1024)}, u32[]{:S(2)}) copy-start(f32[768]{0:T(1024)} %gain_ref.7) | copy-start | bytes 9220
  103.9 19.6 %collective-permute-start.27 = (bf16[96,768]{1,0:T(8,128)(2,1)S(1)}, bf16[96,768]{1,0:T(8,128)(2,1)S(1)}, u32[]{:S(2)}, u32[]{:S(2)}) collective-permute-start(bf16[96,768]{1,0:T(8,128)(2,1)S(1)} %shard_map.286), channel_id=1, source_target_pairs={{0,8},{8,0},{16,24},{24,16},{1,9},{9,1},{17,25},{25,17},{2,10},{10... | collective-permute-start | bytes 442376 | tf_op jit(solution)/shard_map/ppermute | solution.py:481
  105.6 11.0 %collective-permute-start.24 = (bf16[144,768]{1,0:T(8,128)(2,1)S(1)}, bf16[144,768]{1,0:T(8,128)(2,1)S(1)}, u32[]{:S(2)}, u32[]{:S(2)}) collective-permute-start(bf16[144,768]{1,0:T(8,128)(2,1)S(1)} %get-tuple-element.194), channel_id=1, source_target_pairs={{0,2},{2,0},{4,6},{6,4},{1,3},{3,1},{5,7},{7,5},{8,10},{10,8},{12,... | collective-permute-start | bytes 663560 | tf_op jit(solution)/shard_map/ppermute | solution.py:426
  106.2 11.7 %collective-permute-start.25 = (bf16[144,768]{1,0:T(8,128)(2,1)S(1)}, bf16[144,768]{1,0:T(8,128)(2,1)S(1)}, u32[]{:S(2)}, u32[]{:S(2)}) collective-permute-start(bf16[144,768]{1,0:T(8,128)(2,1)S(1)} %get-tuple-element.195), channel_id=1, source_target_pairs={{0,4},{2,6},{4,0},{6,2},{1,5},{3,7},{5,1},{7,3},{8,12},{10,14},{12... | collective-permute-start | bytes 663560 | tf_op jit(solution)/shard_map/ppermute | solution.py:426
  107.3 13.1 %collective-permute-start.26 = (bf16[144,768]{1,0:T(8,128)(2,1)S(1)}, bf16[144,768]{1,0:T(8,128)(2,1)S(1)}, u32[]{:S(2)}, u32[]{:S(2)}) collective-permute-start(bf16[144,768]{1,0:T(8,128)(2,1)S(1)} %get-tuple-element.196), channel_id=1, source_target_pairs={{0,6},{2,4},{4,2},{6,0},{1,7},{3,5},{5,3},{7,1},{8,14},{10,12},{12... | collective-permute-start | bytes 663560 | tf_op jit(solution)/shard_map/ppermute | solution.py:426
  113.4 21.8 %collective-permute-start.20 = (bf16[192,768]{1,0:T(8,128)(2,1)S(1)}, bf16[192,768]{1,0:T(8,128)(2,1)S(1)}, u32[]{:S(2)}, u32[]{:S(2)}) collective-permute-start(bf16[192,768]{1,0:T(8,128)(2,1)S(1)} %shard_map.282.a_ref), channel_id=1, source_target_pairs={{0,16},{8,24},{16,0},{24,8},{1,17},{9,25},{17,1},{25,9},{2,18},{10... | collective-permute-start | bytes 884744 | tf_op jit(solution)/shard_map/ppermute | solution.py:492
  116.6 15.2 %collective-permute-start.22 = (bf16[192,768]{1,0:T(8,128)(2,1)S(1)}, bf16[192,768]{1,0:T(8,128)(2,1)S(1)}, u32[]{:S(2)}, u32[]{:S(2)}) collective-permute-start(bf16[192,768]{1,0:T(8,128)(2,1)S(1)} %shard_map.287.own_ref), channel_id=1, source_target_pairs={{0,8},{8,0},{16,24},{24,16},{1,9},{9,1},{17,25},{25,17},{2,10},{10... | collective-permute-start | bytes 884744 | tf_op jit(solution)/shard_map/ppermute | solution.py:499
  117.8 27.0 %collective-permute-start.33 = (bf16[96,768]{1,0:T(8,128)(2,1)S(1)}, bf16[96,768]{1,0:T(8,128)(2,1)S(1)}, u32[]{:S(2)}, u32[]{:S(2)}) collective-permute-start(bf16[96,768]{1,0:T(8,128)(2,1)S(1)} %shard_map.288.a_ref), channel_id=1, source_target_pairs={{0,16},{8,24},{16,0},{24,8},{1,17},{9,25},{17,1},{25,9},{2,18},{10... | collective-permute-start | bytes 442376 | tf_op jit(solution)/shard_map/ppermute | solution.py:492
  123.5 18.4 %copy-start.15 = (f32[768]{0:T(1024)S(1)}, f32[768]{0:T(1024)}, u32[]{:S(2)}) copy-start(f32[768]{0:T(1024)} %bias_ref.1) | copy-start | bytes 9220
  124.1 11.1 %collective-permute-start.28 = (bf16[128,768]{1,0:T(8,128)(2,1)S(1)}, bf16[128,768]{1,0:T(8,128)(2,1)S(1)}, u32[]{:S(2)}, u32[]{:S(2)}) collective-permute-start(bf16[128,768]{1,0:T(8,128)(2,1)S(1)} %get-tuple-element.214), channel_id=1, source_target_pairs={{0,2},{2,0},{4,6},{6,4},{1,3},{3,1},{5,7},{7,5},{8,10},{10,8},{12,... | collective-permute-start | bytes 589832 | tf_op jit(solution)/shard_map/ppermute | solution.py:426
  127.5 11.2 %collective-permute-start.29 = (bf16[128,768]{1,0:T(8,128)(2,1)S(1)}, bf16[128,768]{1,0:T(8,128)(2,1)S(1)}, u32[]{:S(2)}, u32[]{:S(2)}) collective-permute-start(bf16[128,768]{1,0:T(8,128)(2,1)S(1)} %get-tuple-element.216), channel_id=1, source_target_pairs={{0,4},{2,6},{4,0},{6,2},{1,5},{3,7},{5,1},{7,3},{8,12},{10,14},{12... | collective-permute-start | bytes 589832 | tf_op jit(solution)/shard_map/ppermute | solution.py:426
  131.7 10.2 %collective-permute-start.30 = (bf16[128,768]{1,0:T(8,128)(2,1)S(1)}, bf16[128,768]{1,0:T(8,128)(2,1)S(1)}, u32[]{:S(2)}, u32[]{:S(2)}) collective-permute-start(bf16[128,768]{1,0:T(8,128)(2,1)S(1)} %get-tuple-element.218), channel_id=1, source_target_pairs={{0,6},{2,4},{4,2},{6,0},{1,7},{3,5},{5,3},{7,1},{8,14},{10,12},{12... | collective-permute-start | bytes 589832 | tf_op jit(solution)/shard_map/ppermute | solution.py:426
  135.2 12.9 %collective-permute-start.32 = (bf16[96,768]{1,0:T(8,128)(2,1)S(1)}, bf16[96,768]{1,0:T(8,128)(2,1)S(1)}, u32[]{:S(2)}, u32[]{:S(2)}) collective-permute-start(bf16[96,768]{1,0:T(8,128)(2,1)S(1)} %shard_map.290.a_ref), channel_id=1, source_target_pairs={{0,16},{8,24},{16,0},{24,8},{1,17},{9,25},{17,1},{25,9},{2,18},{10... | collective-permute-start | bytes 442376 | tf_op jit(solution)/shard_map/ppermute | solution.py:492
  135.2 15.8 %collective-permute-start.31 = (bf16[192,768]{1,0:T(8,128)(2,1)S(1)}, bf16[192,768]{1,0:T(8,128)(2,1)S(1)}, u32[]{:S(2)}, u32[]{:S(2)}) collective-permute-start(bf16[192,768]{1,0:T(8,128)(2,1)S(1)} %shard_map.291.own_ref), channel_id=1, source_target_pairs={{0,8},{8,0},{16,24},{24,16},{1,9},{9,1},{17,25},{25,17},{2,10},{10... | collective-permute-start | bytes 884744 | tf_op jit(solution)/shard_map/ppermute | solution.py:499
  138.6 17.8 %collective-permute-start.36 = (f32[8,768]{1,0:T(8,128)S(1)}, f32[8,768]{1,0:T(8,128)S(1)}, u32[]{:S(2)}, u32[]{:S(2)}) collective-permute-start(f32[8,768]{1,0:T(8,128)S(1)} %slice_add_fusion.a), channel_id=1, source_target_pairs={{0,24},{8,16},{16,8},{24,0},{1,25},{9,17},{17,9},{25,1},{2,26},{10... | collective-permute-start | bytes 73736 | tf_op jit(solution)/shard_map/ppermute | solution.py:707
  141.9 14.5 %collective-permute-start.35 = (f32[8,768]{1,0:T(8,128)S(1)}, f32[8,768]{1,0:T(8,128)S(1)}, u32[]{:S(2)}, u32[]{:S(2)}) collective-permute-start(f32[8,768]{1,0:T(8,128)S(1)} %slice_add_fusion.a), channel_id=1, source_target_pairs={{0,16},{8,24},{16,0},{24,8},{1,17},{9,25},{17,1},{25,9},{2,18},{10... | collective-permute-start | bytes 73736 | tf_op jit(solution)/shard_map/ppermute | solution.py:707
  144.8 11.6 %collective-permute-start.34 = (f32[8,768]{1,0:T(8,128)S(1)}, f32[8,768]{1,0:T(8,128)S(1)}, u32[]{:S(2)}, u32[]{:S(2)}) collective-permute-start(f32[8,768]{1,0:T(8,128)S(1)} %slice_add_fusion.a), channel_id=1, source_target_pairs={{0,8},{8,0},{16,24},{24,16},{1,9},{9,1},{17,25},{25,17},{2,10},{10... | collective-permute-start | bytes 73736 | tf_op jit(solution)/shard_map/ppermute | solution.py:707
  148.0 9.0 %collective-permute-start.37 = (bf16[96,768]{1,0:T(8,128)(2,1)S(1)}, bf16[96,768]{1,0:T(8,128)(2,1)S(1)}, u32[]{:S(2)}, u32[]{:S(2)}) collective-permute-start(bf16[96,768]{1,0:T(8,128)(2,1)S(1)} %shard_map.294.refs_0_), channel_id=1, source_target_pairs={{0,8},{8,0},{16,24},{24,16},{1,9},{9,1},{17,25},{25,17},{2,10},{10... | collective-permute-start | bytes 442376 | tf_op jit(solution)/shard_map/ppermute | solution.py:499
  151.0 8.1 %collective-permute-start.38 = (bf16[96,768]{1,0:T(8,128)(2,1)S(1)}, bf16[96,768]{1,0:T(8,128)(2,1)S(1)}, u32[]{:S(2)}, u32[]{:S(2)}) collective-permute-start(bf16[96,768]{1,0:T(8,128)(2,1)S(1)} %shard_map.295.refs_4_), channel_id=1, source_target_pairs={{0,8},{8,0},{16,24},{24,16},{1,9},{9,1},{17,25},{25,17},{2,10},{10... | collective-permute-start | bytes 442376 | tf_op jit(solution)/shard_map/ppermute | solution.py:499

commit v3 on v2

--- a/solution.py
+++ b/solution.py
@@ -65,30 +65,51 @@
     )(*args)
 
 
-def vec(ref):
-    return ref[...].reshape(1, ref.shape[0])
+GAIN1, SHIFT1, QUERY_BIAS, VALUE_BIAS = range(4)
+OUT_BIAS, GAIN2, SHIFT2, UP_BIAS, DOWN_BIAS = range(5)
+
+
+def vec(ref, row, size=None):
+    return ref[row : row + 1, :size]
 
 
 def shape(dims, dtype):
     return jax.ShapeDtypeStruct(dims, dtype)
 
 
+def pack_kernel(*refs):
+    *vectors, vec_ref = refs
+    for i, v in enumerate(vectors):
+        vec_ref[i : i + 1, : v.shape[0]] = v[...].reshape(1, v.shape[0])
+
+
+def first_kernel(meta_ref, *refs):
+    vectors, (w_ref, x_ref, cot_ref, ow_ref) = refs[:4], refs[4:8]
+    vec_ref, w_out, x_out, message = refs[8:]
+    pack_kernel(*vectors, vec_ref)
+    w_out[...] = w_ref[...]
+    x_out[...] = x_ref[...]
+    own = cot_ref.shape[0]
+    message[:own] = cot_ref[...]
+    message[own:] = ow_ref[rows_at(meta_ref[1], message.shape[0] - own)]
+
+
 def qkv_kernel(
-    meta_ref, x0, x1, x2, x3, gain_ref, shift_ref, w_ref, qb_ref, vb_ref, rows_ref, normed_ref, q_ref, kv_ref
+    meta_ref, x0, x1, x2, x3, vec_ref, w_ref, rows_ref, normed_ref, q_ref, kv_ref
 ):
     local = q_ref.shape[1]
     own = x0.shape[0]
     rank = meta_ref[0]
-    gain, shift = vec(gain_ref), vec(shift_ref)
+    gain, shift = vec(vec_ref, GAIN1), vec(vec_ref, SHIFT1)
     for r, x in enumerate((x0, x1, x2, x3)):
         at = rows_at(rank ^ r, own)
         rows_ref[at] = x[...]
         xhat, _ = norm_parts(x[...].astype(F32))
         normed_ref[at] = (xhat * gain + shift).astype(BF16)
     normed = normed_ref[...]
-    q_ref[...] = (dot(normed, w_ref[:local], 1, 1) + vec(qb_ref)).astype(BF16)
+    q_ref[...] = (dot(normed, w_ref[:local], 1, 1) + vec(vec_ref, QUERY_BIAS, local)).astype(BF16)
     kv_ref[:, :local] = dot(normed, w_ref[local : 2 * local], 1, 1).astype(BF16)
-    kv_ref[:, local:] = (dot(normed, w_ref[2 * local :], 1, 1) + vec(vb_ref)).astype(BF16)
+    kv_ref[:, local:] = (dot(normed, w_ref[2 * local :], 1, 1) + vec(vec_ref, VALUE_BIAS, local)).astype(BF16)
 
 
 def blocks_of(ctx, half, size):
@@ -222,7 +243,7 @@
 
 
 def ff_kernel(
-    meta_ref, m0, m1, m2, m3, x_ref, w_ref, wa_ref, wb_ref, ob_ref, gain_ref, shift_ref, up_ref, ub_ref, down_ref, c0, c1, c2, c3,
+    meta_ref, m0, m1, m2, m3, x_ref, w_ref, wc_ref, vec_ref, up_ref, down_ref, c0, c1, c2, c3,
     normed_ref, active_ref, upg_ref, cot_ref, hidden_ref, s0, s1, s2, s3, ub_out, db_out, w_all, mix_all, part,
 ):
     own = c0.shape[0]
@@ -231,15 +252,15 @@
     rank, ctx = meta_ref[0], meta_ref[1]
     piece = local // 2
     w_all[:local] = w_ref[...]
-    for r in range(wa_ref.shape[0] // piece):
-        w_all[rows_at(2 * (r + 1) + ctx, piece)] = wa_ref[r * piece : (r + 1) * piece]
-        w_all[rows_at(2 * (r + 1) + 1 - ctx, piece)] = wb_ref[rows_at((1 - ctx) * 3 + r, piece)]
+    for r, c in enumerate((c1, c2, c3)):
+        w_all[rows_at(2 * (r + 1) + ctx, piece)] = c[own:]
+        w_all[rows_at(2 * (r + 1) + 1 - ctx, piece)] = wc_ref[rows_at(3 * (1 - ctx) + r, piece)]
     for r, m in enumerate((m0, m1, m2, m3)):
         mix_all[r * local : (r + 1) * local] = m[...]
     for r, c in enumerate((c0, c1, c2, c3)):
-        cot_ref[rows_at(rank ^ r, own)] = c[...]
+        cot_ref[rows_at(rank ^ r, own)] = c[:own]
     chunk = 256
-    ob, gain, shift, ub = vec(ob_ref), vec(gain_ref), vec(shift_ref), vec(ub_ref)
+    ob, gain, shift, ub = (vec(vec_ref, r) for r in (OUT_BIAS, GAIN2, SHIFT2, UP_BIAS))
     ub_total = jnp.zeros(ub_out.shape, F32)
     db_total = jnp.zeros(db_out.shape, F32)
     for i in range(half // chunk):
@@ -281,19 +302,37 @@
     far_own[...] = total[rows_at(2 - 2 * ctx + bit, size)]
 
 
+def quarters_out3(meta_ref, total, quarters):
+    own, near, far = quarters
+    size = own.shape[0]
+    quarters_out(meta_ref, total, (own, near, far.at[:size], far.at[size:]))
+
+
 def weight_grad_kernel(meta_ref, a_ref, b_ref, *refs):
     total = refs[4]
     total[...] = dot(a_ref[...], b_ref[...], 0, 0).astype(BF16)
     quarters_out(meta_ref, total, refs[:4])
 
 
-def out_part_kernel(meta_ref, active_ref, down_ref, s0, s1, s2, s3, part):
+def out_part_kernel(meta_ref, active_ref, down_ref, s0, s2, first, part):
     rank = meta_ref[0]
     own = s0.shape[0]
     part[...] = dot(active_ref[...], down_ref[...], 1, 0)
     s0[...] = part[rows_at(rank, own)]
-    for r, s in enumerate((s1, s2, s3), 1):
-        s[...] = part[rows_at(rank ^ r, own)].astype(BF16)
+    s2[...] = part[rows_at(rank ^ 2, own)]
+    first[:own] = part[rows_at(rank ^ 1, own)].astype(BF16)
+    first[own:] = part[rows_at(rank ^ 3, own)].astype(BF16)
+
+
+def out_second_kernel(s2, got, out_ref):
+    own = s2.shape[0]
+    out_ref[...] = (s2[...] + got[own:].astype(F32)).astype(BF16)
+
+
+def output_kernel(s0, g1, g2, hidden_ref, vec_ref, out_ref):
+    own = s0.shape[0]
+    total = s0[...] + g1[:own].astype(F32) + g2[...].astype(F32)
+    out_ref[...] = (hidden_ref[...] + total + vec(vec_ref, DOWN_BIAS)).astype(BF16)
 
 
 def sum4(refs):
@@ -303,10 +342,10 @@
     return total
 
 
-def norm2_back_kernel(s0, g1, g2, g3, hidden_ref, cot_ref, gain_ref, grad_ref, low_ref, small_ref):
+def norm2_back_kernel(s0, g1, g2, g3, hidden_ref, cot_ref, vec_ref, grad_ref, low_ref, small_ref):
     grad = sum4((s0, g1, g2, g3))
     xhat, scale = norm_parts(hidden_ref[...])
-    hidden_grad = cot_ref[...].astype(F32) + norm_back(grad, vec(gain_ref), xhat, scale)
+    hidden_grad = cot_ref[...].astype(F32) + norm_back(grad, vec(vec_ref, GAIN2), xhat, scale)
     grad_ref[...] = hidden_grad
     low_ref[...] = hidden_grad.astype(BF16)
     small_ref[0:1] = jnp.sum(grad * xhat, axis=0, keepdims=True)
@@ -314,21 +353,20 @@
 
 
 def q_back_kernel(
-    meta_ref, dq_ref, normed_ref, mix_ref, rows_ref, w_ref, t0, t1, t2, t3, part_ref, qb_ref, ob_ref, total
+    meta_ref, dq_ref, normed_ref, mix_ref, rows_ref, t0, t1, t2, qb_ref, ob_ref, total
 ):
     local = dq_ref.shape[0]
     dq = dq_ref[...]
     total[:local] = dot(dq, normed_ref[...], 1, 0).astype(BF16)
     total[local:] = dot(mix_ref[...], rows_ref[...], 1, 0).astype(BF16)
-    quarters_out(meta_ref, total, (t0, t1, t2, t3))
-    part_ref[...] = dot(dq, w_ref[:local], 0, 0)
+    quarters_out3(meta_ref, total, (t0, t1, t2))
     qb_ref[...] = dot(jnp.ones((8, dq.shape[1]), BF16), dq, 1, 1)[0:1]
     ob_ref[...] = jnp.sum(rows_ref[...].astype(F32), axis=0, keepdims=True)
 
 
 def kv_back_kernel(
-    meta_ref, keep_kv, got_kv, normed_ref, w_ref, x_ref, norm2_ref, qpart_ref,
-    t0, t1, t2, t3, s0, s1, s2, s3, norm_ref, vb_ref, total, part,
+    meta_ref, dq_ref, keep_kv, got_kv, normed_ref, w_ref, x_ref, norm2_ref,
+    t0, t1, t2, s0, s2, first, norm_ref, vb_ref, total, part,
 ):
     rank, ctx = meta_ref[0], meta_ref[1]
     own, width = s0.shape
@@ -336,8 +374,8 @@
     normed = normed_ref[...]
     dkv = (keep_kv[...] + got_kv[rows_at(1 - ctx, half)].astype(F32)).astype(BF16)
     total[...] = dot(dkv, normed, 0, 0).astype(BF16)
-    quarters_out(meta_ref, total, (t0, t1, t2, t3))
-    part[...] = qpart_ref[...] + dot(dkv, w_ref[local:], 1, 0)
+    quarters_out3(meta_ref, total, (t0, t1, t2))
+    part[...] = dot(dq_ref[...], w_ref[:local], 0, 0) + dot(dkv, w_ref[local:], 1, 0)
     gain_total = jnp.zeros((1, width), F32)
     shift_total = jnp.zeros((1, width), F32)
     chunk = 128
@@ -350,28 +388,31 @@
         [gain_total, shift_total, norm2_ref[...], jnp.zeros((4, width), F32)], 0
     )
     norm_ref[...] = norms
-    high = norms.astype(BF16)
-    tail = jnp.concatenate([high.astype(F32), norms - high.astype(F32)], 0).astype(BF16)
     s0[...] = part[rows_at(rank, own)]
-    for r, s in enumerate((s1, s2, s3), 1):
-        s[:own] = part[rows_at(rank ^ r, own)].astype(BF16)
-        s[own:] = tail
+    s2[...] = part[rows_at(rank ^ 2, own)]
+    first[:own] = part[rows_at(rank ^ 1, own)].astype(BF16)
+    first[own : 2 * own] = part[rows_at(rank ^ 3, own)].astype(BF16)
+    first[2 * own :] = high_low(norms)
     vb_ref[...] = jnp.sum(dkv.astype(F32), axis=0, keepdims=True)[:, local:]
 
 
-def norm1_back_kernel(
-    s0, g1, g2, g3, x_ref, gain_ref, hidden_ref, norm_ref, ob_ref, db_ref, ub_ref, qb_ref, vb_ref, out_ref, small_ref
+def rows_second_kernel(s2, got, norm_ref, out_ref, norm_out):
+    own = s2.shape[0]
+    out_ref[:own] = (s2[...] + got[own : 2 * own].astype(F32)).astype(BF16)
+    norms = norm_ref[...] + from_high_low(got[2 * own :])
+    norm_out[...] = norms
+    out_ref[own:] = high_low(norms)
+
+
+def last_rows_kernel(
+    s0, g1, g2, x_ref, vec1_ref, grad_ref, norm_ref, ob_ref, db_ref, ub_ref, qb_ref, vb_ref, in_out, small_ref
 ):
     own = s0.shape[0]
-    grad = s0[...]
-    norms = norm_ref[...]
-    for g in (g1, g2, g3):
-        grad = grad + g[:own].astype(F32)
-        tail = g[own:].astype(F32)
-        norms = norms + (tail[:8] + tail[8:])
+    grad = s0[...] + g1[:own].astype(F32) + g2[:own].astype(F32)
+    norms = norm_ref[...] + from_high_low(g2[own:])
     xhat, scale = norm_parts(x_ref[...].astype(F32))
-    out = hidden_ref[...] + norm_back(grad, vec(gain_ref), xhat, scale)
-    out_ref[...] = out.astype(BF16)
+    grad = grad_ref[...] + norm_back(grad, vec(vec1_ref, GAIN1), xhat, scale)
+    in_out[...] = grad.astype(BF16)
     local = qb_ref.shape[1]
     small_ref[0:4] = norms[:4]
     small_ref[4:5] = ob_ref[...]
@@ -383,42 +424,42 @@
     small_ref[7:8, lanes : lanes + local] = vb_ref[...]
 
 
-def output_kernel(s0, g1, g2, g3, hidden_ref, bias_ref, out_ref):
-    out_ref[...] = (hidden_ref[...] + sum4((s0, g1, g2, g3)) + vec(bias_ref)).astype(BF16)
-
-
-def place(meta_ref, own_ref, other_ref, own_all, other_all, out_ref):
+def peer_rows(ctx, pair_ref):
+    return pair_ref[rows_at(1 - ctx, pair_ref.shape[0] // 2)]
+
+
+def place(meta_ref, own_ref, other_ref, own_pair, other_peer, out_ref):
     ctx, bit = meta_ref[1], meta_ref[6]
-    size = own_ref.shape[0]
-    out_ref[rows_at(2 * ctx + bit, size)] = own_ref[...].astype(F32)
-    out_ref[rows_at(2 * ctx + 1 - bit, size)] = other_ref[...].astype(F32)
-    peer = rows_at(1 - ctx, size)
-    out_ref[rows_at(2 - 2 * ctx + bit, size)] = own_all[peer].astype(F32)
-    out_ref[rows_at(3 - 2 * ctx - bit, size)] = other_all[peer].astype(F32)
-
-
-def whole_kernel(meta_ref, own_ref, other_ref, own_all, other_all, out_ref):
-    place(meta_ref, own_ref, other_ref, own_all, other_all, out_ref)
+    size = out_ref.shape[0] // 4
+    out_ref[rows_at(2 * ctx + bit, size)] = own_ref[:size].astype(F32)
+    out_ref[rows_at(2 * ctx + 1 - bit, size)] = other_ref[:size].astype(F32)
+    out_ref[rows_at(2 - 2 * ctx + bit, size)] = peer_rows(ctx, own_pair)[:size].astype(F32)
+    out_ref[rows_at(3 - 2 * ctx - bit, size)] = other_peer[:size].astype(F32)
+
+
+def whole_kernel(meta_ref, *refs):
+    place(meta_ref, *refs)
 
 
 def attn_whole_kernel(meta_ref, *refs):
-    qkv_out, out_out, total = refs[8:]
+    qkv_out, out_out = refs[8:10]
+    total = refs[19]
     local = out_out.shape[0]
     place(meta_ref, *refs[:4], total)
     qkv_out[:local] = total[:local]
     out_out[...] = total[local:]
     place(meta_ref, *refs[4:8], total)
     qkv_out[local:] = total[...]
-
-
-def small_kernel(a, b, c, d, *outs):
-    total = a[...] + b[...] + c[...] + d[...]
+    rows = total.shape[0] // 4
+    tails = [r[rows:] for r in (refs[0], refs[1], refs[3])]
+    tails.append(peer_rows(meta_ref[1], refs[2])[rows:])
+    small = sum(from_high_low(t) for t in tails)
+    outs = refs[10:19]
     for i, out in enumerate(outs[:7]):
-        out[...] = total[i]
-    local = outs[7].shape[0]
-    lanes = total.shape[1] // 2
-    outs[7][...] = total[7, :local]
-    outs[8][...] = total[7, lanes : lanes + local]
+        out[...] = small[i]
+    lanes = small.shape[1] // 2
+    outs[7][...] = small[7, :local]
+    outs[8][...] = small[7, lanes : lanes + local]
 
 
 def to_peers(blocks):
@@ -429,6 +470,7 @@
 
 
 NEAR, FAR = xor_pairs(4, 1), xor_pairs(4, 2)
+CTX = xor_pairs(2, 1)
 
 
 def peer_add_kernel(meta_ref, a_ref, pair_ref, out_ref):
@@ -437,14 +479,37 @@
     out_ref[...] = (a_ref[...].astype(F32) + got).astype(BF16)
 
 
-def peer_add2_kernel(meta_ref, a_ref, pair_ref, b_ref, out_ref):
+def peer_add2_kernel(meta_ref, a_ref, b_ref, pair_ref, a_out, b_out):
     size = a_ref.shape[0]
-    got = pair_ref[rows_at(1 - meta_ref[1], size)].astype(F32)
-    out_ref[...] = (a_ref[...].astype(F32) + got + b_ref[...].astype(F32)).astype(BF16)
-
-
-def add_kernel(a_ref, b_ref, out_ref):
-    out_ref[...] = (a_ref[...].astype(F32) + b_ref[...].astype(F32)).astype(BF16)
+    peer = 2 - 2 * meta_ref[1]
+    a_out[...] = add(a_ref[...], pair_ref[rows_at(peer, size)]).astype(BF16)
+    b_out[...] = add(b_ref[...], pair_ref[rows_at(peer + 1, size)]).astype(BF16)
+
+
+def add(*parts):
+    return sum((p.astype(F32) for p in parts[1:]), parts[0].astype(F32))
+
+
+def high_low(x):
+    high = x.astype(BF16).astype(F32)
+    return jnp.concatenate([high, x - high], 0).astype(BF16)
+
+
+def from_high_low(pair):
+    pair = pair.astype(F32)
+    return pair[:8] + pair[8:]
+
+
+def sum_kernel(append, tailed, *refs):
+    *ins, out_ref = refs
+    if append:
+        *ins, small_ref = ins
+    rows = ins[0].shape[0] - (16 if tailed else 0)
+    out_ref[:rows] = add(*(i[:rows] for i in ins)).astype(BF16)
+    if append:
+        out_ref[rows:] = high_low(small_ref[...])
+    if tailed:
+        out_ref[rows:] = high_low(sum(from_high_low(i[rows:]) for i in ins))
 
 
 class Order:
@@ -461,6 +526,10 @@
         self.last = out[0]
         return out
 
+    def step(self, x):
+        self.last = self.first(x)
+        return self.last
+
     def pair(self, x):
         self.last = lax.all_gather(self.first(x), "ctx", axis=0, tiled=True)
         return self.last
@@ -469,9 +538,20 @@
 class WeightSum:
     def __init__(self, order, meta, quarters):
         self.order, self.meta = order, meta
-        self.own, self.near, self.far_near, self.far_own = quarters
+        if len(quarters) == 3:
+            self.own, self.near, self.far = quarters
+        else:
+            self.own, self.near, self.far_near, self.far_own = quarters
         self.shape = [shape(self.own.shape, BF16)]
         self.short = lax.axis_size("dp") == 4
+
+    def both(self):
+        got = self.order.pair(self.far)
+        send, self.own = self.order.call(
+            peer_add2_kernel, self.shape * 2, [self.meta, self.near, self.own, got], smem=1
+        )
+        self.got = lax.ppermute(send, "dp", NEAR) if self.short else lax.psum(send, "dp")
+        self.pair = None
 
     def one(self):
         got = self.order.pair(self.far_near)
@@ -480,34 +560,51 @@
         )
         self.got = lax.ppermute(send, "dp", NEAR) if self.short else lax.psum(send, "dp")
 
-    def two(self):
-        self.pairs = self.order.pair(self.far_own)
-
-    def three(self):
+        self.pair = lax.ppermute(self.far_own, "ctx", CTX)
+
+    def three(self, small=None):
         other = self.got if self.short else jnp.zeros_like(self.got)
-        (self.own,) = self.order.call(
-            peer_add2_kernel, self.shape, [self.meta, self.own, self.pairs, other], smem=1
-        )
+        args = [self.own, other] + ([] if self.pair is None else [self.pair])
+        out = self.shape
+        if small is not None:
+            rows, cols = self.own.shape
+            if not self.short:
+                small = lax.psum(small, "dp")
+                args = [lax.psum(add(*args).astype(BF16), "dp")]
+                self.got = jnp.pad(self.got, ((0, 16), (0, 0)))
+            args, out = args + [small], [shape((rows + 16, cols), BF16)]
+        kernel = functools.partial(sum_kernel, small is not None, False)
+        (self.own,) = self.order.call(kernel, out, args, at=0)
         if self.short:
             self.got = lax.ppermute(self.own, "dp", FAR)
-        else:
+        elif small is None:
             self.own = lax.psum(self.own, "dp")
 
+    def four_add(self):
+        if self.short:
+            kernel = functools.partial(sum_kernel, False, self.own.shape != self.shape[0].shape)
+            out = [shape(self.own.shape, BF16)]
+            (self.own,) = self.order.call(kernel, out, [self.own, self.got], at=0)
+
+    def four_send(self):
+        if self.short:
+            self.got = lax.ppermute(self.own, "dp", NEAR)
+
     def four(self):
-        if self.short:
-            (self.own,) = self.order.call(add_kernel, self.shape, [self.own, self.got])
-            self.got = lax.ppermute(self.own, "dp", NEAR)
+        self.four_add()
+        self.four_send()
 
     def five(self):
-        self.own_all = self.order.pair(self.own)
+        self.own_pair = self.order.pair(self.own)
 
     def six(self):
-        self.got_all = self.order.pair(self.got)
+        self.got_peer = lax.ppermute(self.got, "ctx", CTX)
 
     def parts(self):
-        return [self.own, self.got, self.own_all, self.got_all]
+        return [self.own, self.got, self.own_pair, self.got_peer]
 
     def whole(self):
+        self.six()
         rows, cols = self.own.shape
         return self.order.call(
             whole_kernel, [shape((4 * rows, cols), F32)], [self.meta, *self.parts()], smem=1
@@ -554,18 +651,31 @@
     def quarters(rows_all, cols):
         return [shape((rows_all // 4, cols), BF16)] * 4
 
+    def quarters3(rows_all, cols):
+        return quarters(rows_all, cols)[:2] + [shape((rows_all // 2, cols), BF16)]
+
     order = Order()
     xs = to_peers([tokens] * 3)
-    out_half = pick(out_weight.reshape(2, local // 2, width), ctx)
-    out_halves = to_peers([out_half] * 3)
+    vectors1, weight_t, own_x, message = call(
+        first_kernel,
+        [
+            shape((8, width), F32),
+            shape(weight_t.shape, BF16),
+            block_low,
+            shape((own + local // 2, width), BF16),
+        ],
+        [meta, norm1_gain, norm1_shift, query_bias, value_bias]
+        + [weight_t, tokens, cotangent, out_weight],
+        smem=1,
+    )
     rows, normed1, q, kv = order.call(
         qkv_kernel,
         [shape((half, width), BF16)] * 2
         + [shape((half, local), BF16), shape((half, 2 * local), BF16)],
-        [meta, tokens, *xs, norm1_gain, norm1_shift, weight_t, query_bias, value_bias],
+        [meta, own_x, *xs, vectors1, weight_t],
         smem=1,
     )
-    cots = to_peers([after(cotangent, kv)] * 3)
+    cots = to_peers([after(message, *xs)] * 3)
     kv_all = order.pair(kv)
     mix, lse = order.call(
         functools.partial(attend_kernel, size),
@@ -575,8 +685,13 @@
         scratch=[pltpu.VMEM((full, local), BF16), pltpu.VMEM((local, full), BF16)],
     )
     mixes = to_peers([mix] * 3)
-    out_half = jnp.concatenate([after(out_halves[0], mix, *cots), *out_halves[1:]], 0)
-    out_both = order.pair(out_half)
+    pieces = jnp.concatenate([after(cots[0], mix)[own:], cots[1][own:], cots[2][own:]], 0)
+    pieces_ctx = order.pair(pieces)
+    (vectors,) = order.call(
+        pack_kernel,
+        [shape((8, width), F32)],
+        [out_bias, norm2_gain, norm2_shift, up_bias, down_bias],
+    )
     (normed2, active, up_grad, cot_rows, hidden, *normed2_parts, up_bias_part, down_bias_part) = order.call(
         ff_kernel,
         [
@@ -592,8 +707,8 @@
             shape((1, hidden_units), F32),
             row_out,
         ],
-        [meta, mix, *mixes, rows, out_weight, out_half, out_both, out_bias, norm2_gain, norm2_shift]
-        + [up_weight, up_bias, down_weight, cotangent, *cots],
+        [meta, mix, *mixes, rows, out_weight, pieces_ctx, vectors]
+        + [up_weight, down_weight, cotangent, *cots],
         smem=1,
         vmem=28,
         scratch=[
@@ -621,22 +736,20 @@
     hidden_grad, branch_grad, norm2_part = order.call(
         norm2_back_kernel,
         [block, block_low, shape((2, width), F32)],
-        [normed2_parts[0], *normed2_got, hidden, cotangent, norm2_gain],
+        [normed2_parts[0], *normed2_got, hidden, cotangent, vectors],
         at=0,
     )
     branches = to_peers([branch_grad] * 3)
-    down_sum.two()
     up_sum.one()
-    out_parts = order.call(
+    down_sum.three()
+    o0, o2, o_first = order.call(
         out_part_kernel,
-        [block, block_low, block_low, block_low],
+        [block, block, shape((2 * own, width), BF16)],
         [meta, active, down_weight],
         at=1,
         smem=1,
         scratch=[pltpu.VMEM((half, width), F32)],
     )
-    down_sum.three()
-    up_sum.two()
     dq, kv_keep, kv_send, branch_rows = order.call(
         functools.partial(back_kernel, size),
         [
@@ -660,75 +773,79 @@
             pltpu.VMEM((full, local // HEAD_DIM * size), BF16),
         ],
     )
+    kv_got = order.pair(kv_send)
     up_sum.three()
-    kv_got = order.pair(kv_send)
-    *qo_quarters, q_part, q_bias_part, out_bias_part = order.call(
+    down_sum.four_add()
+    x_pairs, y_pairs = xor_pairs(ranks, 1), xor_pairs(ranks, 2)
+    *kv_quarters, n0, n2, n_first, norm_part, v_bias_part = order.call(
+        kv_back_kernel,
+        quarters3(2 * local, width)
+        + [block, block, shape((2 * own + 16, width), BF16)]
+        + [shape((8, width), F32), shape((1, local), F32)],
+        [meta, dq, kv_keep, kv_got, normed1, weight_t, rows, norm2_part],
+        at=1,
+        smem=1,
+        scratch=[pltpu.VMEM((2 * local, width), BF16), pltpu.VMEM((half, width), F32)],
+    )
+    n_first_got = lax.ppermute(n_first, "tensor", x_pairs)
+    kv_sum = WeightSum(order, meta, kv_quarters)
+    kv_sum.both()
+    *qo_quarters, q_bias_part, out_bias_part = order.call(
         q_back_kernel,
-        quarters(2 * local, width) + [shape((half, width), F32), shape((1, local), F32), row_out],
-        [meta, dq, normed1, mix, branch_rows, weight_t],
+        quarters3(2 * local, width) + [shape((1, local), F32), row_out],
+        [meta, dq, normed1, mix, branch_rows],
         at=1,
         smem=1,
         scratch=[pltpu.VMEM((2 * local, width), BF16)],
     )
     qo_sum = WeightSum(order, meta, qo_quarters)
-    qo_sum.one()
-    tail_low = shape((own + 16, width), BF16)
-    *kv_quarters, n0, n1, n2, n3, norm_part, v_bias_part = order.call(
-        kv_back_kernel,
-        quarters(2 * local, width)
-        + [block, tail_low, tail_low, tail_low, shape((8, width), F32), shape((1, local), F32)],
-        [meta, kv_keep, kv_got, normed1, weight_t, rows, norm2_part, q_part],
-        smem=1,
-        scratch=[pltpu.VMEM((2 * local, width), BF16), pltpu.VMEM((half, width), F32)],
-    )
-    normed1_got = to_peers([n1, n2, n3])
-    kv_sum = WeightSum(order, meta, kv_quarters)
-    kv_sum.one()
-    down_sum.four()
-    qo_sum.two()
+    qo_sum.both()
+    n_second, norm_part = order.call(
+        rows_second_kernel,
+        [shape((own + 16, width), BF16), shape((8, width), F32)],
+        [n2, n_first_got, norm_part],
+        at=0,
+    )
+    n_second_got = lax.ppermute(n_second, "tensor", y_pairs)
+    kv_sum.three()
+    up_sum.four_add()
+    input_grad, small = order.call(
+        last_rows_kernel,
+        [block_low, shape((8, width), F32)],
+        [n0, n_first_got, n_second_got, own_x, vectors1, hidden_grad, norm_part]
+        + [out_bias_part, down_bias_part, up_bias_part, q_bias_part, v_bias_part],
+        at=0,
+    )
+    qo_sum.three(small)
+    down_sum.own = after(down_sum.own, qo_sum.own)
+    down_sum.four_send()
+    up_sum.own = after(up_sum.own, qo_sum.own)
+    up_sum.four_send()
+    o_first_got = lax.ppermute(after(o_first, small), "tensor", x_pairs)
     down_sum.five()
-    qo_sum.three()
-    input_grad, small = order.call(
-        norm1_back_kernel,
-        [block_low, shape((8, width), F32)],
-        [n0, *normed1_got, tokens, norm1_gain, hidden_grad, norm_part, out_bias_part]
-        + [down_bias_part, up_bias_part, q_bias_part, v_bias_part],
-        at=0,
-    )
-    out_got = to_peers([after(b, input_grad) for b in out_parts[1:]])
-    kv_sum.two()
-    kv_sum.three()
-    small = order.pair(small)
-    small = small[:8] + small[8:]
-    down_sum.six()
-    up_sum.four()
     up_sum.five()
-    if lax.axis_size("dp") == 4:
-        smalls = [small] + [lax.ppermute(small, "dp", xor_pairs(4, r)) for r in (1, 2, 3)]
-    else:
-        small = lax.psum(small, "dp")
-        smalls = [small] + [jnp.zeros_like(small)] * 3
+    (o_second,) = order.call(out_second_kernel, [block_low], [o2, o_first_got], at=0)
+    o_second_got = lax.ppermute(o_second, "tensor", y_pairs)
+    down_sum.got = order.step(down_sum.got)
+    up_sum.got = order.step(up_sum.got)
+    kv_sum.four()
+    qo_sum.four()
+    kv_sum.five()
+    qo_sum.five()
+    kv_sum.got = order.step(kv_sum.got)
+    qo_sum.got = order.step(qo_sum.got)
+    down_grad = down_sum.whole()
+    up_weight_grad = up_sum.whole()
     (output,) = order.call(
-        output_kernel, [block_low], [out_parts[0], *out_got, hidden, down_bias], at=0
-    )
-    down_grad = down_sum.whole()
-    qo_sum.four()
-    qo_sum.five()
-    kv_sum.four()
-    kv_sum.five()
-    up_sum.six()
-    up_weight_grad = up_sum.whole()
-    outs = order.call(
-        small_kernel,
-        [shape((width,), F32)] * 7 + [shape((local,), F32)] * 2,
-        smalls,
-        at=0,
-    )
+        output_kernel, [block_low], [o0, o_first_got, o_second_got, hidden, vectors], at=0
+    )
+    kv_sum.six()
     qo_sum.six()
-    kv_sum.six()
-    attn_grad, out_weight_grad = order.call(
+    attn_grad, out_weight_grad, *outs = order.call(
         attn_whole_kernel,
-        [shape((3 * local, width), F32), shape((local, width), F32)],
+        [shape((3 * local, width), F32), shape((local, width), F32)]
+        + [shape((width,), F32)] * 7
+        + [shape((local,), F32)] * 2,
         [meta, *qo_sum.parts(), *kv_sum.parts()],
         smem=1,
         scratch=[pltpu.VMEM((2 * local, width), F32)],

time: 164 us -> 146 us (0.89)
  blocking collectives: 46.7 us -> 26.1 us
  waiting for transfers between devices: 19.4 us -> 34.1 us
  starting transfers between devices: 51.2 us -> 40.4 us
  Pallas kernels: 38.4 us -> 36.3 us
    all_gather x20 -> x11, blocking collectives: 46.7 us -> 26.1 us  [pair(): self.last = lax.all_gather(self.first(x), 'ctx', axis=0, tiled=True)]
    ppermute x7 -> x16, waiting for transfers between devices: 3.69 us -> 21 us  [the longest x4 13.5 us: four_send(): self.got = lax.ppermute(self.own, 'dp', NEAR)]
    ppermute x24 -> x15, starting transfers between devices: 30.5 us -> 18.8 us  [to_peers(): lax.ppermute(b, 'tensor', xor_pairs(lax.axis_size('tensor'), r))]
    ppermute x7 -> x16, starting transfers between devices: 7.44 us -> 12.7 us  [the longest x4 4.11 us: four_send(): self.got = lax.ppermute(self.own, 'dp', NEAR)]
    ppermute x24 -> x15, waiting for transfers between devices: 15.6 us -> 10.8 us  [to_peers(): lax.ppermute(b, 'tensor', xor_pairs(lax.axis_size('tensor'), r))]
    ppermute x4, waiting for transfers between devices: 0.01 us -> 2.31 us  [three(): self.got = lax.ppermute(self.own, 'dp', FAR)]
    ppermute x4 -> x2, starting transfers between devices: 5.45 us -> 3.24 us  [one(): lax.ppermute(send, 'dp', NEAR)]
    pallas_call x28 -> x31, Pallas kernels: 38.4 us -> 36.3 us  [call(): pl.pallas_call(kernel, out_shape=out_shape, in_specs=[pl.BlockSpec(memory...]
  transfers between devices with their start and end apart: 39 -> 37, of which waited for: 10 -> 13; matrix products, arithmetic and copies ran while one was open for 1% -> 1% of each run, Pallas kernels for 20% -> 19%
where the time goes in v3:
time: 146 us
  starting transfers between devices  40.4 us (28%)
  Pallas kernels  36.3 us (25%)
  waiting for transfers between devices  34.1 us (23%)
  blocking collectives  26.1 us (18%)
  local copies, waits for them, and re-layouts  6.8 us (5%)
    pallas_call x31, Pallas kernels, call(): pl.pallas_call(kernel, out_shape=out_shape, in_specs=[pl.BlockSpec(memory...  36.3 us
    all_gather x11, blocking collectives, pair(): self.last = lax.all_gather(self.first(x), 'ctx', axis=0, tiled=True)  26.1 us
    ppermute x15, starting transfers between devices, to_peers(): lax.ppermute(b, 'tensor', xor_pairs(lax.axis_size('tensor'), r))  18.8 us
    ppermute x4, waiting for transfers between devices, four_send(): self.got = lax.ppermute(self.own, 'dp', NEAR)  13.5 us
    ppermute x15, waiting for transfers between devices, to_peers(): lax.ppermute(b, 'tensor', xor_pairs(lax.axis_size('tensor'), r))  10.8 us
    unnamed x34, local copies, waits for them, and re-layouts  6.77 us
    ppermute x4, starting transfers between devices, three(): self.got = lax.ppermute(self.own, 'dp', FAR)  5.72 us
    ppermute x2, waiting for transfers between devices, both(): lax.ppermute(send, 'dp', NEAR)  5.45 us
  transfers between devices with their start and end apart: 37, of which 13 were waited for; matrix products, arithmetic and copies ran while one was open for 1% of the time, Pallas kernels for 19%

profile of v3, /device:TPU:0, one launch (start us, length us, event | category | flops | bytes accessed | tf_op | source)
XLA Modules:
  0.0 145.6 jit_solution(11705168985784452556)
XLA Ops:
  0.6 4.0 %collective-permute-start.2 = (bf16[128,768]{1,0:T(8,128)(2,1)}, bf16[128,768]{1,0:T(8,128)(2,1)S(1)}, u32[]{:S(2)}, u32[]{:S(2)}) collective-permute-start(bf16[128,768]{1,0:T(8,128)(2,1)} %bitcast.18), channel_id=1, source_target_pairs={{0,6},{2,4},{4,2},{6,0},{1,7},{3,5},{5,3},{7,1},{8,14},{10,12},{12... | collective-permute-start | bytes 589832 | tf_op jit(solution)/shard_map/ppermute | solution.py:467
  5.2 0.7 pad_add_fusion.meta_ref
  6.0 1.0 copy-done.1
  6.9 0.9 copy-done.3
  7.9 1.2 copy-done.6
  9.0 0.9 copy-done.7
  10.0 0.7 copy-done.8
  10.7 0.7 copy-done.9
  11.3 0.7 copy-done.15
  12.0 0.7 copy-done.16
  12.7 0.6 shard_map.271
  14.2 1.5 %collective-permute-start.6 = (bf16[224,768]{1,0:T(8,128)(2,1)S(1)}, bf16[224,768]{1,0:T(8,128)(2,1)S(1)}, u32[]{:S(2)}, u32[]{:S(2)}) collective-permute-start(bf16[224,768]{1,0:T(8,128)(2,1)S(1)} %get-tuple-element.141), channel_id=1, source_target_pairs={{0,2},{2,0},{4,6},{6,4},{1,3},{3,1},{5,7},{7,5},{8,10},{10,8},{12,... | collective-permute-start | bytes 1032200 | tf_op jit(solution)/shard_map/ppermute | solution.py:467
  15.7 1.4 collective-permute-start.8
  17.7 2.1 %shard_map.272 = (bf16[512,768]{1,0:T(8,128)(2,1)S(1)}, bf16[512,768]{1,0:T(8,128)(2,1)S(1)}, bf16[512,192]{1,0:T(8,128)(2,1)S(1)}, bf16[512,384]{1,0:T(8,128)(2,1)S(1)}) custom-call(s32[7]{0:T(128)S(1)} %pad_add_fusion.meta_ref, bf16[128,768]{1,0:T(8,128)(2,1)S(1)} %get-tuple-element.131.x0.x_ref, bf16[128,768]{1,0:T(8,128)(2,1)S(1)} %collective-permute-done.x1, ...), custom_call_target="tpu_custom_call" | custom-call | tf_op jit(solution)/shard_map/pallas_call | solution.py:58
  19.8 2.4 %all_gather.33.kv_ref = bf16[1024,384]{1,0:T(8,128)(2,1)S(1)} all-gather(bf16[512,384]{1,0:T(8,128)(2,1)S(1)} %get-tuple-element.137), channel_id=1, replica_groups=mesh['dp'=4,'tensor'=4,'ctx'=2] {'ctx'}, dimensions={0}, use_global_device_ids=true | all-gather | bytes 1179648 | tf_op jit(solution)/shard_map/all_gather | solution.py:534
  22.2 4.5 %shard_map.273 = (bf16[192,512]{1,0:T(8,128)(2,1)S(1)}, f32[8,512]{1,0:T(8,128)S(1)}) custom-call(s32[7]{0:T(128)S(1)} %pad_add_fusion.meta_ref, bf16[512,192]{1,0:T(8,128)(2,1)S(1)} %get-tuple-element.171.q_ref, bf16[1024,384]{1,0:T(8,128)(2,1)S(1)} %all_gather.33.kv_ref), custom_call_target="tpu_custom_call" | custom-call | tf_op jit(solution)/shard_map/pallas_call | solution.py:58
  26.7 2.1 %collective-permute-start.5 = (bf16[192,512]{1,0:T(8,128)(2,1)S(1)}, bf16[192,512]{1,0:T(8,128)(2,1)S(1)}, u32[]{:S(2)}, u32[]{:S(2)}) collective-permute-start(bf16[192,512]{1,0:T(8,128)(2,1)S(1)} %get-tuple-element.139.m0.mix_ref), channel_id=1, source_target_pairs={{0,6},{2,4},{4,2},{6,0},{1,7},{3,5},{5,3},{7,1},{8,14},{10,12},{12... | collective-permute-start | bytes 589832 | tf_op jit(solution)/shard_map/ppermute | solution.py:467
  28.9 0.9 collective-permute-start.4
  30.3 2.3 %collective-permute-done.8.c3 = bf16[224,768]{1,0:T(8,128)(2,1)S(1)} collective-permute-done((bf16[224,768]{1,0:T(8,128)(2,1)S(1)}, bf16[224,768]{1,0:T(8,128)(2,1)S(1)}, u32[]{:S(2)}, u32[]{:S(2)}) %collective-permute-start.8) | collective-permute-done | bytes 344096 | tf_op jit(solution)/shard_map/ppermute | solution.py:467
  32.6 6.8 %collective-permute-done.7.c2 = bf16[224,768]{1,0:T(8,128)(2,1)S(1)} collective-permute-done((bf16[224,768]{1,0:T(8,128)(2,1)S(1)}, bf16[224,768]{1,0:T(8,128)(2,1)S(1)}, u32[]{:S(2)}, u32[]{:S(2)}) %collective-permute-start.7) | collective-permute-done | bytes 344096 | tf_op jit(solution)/shard_map/ppermute | solution.py:467
  39.5 2.6 %all_gather.34.wc_ref = bf16[576,768]{1,0:T(8,128)(2,1)S(1)} all-gather(bf16[288,768]{1,0:T(8,128)(2,1)S(1)} %pad_maximum_fusion), channel_id=1, replica_groups=mesh['dp'=4,'tensor'=4,'ctx'=2] {'ctx'}, dimensions={0}, use_global_device_ids=true | all-gather | bytes 1327104 | tf_op jit(solution)/shard_map/all_gather | solution.py:534
  42.4 4.4 %shard_map.275 = (bf16[512,768]{1,0:T(8,128)(2,1)S(1)}, bf16[512,768]{1,0:T(8,128)(2,1)S(1)}, bf16[512,768]{1,0:T(8,128)(2,1)S(1)}, bf16[512,768]{1,0:T(8,128)(2...) custom-call(s32[7]{0:T(128)S(1)} %pad_add_fusion.meta_ref, ...), custom_call_target="tpu_custom_call" | custom-call | tf_op jit(solution)/shard_map/pallas_call | solution.py:58
  47.1 1.7 %collective-permute-start.10 = (bf16[128,768]{1,0:T(8,128)(2,1)S(1)}, bf16[128,768]{1,0:T(8,128)(2,1)S(1)}, u32[]{:S(2)}, u32[]{:S(2)}) collective-permute-start(bf16[128,768]{1,0:T(8,128)(2,1)S(1)} %get-tuple-element.162), channel_id=1, source_target_pairs={{0,4},{2,6},{4,0},{6,2},{1,5},{3,7},{5,1},{7,3},{8,12},{10,14},{12... | collective-permute-start | bytes 589832 | tf_op jit(solution)/shard_map/ppermute | solution.py:467
  48.8 1.5 %collective-permute-start.11 = (bf16[128,768]{1,0:T(8,128)(2,1)S(1)}, bf16[128,768]{1,0:T(8,128)(2,1)S(1)}, u32[]{:S(2)}, u32[]{:S(2)}) collective-permute-start(bf16[128,768]{1,0:T(8,128)(2,1)S(1)} %get-tuple-element.163), channel_id=1, source_target_pairs={{0,6},{2,4},{4,2},{6,0},{1,7},{3,5},{5,3},{7,1},{8,14},{10,12},{12... | collective-permute-start | bytes 589832 | tf_op jit(solution)/shard_map/ppermute | solution.py:467
  50.3 1.4 shard_map.276
  51.8 2.2 %all_gather.35.pair_ref = bf16[384,768]{1,0:T(8,128)(2,1)S(1)} all-gather(bf16[192,768]{1,0:T(8,128)(2,1)S(1)} %get-tuple-element.154), channel_id=1, replica_groups=mesh['dp'=4,'tensor'=4,'ctx'=2] {'ctx'}, dimensions={0}, use_global_device_ids=true | all-gather | bytes 884736 | tf_op jit(solution)/shard_map/all_gather | solution.py:534
  54.6 1.7 %collective-permute-start.12 = (bf16[192,768]{1,0:T(8,128)(2,1)S(1)}, bf16[192,768]{1,0:T(8,128)(2,1)S(1)}, u32[]{:S(2)}, u32[]{:S(2)}) collective-permute-start(bf16[192,768]{1,0:T(8,128)(2,1)S(1)} %shard_map.277), channel_id=1, source_target_pairs={{0,8},{8,0},{16,24},{24,16},{1,9},{9,1},{17,25},{25,17},{2,10},{10... | collective-permute-start | bytes 884744 | tf_op jit(solution)/shard_map/ppermute | solution.py:561
  56.3 1.4 shard_map.278
  58.3 1.5 %collective-permute-start.16 = (bf16[128,768]{1,0:T(8,128)(2,1)S(1)}, bf16[128,768]{1,0:T(8,128)(2,1)S(1)}, u32[]{:S(2)}, u32[]{:S(2)}) collective-permute-start(bf16[128,768]{1,0:T(8,128)(2,1)S(1)} %get-tuple-element.173.b0), channel_id=1, source_target_pairs={{0,6},{2,4},{4,2},{6,0},{1,7},{3,5},{5,3},{7,1},{8,14},{10,12},{12... | collective-permute-start | bytes 589832 | tf_op jit(solution)/shard_map/ppermute | solution.py:467
  59.8 1.7 %collective-permute-start.15 = (bf16[128,768]{1,0:T(8,128)(2,1)S(1)}, bf16[128,768]{1,0:T(8,128)(2,1)S(1)}, u32[]{:S(2)}, u32[]{:S(2)}) collective-permute-start(bf16[128,768]{1,0:T(8,128)(2,1)S(1)} %get-tuple-element.173.b0), channel_id=1, source_target_pairs={{0,4},{2,6},{4,0},{6,2},{1,5},{3,7},{5,1},{7,3},{8,12},{10,14},{12... | collective-permute-start | bytes 589832 | tf_op jit(solution)/shard_map/ppermute | solution.py:467
  61.9 2.2 %all_gather.36.pair_ref = bf16[384,768]{1,0:T(8,128)(2,1)S(1)} all-gather(bf16[192,768]{1,0:T(8,128)(2,1)S(1)} %get-tuple-element.166), channel_id=1, replica_groups=mesh['dp'=4,'tensor'=4,'ctx'=2] {'ctx'}, dimensions={0}, use_global_device_ids=true | all-gather | bytes 884736 | tf_op jit(solution)/shard_map/all_gather | solution.py:534
  65.0 1.6 %collective-permute-start.17 = (bf16[192,768]{1,0:T(8,128)(2,1)S(1)}, bf16[192,768]{1,0:T(8,128)(2,1)S(1)}, u32[]{:S(2)}, u32[]{:S(2)}) collective-permute-start(bf16[192,768]{1,0:T(8,128)(2,1)S(1)} %shard_map.280), channel_id=1, source_target_pairs={{0,8},{8,0},{16,24},{24,16},{1,9},{9,1},{17,25},{25,17},{2,10},{10... | collective-permute-start | bytes 884744 | tf_op jit(solution)/shard_map/ppermute | solution.py:561
  67.1 2.6 %collective-permute-start.19 = (bf16[192,768]{1,0:T(8,128)(2,1)S(1)}, bf16[192,768]{1,0:T(8,128)(2,1)S(1)}, u32[]{:S(2)}, u32[]{:S(2)}) collective-permute-start(bf16[192,768]{1,0:T(8,128)(2,1)S(1)} %shard_map.281.refs_0_), channel_id=1, source_target_pairs={{0,16},{8,24},{16,0},{24,8},{1,17},{9,25},{17,1},{25,9},{2,18},{10... | collective-permute-start | bytes 884744 | tf_op jit(solution)/shard_map/ppermute | solution.py:579
  69.7 1.4 shard_map.282
  71.1 5.7 %shard_map.283 = (bf16[192,512]{1,0:T(8,128)(2,1)S(1)}, f32[512,384]{1,0:T(8,128)S(1)}, bf16[512,384]{1,0:T(8,128)(2,1)S(1)}, bf16[512,768]{1,0:T(8,128)(2,1)S(1)}) custom-call(s32[7]{0:T(128)S(1)} %pad_add_fusion.meta_ref, bf16[512,192]{1,0:T(8,128)(2,1)S(1)} %get-tuple-element.171.q_ref, bf16[1024,384]{1,0:T(8,128)(2,1)S(1)} %all_gather.33.kv_ref, ...), custom_call_target="tpu_custom_call" | custom-call | tf_op jit(solution)/shard_map/pallas_call | solution.py:58
  76.8 3.8 %all_gather.37.got_kv = bf16[1024,384]{1,0:T(8,128)(2,1)S(1)} all-gather(bf16[512,384]{1,0:T(8,128)(2,1)S(1)} %get-tuple-element.176), channel_id=1, replica_groups=mesh['dp'=4,'tensor'=4,'ctx'=2] {'ctx'}, dimensions={0}, use_global_device_ids=true | all-gather | bytes 1179648 | tf_op jit(solution)/shard_map/all_gather | solution.py:534
  80.7 2.3 %collective-permute-done.19.refs_1_ = bf16[192,768]{1,0:T(8,128)(2,1)S(1)} collective-permute-done((bf16[192,768]{1,0:T(8,128)(2,1)S(1)}, bf16[192,768]{1,0:T(8,128)(2,1)S(1)}, u32[]{:S(2)}, u32[]{:S(2)}) %collective-permute-start.19) | collective-permute-done | bytes 294944 | tf_op jit(solution)/shard_map/ppermute | solution.py:579
  83.1 2.0 %shard_map.286 = (bf16[96,768]{1,0:T(8,128)(2,1)S(1)}, bf16[96,768]{1,0:T(8,128)(2,1)S(1)}, bf16[192,768]{1,0:T(8,128)(2,1)S(1)}, f32[128,768]{1,0:T(8,128)S(1)}...) custom-call(s32[7]{0:T(128)S(1)} %pad_add_fusion.meta_ref, ...), custom_call_target="tpu_custom_call" | custom-call | tf_op jit(solution)/shard_map/pallas_call | solution.py:58
  85.0 1.7 %collective-permute-start.20 = (bf16[272,768]{1,0:T(8,128)(2,1)S(1)}, bf16[272,768]{1,0:T(8,128)(2,1)S(1)}, u32[]{:S(2)}, u32[]{:S(2)}) collective-permute-start(bf16[272,768]{1,0:T(8,128)(2,1)S(1)} %get-tuple-element.199), channel_id=1, source_target_pairs={{0,2},{2,0},{4,6},{6,4},{1,3},{3,1},{5,7},{7,5},{8,10},{10,8},{12,... | collective-permute-start | bytes 1253384 | tf_op jit(solution)/shard_map/ppermute | solution.py:790
  86.9 2.2 %all_gather.38.pair_ref = bf16[384,768]{1,0:T(8,128)(2,1)S(1)} all-gather(bf16[192,768]{1,0:T(8,128)(2,1)S(1)} %get-tuple-element.187), channel_id=1, replica_groups=mesh['dp'=4,'tensor'=4,'ctx'=2] {'ctx'}, dimensions={0}, use_global_device_ids=true | all-gather | bytes 884736 | tf_op jit(solution)/shard_map/all_gather | solution.py:534
  89.8 1.1 shard_map.288
  90.9 2.2 %all_gather.39.pair_ref = bf16[384,768]{1,0:T(8,128)(2,1)S(1)} all-gather(bf16[192,768]{1,0:T(8,128)(2,1)S(1)} %get-tuple-element.196), channel_id=1, replica_groups=mesh['dp'=4,'tensor'=4,'ctx'=2] {'ctx'}, dimensions={0}, use_global_device_ids=true | all-gather | bytes 884736 | tf_op jit(solution)/shard_map/all_gather | solution.py:534
  93.7 1.0 collective-permute-done.20.got.g1
  94.8 1.6 %collective-permute-start.23 = (bf16[144,768]{1,0:T(8,128)(2,1)S(1)}, bf16[144,768]{1,0:T(8,128)(2,1)S(1)}, u32[]{:S(2)}, u32[]{:S(2)}) collective-permute-start(bf16[144,768]{1,0:T(8,128)(2,1)S(1)} %get-tuple-element.201), channel_id=1, source_target_pairs={{0,4},{2,6},{4,0},{6,2},{1,5},{3,7},{5,1},{7,3},{8,12},{10,14},{12... | collective-permute-start | bytes 663560 | tf_op jit(solution)/shard_map/ppermute | solution.py:809
  96.4 1.8 %collective-permute-start.21 = (bf16[96,768]{1,0:T(8,128)(2,1)S(1)}, bf16[96,768]{1,0:T(8,128)(2,1)S(1)}, u32[]{:S(2)}, u32[]{:S(2)}) collective-permute-start(bf16[96,768]{1,0:T(8,128)(2,1)S(1)} %get-tuple-element.190), channel_id=1, source_target_pairs={{0,8},{8,0},{16,24},{24,16},{1,9},{9,1},{17,25},{25,17},{2,10},{10... | collective-permute-start | bytes 442376 | tf_op jit(solution)/shard_map/ppermute | solution.py:553
  98.4 5.4 %collective-permute-done.21.refs_1_ = bf16[96,768]{1,0:T(8,128)(2,1)S(1)} collective-permute-done((bf16[96,768]{1,0:T(8,128)(2,1)S(1)}, bf16[96,768]{1,0:T(8,128)(2,1)S(1)}, u32[]{:S(2)}, u32[]{:S(2)}) %collective-permute-start.21) | collective-permute-done | bytes 147488 | tf_op jit(solution)/shard_map/ppermute | solution.py:553
  104.0 1.1 shard_map.293
  105.5 1.7 %collective-permute-start.30 = (bf16[96,768]{1,0:T(8,128)(2,1)S(1)}, bf16[96,768]{1,0:T(8,128)(2,1)S(1)}, u32[]{:S(2)}, u32[]{:S(2)}) collective-permute-start(bf16[96,768]{1,0:T(8,128)(2,1)S(1)} %shard_map.291.refs_0_), channel_id=1, source_target_pairs={{0,16},{8,24},{16,0},{24,8},{1,17},{9,25},{17,1},{25,9},{2,18},{10... | collective-permute-start | bytes 442376 | tf_op jit(solution)/shard_map/ppermute | solution.py:579
  107.3 1.3 collective-permute-start.31
  108.6 1.1 collective-permute-start.26
  109.7 0.9 collective-permute-start.25
  110.6 2.2 %all_gather.40.refs_2_ = bf16[384,768]{1,0:T(8,128)(2,1)S(1)} all-gather(bf16[192,768]{1,0:T(8,128)(2,1)S(1)} %shard_map.285.refs_0_), channel_id=1, replica_groups=mesh['dp'=4,'tensor'=4,'ctx'=2] {'ctx'}, dimensions={0}, use_global_device_ids=true | all-gather | bytes 884736 | tf_op jit(solution)/shard_map/all_gather | solution.py:534
  112.8 2.2 %all_gather.41.refs_2_ = bf16[384,768]{1,0:T(8,128)(2,1)S(1)} all-gather(bf16[192,768]{1,0:T(8,128)(2,1)S(1)} %shard_map.292.refs_0_), channel_id=1, replica_groups=mesh['dp'=4,'tensor'=4,'ctx'=2] {'ctx'}, dimensions={0}, use_global_device_ids=true | all-gather | bytes 884736 | tf_op jit(solution)/shard_map/all_gather | solution.py:534
  115.0 0.9 collective-permute-done.27.got.g1
  116.0 8.8 %collective-permute-done.26.refs_1_ = bf16[192,768]{1,0:T(8,128)(2,1)S(1)} collective-permute-done((bf16[192,768]{1,0:T(8,128)(2,1)S(1)}, bf16[192,768]{1,0:T(8,128)(2,1)S(1)}, u32[]{:S(2)}, u32[]{:S(2)}) %collective-permute-start.26) | collective-permute-done | bytes 294944 | tf_op jit(solution)/shard_map/ppermute | solution.py:591
  124.9 4.7 %collective-permute-done.25.refs_1_ = bf16[192,768]{1,0:T(8,128)(2,1)S(1)} collective-permute-done((bf16[192,768]{1,0:T(8,128)(2,1)S(1)}, bf16[192,768]{1,0:T(8,128)(2,1)S(1)}, u32[]{:S(2)}, u32[]{:S(2)}) %collective-permute-start.25) | collective-permute-done | bytes 294944 | tf_op jit(solution)/shard_map/ppermute | solution.py:591
  129.7 2.0 %collective-permute-start.33 = (bf16[96,768]{1,0:T(8,128)(2,1)S(1)}, bf16[96,768]{1,0:T(8,128)(2,1)S(1)}, u32[]{:S(2)}, u32[]{:S(2)}) collective-permute-start(bf16[96,768]{1,0:T(8,128)(2,1)S(1)} %shard_map.296.refs_4_), channel_id=1, source_target_pairs={{0,8},{8,0},{16,24},{24,16},{1,9},{9,1},{17,25},{25,17},{2,10},{10... | collective-permute-start | bytes 442376 | tf_op jit(solution)/shard_map/ppermute | solution.py:591
  131.8 1.5 %collective-permute-start.34 = (bf16[128,768]{1,0:T(8,128)(2,1)S(1)}, bf16[128,768]{1,0:T(8,128)(2,1)S(1)}, u32[]{:S(2)}, u32[]{:S(2)}) collective-permute-start(bf16[128,768]{1,0:T(8,128)(2,1)S(1)} %shard_map.295), channel_id=1, source_target_pairs={{0,4},{2,6},{4,0},{6,2},{1,5},{3,7},{5,1},{7,3},{8,12},{10,14},{12... | collective-permute-start | bytes 589832 | tf_op jit(solution)/shard_map/ppermute | solution.py:828
  133.8 2.0 %all_gather.42.refs_6_ = bf16[192,768]{1,0:T(8,128)(2,1)S(1)} all-gather(bf16[96,768]{1,0:T(8,128)(2,1)S(1)} %shard_map.296.refs_4_), channel_id=1, replica_groups=mesh['dp'=4,'tensor'=4,'ctx'=2] {'ctx'}, dimensions={0}, use_global_device_ids=true | all-gather | bytes 442368 | tf_op jit(solution)/shard_map/all_gather | solution.py:534
  135.8 2.0 %all_gather.43.refs_2_ = bf16[224,768]{1,0:T(8,128)(2,1)S(1)} all-gather(bf16[112,768]{1,0:T(8,128)(2,1)S(1)} %shard_map.297.refs_0_), channel_id=1, replica_groups=mesh['dp'=4,'tensor'=4,'ctx'=2] {'ctx'}, dimensions={0}, use_global_device_ids=true | all-gather | bytes 516096 | tf_op jit(solution)/shard_map/all_gather | solution.py:534
  138.4 2.1 %shard_map.298 = f32[768,768]{1,0:T(8,128)} custom-call(s32[7]{0:T(128)S(1)} %pad_add_fusion.meta_ref, bf16[192,768]{1,0:T(8,128)(2,1)S(1)} %shard_map.285.refs_0_, bf16[192,768]{1,0:T(8,128)(2,1)S(1)} %collective-permute-done.26.refs_1_, bf16[384,768]{1,0:T(8,128)(2,1)S(1)} %all_gather.40.refs_2_, bf16[192,768]{1,0:T(8,128)(2,1)S(1)} %collective-permute-done.29.refs_3_), custom_call_target="tpu_custom_call" | custom-call | tf_op jit(solution)/shard_map/pallas_call | solution.py:58
  140.5 2.1 %shard_map.299 = f32[768,768]{1,0:T(8,128)} custom-call(s32[7]{0:T(128)S(1)} %pad_add_fusion.meta_ref, bf16[192,768]{1,0:T(8,128)(2,1)S(1)} %shard_map.292.refs_0_, bf16[192,768]{1,0:T(8,128)(2,1)S(1)} %collective-permute-done.25.refs_1_, bf16[384,768]{1,0:T(8,128)(2,1)S(1)} %all_gather.41.refs_2_, bf16[192,768]{1,0:T(8,128)(2,1)S(1)} %collective-permute-done.28.refs_3_), custom_call_target="tpu_custom_call" | custom-call | tf_op jit(solution)/shard_map/pallas_call | solution.py:58
  142.6 0.8 shard_map.300
  143.4 2.1 %shard_map.301 = (f32[576,768]{1,0:T(8,128)}, f32[192,768]{1,0:T(8,128)}, f32[768]{0:T(1024)}, f32[768]{0:T(1024)}, f32[768]{0:T(1024)}, /*index=5*/f32[768]{0:T...) custom-call(s32[7]{0:T(128)S(1)} %pad_add_fusion.meta_ref, ...), custom_call_target="tpu_custom_call" | custom-call | tf_op jit(solution)/shard_map/pallas_call | solution.py:58
  (91 shorter events, 10.0 us)
Async XLA Ops:
  0.6 12.7 %collective-permute-start.2 = (bf16[128,768]{1,0:T(8,128)(2,1)}, bf16[128,768]{1,0:T(8,128)(2,1)S(1)}, u32[]{:S(2)}, u32[]{:S(2)}) collective-permute-start(bf16[128,768]{1,0:T(8,128)(2,1)} %bitcast.18), channel_id=1, source_target_pairs={{0,6},{2,4},{4,2},{6,0},{1,7},{3,5},{5,3},{7,1},{8,14},{10,12},{12... | collective-permute-start | bytes 589832 | tf_op jit(solution)/shard_map/ppermute | solution.py:467
  4.6 9.3 %collective-permute-start.1 = (bf16[128,768]{1,0:T(8,128)(2,1)}, bf16[128,768]{1,0:T(8,128)(2,1)S(1)}, u32[]{:S(2)}, u32[]{:S(2)}) collective-permute-start(bf16[128,768]{1,0:T(8,128)(2,1)} %bitcast.19), channel_id=1, source_target_pairs={{0,4},{2,6},{4,0},{6,2},{1,5},{3,7},{5,1},{7,3},{8,12},{10,14},{12... | collective-permute-start | bytes 589832 | tf_op jit(solution)/shard_map/ppermute | solution.py:467
  5.1 9.1 %collective-permute-start = (bf16[128,768]{1,0:T(8,128)(2,1)}, bf16[128,768]{1,0:T(8,128)(2,1)S(1)}, u32[]{:S(2)}, u32[]{:S(2)}) collective-permute-start(bf16[128,768]{1,0:T(8,128)(2,1)} %bitcast.20), channel_id=1, source_target_pairs={{0,2},{2,0},{4,6},{6,4},{1,3},{3,1},{5,7},{7,5},{8,10},{10,8},{12,... | collective-permute-start | bytes 589832 | tf_op jit(solution)/shard_map/ppermute | solution.py:467
  6.0 1.0 copy-start.1
  6.9 0.9 copy-start.3
  7.9 1.2 copy-start.6
  9.0 0.9 copy-start.7
  10.0 0.7 copy-start.8
  10.7 0.7 copy-start.9
  11.3 0.7 copy-start.15
  12.0 0.7 copy-start.16
  14.2 15.5 %collective-permute-start.6 = (bf16[224,768]{1,0:T(8,128)(2,1)S(1)}, bf16[224,768]{1,0:T(8,128)(2,1)S(1)}, u32[]{:S(2)}, u32[]{:S(2)}) collective-permute-start(bf16[224,768]{1,0:T(8,128)(2,1)S(1)} %get-tuple-element.141), channel_id=1, source_target_pairs={{0,2},{2,0},{4,6},{6,4},{1,3},{3,1},{5,7},{7,5},{8,10},{10,8},{12,... | collective-permute-start | bytes 1032200 | tf_op jit(solution)/shard_map/ppermute | solution.py:467
  15.7 16.9 %collective-permute-start.8 = (bf16[224,768]{1,0:T(8,128)(2,1)S(1)}, bf16[224,768]{1,0:T(8,128)(2,1)S(1)}, u32[]{:S(2)}, u32[]{:S(2)}) collective-permute-start(bf16[224,768]{1,0:T(8,128)(2,1)S(1)} %get-tuple-element.141), channel_id=1, source_target_pairs={{0,6},{2,4},{4,2},{6,0},{1,7},{3,5},{5,3},{7,1},{8,14},{10,12},{12... | collective-permute-start | bytes 1032200 | tf_op jit(solution)/shard_map/ppermute | solution.py:467
  17.1 22.3 %collective-permute-start.7 = (bf16[224,768]{1,0:T(8,128)(2,1)S(1)}, bf16[224,768]{1,0:T(8,128)(2,1)S(1)}, u32[]{:S(2)}, u32[]{:S(2)}) collective-permute-start(bf16[224,768]{1,0:T(8,128)(2,1)S(1)} %get-tuple-element.141), channel_id=1, source_target_pairs={{0,4},{2,6},{4,0},{6,2},{1,5},{3,7},{5,1},{7,3},{8,12},{10,14},{12... | collective-permute-start | bytes 1032200 | tf_op jit(solution)/shard_map/ppermute | solution.py:467
  26.6 15.5 %copy-start.10 = (f32[768]{0:T(1024)S(1)}, f32[768]{0:T(1024)}, u32[]{:S(2)}) copy-start(f32[768]{0:T(1024)} %refs_0_.3) | copy-start | bytes 9220
  26.6 15.5 %copy-start.11 = (f32[768]{0:T(1024)S(1)}, f32[768]{0:T(1024)}, u32[]{:S(2)}) copy-start(f32[768]{0:T(1024)} %refs_1_.3) | copy-start | bytes 9220
  26.6 15.5 %copy-start.12 = (f32[768]{0:T(1024)S(1)}, f32[768]{0:T(1024)}, u32[]{:S(2)}) copy-start(f32[768]{0:T(1024)} %refs_2_.3) | copy-start | bytes 9220
  26.7 15.4 %copy-start.13 = (f32[768]{0:T(1024)S(1)}, f32[768]{0:T(1024)}, u32[]{:S(2)}) copy-start(f32[768]{0:T(1024)} %refs_3_.3) | copy-start | bytes 9220
  26.7 15.4 %copy-start.14 = (f32[768]{0:T(1024)S(1)}, f32[768]{0:T(1024)}, u32[]{:S(2)}) copy-start(f32[768]{0:T(1024)} %refs_4_) | copy-start | bytes 9220
  26.7 15.7 %copy-start = (bf16[768,768]{1,0:T(8,128)(2,1)S(1)}, bf16[768,768]{1,0:T(8,128)(2,1)}, u32[]{:S(2)}) copy-start(bf16[768,768]{1,0:T(8,128)(2,1)} %down_ref.3) | copy-start | bytes 3538948
  26.7 15.6 %copy-start.2 = (bf16[192,768]{1,0:T(8,128)(2,1)S(1)}, bf16[192,768]{1,0:T(8,128)(2,1)}, u32[]{:S(2)}) copy-start(bf16[192,768]{1,0:T(8,128)(2,1)} %w_ref.3) | copy-start | bytes 884740
  26.7 15.6 %copy-start.4 = (bf16[1,128,768]{2,1,0:T(8,128)(2,1)S(1)}, bf16[1,128,768]{2,1,0:T(8,128)(2,1)}, u32[]{:S(2)}) copy-start(bf16[1,128,768]{2,1,0:T(8,128)(2,1)} %param.31) | copy-start | bytes 589828
  26.7 15.6 %copy-start.5 = (bf16[768,768]{1,0:T(8,128)(2,1)S(1)}, bf16[768,768]{1,0:T(8,128)(2,1)}, u32[]{:S(2)}) copy-start(bf16[768,768]{1,0:T(8,128)(2,1)} %up_ref.1) | copy-start | bytes 3538948
  26.7 15.4 %collective-permute-start.5 = (bf16[192,512]{1,0:T(8,128)(2,1)S(1)}, bf16[192,512]{1,0:T(8,128)(2,1)S(1)}, u32[]{:S(2)}, u32[]{:S(2)}) collective-permute-start(bf16[192,512]{1,0:T(8,128)(2,1)S(1)} %get-tuple-element.139.m0.mix_ref), channel_id=1, source_target_pairs={{0,6},{2,4},{4,2},{6,0},{1,7},{3,5},{5,3},{7,1},{8,14},{10,12},{12... | collective-permute-start | bytes 589832 | tf_op jit(solution)/shard_map/ppermute | solution.py:467
  28.9 13.5 %collective-permute-start.4 = (bf16[192,512]{1,0:T(8,128)(2,1)S(1)}, bf16[192,512]{1,0:T(8,128)(2,1)S(1)}, u32[]{:S(2)}, u32[]{:S(2)}) collective-permute-start(bf16[192,512]{1,0:T(8,128)(2,1)S(1)} %get-tuple-element.139.m0.mix_ref), channel_id=1, source_target_pairs={{0,4},{2,6},{4,0},{6,2},{1,5},{3,7},{5,1},{7,3},{8,12},{10,14},{12... | collective-permute-start | bytes 589832 | tf_op jit(solution)/shard_map/ppermute | solution.py:467
  29.8 12.6 %collective-permute-start.3 = (bf16[192,512]{1,0:T(8,128)(2,1)S(1)}, bf16[192,512]{1,0:T(8,128)(2,1)S(1)}, u32[]{:S(2)}, u32[]{:S(2)}) collective-permute-start(bf16[192,512]{1,0:T(8,128)(2,1)S(1)} %get-tuple-element.139.m0.mix_ref), channel_id=1, source_target_pairs={{0,2},{2,0},{4,6},{6,4},{1,3},{3,1},{5,7},{7,5},{8,10},{10,8},{12,... | collective-permute-start | bytes 589832 | tf_op jit(solution)/shard_map/ppermute | solution.py:467
  46.8 11.0 %collective-permute-start.9 = (bf16[128,768]{1,0:T(8,128)(2,1)S(1)}, bf16[128,768]{1,0:T(8,128)(2,1)S(1)}, u32[]{:S(2)}, u32[]{:S(2)}) collective-permute-start(bf16[128,768]{1,0:T(8,128)(2,1)S(1)} %get-tuple-element.161), channel_id=1, source_target_pairs={{0,2},{2,0},{4,6},{6,4},{1,3},{3,1},{5,7},{7,5},{8,10},{10,8},{12,... | collective-permute-start | bytes 589832 | tf_op jit(solution)/shard_map/ppermute | solution.py:467
  47.1 10.8 %collective-permute-start.10 = (bf16[128,768]{1,0:T(8,128)(2,1)S(1)}, bf16[128,768]{1,0:T(8,128)(2,1)S(1)}, u32[]{:S(2)}, u32[]{:S(2)}) collective-permute-start(bf16[128,768]{1,0:T(8,128)(2,1)S(1)} %get-tuple-element.162), channel_id=1, source_target_pairs={{0,4},{2,6},{4,0},{6,2},{1,5},{3,7},{5,1},{7,3},{8,12},{10,14},{12... | collective-permute-start | bytes 589832 | tf_op jit(solution)/shard_map/ppermute | solution.py:467
  48.8 9.1 %collective-permute-start.11 = (bf16[128,768]{1,0:T(8,128)(2,1)S(1)}, bf16[128,768]{1,0:T(8,128)(2,1)S(1)}, u32[]{:S(2)}, u32[]{:S(2)}) collective-permute-start(bf16[128,768]{1,0:T(8,128)(2,1)S(1)} %get-tuple-element.163), channel_id=1, source_target_pairs={{0,6},{2,4},{4,2},{6,0},{1,7},{3,5},{5,3},{7,1},{8,14},{10,12},{12... | collective-permute-start | bytes 589832 | tf_op jit(solution)/shard_map/ppermute | solution.py:467
  54.6 10.1 %collective-permute-start.12 = (bf16[192,768]{1,0:T(8,128)(2,1)S(1)}, bf16[192,768]{1,0:T(8,128)(2,1)S(1)}, u32[]{:S(2)}, u32[]{:S(2)}) collective-permute-start(bf16[192,768]{1,0:T(8,128)(2,1)S(1)} %shard_map.277), channel_id=1, source_target_pairs={{0,8},{8,0},{16,24},{24,16},{1,9},{9,1},{17,25},{25,17},{2,10},{10... | collective-permute-start | bytes 884744 | tf_op jit(solution)/shard_map/ppermute | solution.py:561
  56.3 8.7 %collective-permute-start.13 = (bf16[192,768]{1,0:T(8,128)(2,1)S(1)}, bf16[192,768]{1,0:T(8,128)(2,1)S(1)}, u32[]{:S(2)}, u32[]{:S(2)}) collective-permute-start(bf16[192,768]{1,0:T(8,128)(2,1)S(1)} %get-tuple-element.168), channel_id=1, source_target_pairs={{0,1},{1,0},{2,3},{3,2},{4,5},{5,4},{6,7},{7,6},{8,9},{9,8},{10,11... | collective-permute-start | bytes 884744 | tf_op jit(solution)/shard_map/ppermute | solution.py:563
  58.3 8.7 %collective-permute-start.16 = (bf16[128,768]{1,0:T(8,128)(2,1)S(1)}, bf16[128,768]{1,0:T(8,128)(2,1)S(1)}, u32[]{:S(2)}, u32[]{:S(2)}) collective-permute-start(bf16[128,768]{1,0:T(8,128)(2,1)S(1)} %get-tuple-element.173.b0), channel_id=1, source_target_pairs={{0,6},{2,4},{4,2},{6,0},{1,7},{3,5},{5,3},{7,1},{8,14},{10,12},{12... | collective-permute-start | bytes 589832 | tf_op jit(solution)/shard_map/ppermute | solution.py:467
  59.8 11.2 %collective-permute-start.15 = (bf16[128,768]{1,0:T(8,128)(2,1)S(1)}, bf16[128,768]{1,0:T(8,128)(2,1)S(1)}, u32[]{:S(2)}, u32[]{:S(2)}) collective-permute-start(bf16[128,768]{1,0:T(8,128)(2,1)S(1)} %get-tuple-element.173.b0), channel_id=1, source_target_pairs={{0,4},{2,6},{4,0},{6,2},{1,5},{3,7},{5,1},{7,3},{8,12},{10,14},{12... | collective-permute-start | bytes 589832 | tf_op jit(solution)/shard_map/ppermute | solution.py:467
  61.5 9.5 %collective-permute-start.14 = (bf16[128,768]{1,0:T(8,128)(2,1)S(1)}, bf16[128,768]{1,0:T(8,128)(2,1)S(1)}, u32[]{:S(2)}, u32[]{:S(2)}) collective-permute-start(bf16[128,768]{1,0:T(8,128)(2,1)S(1)} %get-tuple-element.173.b0), channel_id=1, source_target_pairs={{0,2},{2,0},{4,6},{6,4},{1,3},{3,1},{5,7},{7,5},{8,10},{10,8},{12,... | collective-permute-start | bytes 589832 | tf_op jit(solution)/shard_map/ppermute | solution.py:467
  64.8 15.8 %collective-permute-start.18 = (bf16[192,768]{1,0:T(8,128)(2,1)S(1)}, bf16[192,768]{1,0:T(8,128)(2,1)S(1)}, u32[]{:S(2)}, u32[]{:S(2)}) collective-permute-start(bf16[192,768]{1,0:T(8,128)(2,1)S(1)} %get-tuple-element.178), channel_id=1, source_target_pairs={{0,1},{1,0},{2,3},{3,2},{4,5},{5,4},{6,7},{7,6},{8,9},{9,8},{10,11... | collective-permute-start | bytes 884744 | tf_op jit(solution)/shard_map/ppermute | solution.py:563
  65.0 15.6 %collective-permute-start.17 = (bf16[192,768]{1,0:T(8,128)(2,1)S(1)}, bf16[192,768]{1,0:T(8,128)(2,1)S(1)}, u32[]{:S(2)}, u32[]{:S(2)}) collective-permute-start(bf16[192,768]{1,0:T(8,128)(2,1)S(1)} %shard_map.280), channel_id=1, source_target_pairs={{0,8},{8,0},{16,24},{24,16},{1,9},{9,1},{17,25},{25,17},{2,10},{10... | collective-permute-start | bytes 884744 | tf_op jit(solution)/shard_map/ppermute | solution.py:561
  67.1 15.9 %collective-permute-start.19 = (bf16[192,768]{1,0:T(8,128)(2,1)S(1)}, bf16[192,768]{1,0:T(8,128)(2,1)S(1)}, u32[]{:S(2)}, u32[]{:S(2)}) collective-permute-start(bf16[192,768]{1,0:T(8,128)(2,1)S(1)} %shard_map.281.refs_0_), channel_id=1, source_target_pairs={{0,16},{8,24},{16,0},{24,8},{1,17},{9,25},{17,1},{25,9},{2,18},{10... | collective-permute-start | bytes 884744 | tf_op jit(solution)/shard_map/ppermute | solution.py:579
  85.0 9.7 %collective-permute-start.20 = (bf16[272,768]{1,0:T(8,128)(2,1)S(1)}, bf16[272,768]{1,0:T(8,128)(2,1)S(1)}, u32[]{:S(2)}, u32[]{:S(2)}) collective-permute-start(bf16[272,768]{1,0:T(8,128)(2,1)S(1)} %get-tuple-element.199), channel_id=1, source_target_pairs={{0,2},{2,0},{4,6},{6,4},{1,3},{3,1},{5,7},{7,5},{8,10},{10,8},{12,... | collective-permute-start | bytes 1253384 | tf_op jit(solution)/shard_map/ppermute | solution.py:790
  86.8 17.1 %collective-permute-start.22 = (bf16[192,768]{1,0:T(8,128)(2,1)S(1)}, bf16[192,768]{1,0:T(8,128)(2,1)S(1)}, u32[]{:S(2)}, u32[]{:S(2)}) collective-permute-start(bf16[192,768]{1,0:T(8,128)(2,1)S(1)} %shard_map.284.refs_0_), channel_id=1, source_target_pairs={{0,16},{8,24},{16,0},{24,8},{1,17},{9,25},{17,1},{25,9},{2,18},{10... | collective-permute-start | bytes 884744 | tf_op jit(solution)/shard_map/ppermute | solution.py:579
  94.8 9.2 %collective-permute-start.23 = (bf16[144,768]{1,0:T(8,128)(2,1)S(1)}, bf16[144,768]{1,0:T(8,128)(2,1)S(1)}, u32[]{:S(2)}, u32[]{:S(2)}) collective-permute-start(bf16[144,768]{1,0:T(8,128)(2,1)S(1)} %get-tuple-element.201), channel_id=1, source_target_pairs={{0,4},{2,6},{4,0},{6,2},{1,5},{3,7},{5,1},{7,3},{8,12},{10,14},{12... | collective-permute-start | bytes 663560 | tf_op jit(solution)/shard_map/ppermute | solution.py:809
  96.4 7.5 %collective-permute-start.21 = (bf16[96,768]{1,0:T(8,128)(2,1)S(1)}, bf16[96,768]{1,0:T(8,128)(2,1)S(1)}, u32[]{:S(2)}, u32[]{:S(2)}) collective-permute-start(bf16[96,768]{1,0:T(8,128)(2,1)S(1)} %get-tuple-element.190), channel_id=1, source_target_pairs={{0,8},{8,0},{16,24},{24,16},{1,9},{9,1},{17,25},{25,17},{2,10},{10... | collective-permute-start | bytes 442376 | tf_op jit(solution)/shard_map/ppermute | solution.py:553
  98.2 9.1 %collective-permute-start.24 = (bf16[96,768]{1,0:T(8,128)(2,1)S(1)}, bf16[96,768]{1,0:T(8,128)(2,1)S(1)}, u32[]{:S(2)}, u32[]{:S(2)}) collective-permute-start(bf16[96,768]{1,0:T(8,128)(2,1)S(1)} %get-tuple-element.197), channel_id=1, source_target_pairs={{0,8},{8,0},{16,24},{24,16},{1,9},{9,1},{17,25},{25,17},{2,10},{10... | collective-permute-start | bytes 442376 | tf_op jit(solution)/shard_map/ppermute | solution.py:553
  105.0 10.9 %collective-permute-start.27 = (bf16[256,768]{1,0:T(8,128)(2,1)S(1)}, bf16[256,768]{1,0:T(8,128)(2,1)S(1)}, u32[]{:S(2)}, u32[]{:S(2)}) collective-permute-start(bf16[256,768]{1,0:T(8,128)(2,1)S(1)} %get-tuple-element.223), channel_id=1, source_target_pairs={{0,2},{2,0},{4,6},{6,4},{1,3},{3,1},{5,7},{7,5},{8,10},{10,8},{12,... | collective-permute-start | bytes 1179656 | tf_op jit(solution)/shard_map/ppermute | solution.py:824
  105.5 24.0 %collective-permute-start.30 = (bf16[96,768]{1,0:T(8,128)(2,1)S(1)}, bf16[96,768]{1,0:T(8,128)(2,1)S(1)}, u32[]{:S(2)}, u32[]{:S(2)}) collective-permute-start(bf16[96,768]{1,0:T(8,128)(2,1)S(1)} %shard_map.291.refs_0_), channel_id=1, source_target_pairs={{0,16},{8,24},{16,0},{24,8},{1,17},{9,25},{17,1},{25,9},{2,18},{10... | collective-permute-start | bytes 442376 | tf_op jit(solution)/shard_map/ppermute | solution.py:579
  107.3 22.3 %collective-permute-start.31 = (bf16[112,768]{1,0:T(8,128)(2,1)S(1)}, bf16[112,768]{1,0:T(8,128)(2,1)S(1)}, u32[]{:S(2)}, u32[]{:S(2)}) collective-permute-start(bf16[112,768]{1,0:T(8,128)(2,1)S(1)} %shard_map.294.refs_0_), channel_id=1, source_target_pairs={{0,16},{8,24},{16,0},{24,8},{1,17},{9,25},{17,1},{25,9},{2,18},{10... | collective-permute-start | bytes 516104 | tf_op jit(solution)/shard_map/ppermute | solution.py:579
  108.6 16.3 %collective-permute-start.26 = (bf16[192,768]{1,0:T(8,128)(2,1)S(1)}, bf16[192,768]{1,0:T(8,128)(2,1)S(1)}, u32[]{:S(2)}, u32[]{:S(2)}) collective-permute-start(bf16[192,768]{1,0:T(8,128)(2,1)S(1)} %shard_map.285.refs_0_), channel_id=1, source_target_pairs={{0,8},{8,0},{16,24},{24,16},{1,9},{9,1},{17,25},{25,17},{2,10},{10... | collective-permute-start | bytes 884744 | tf_op jit(solution)/shard_map/ppermute | solution.py:591
  109.7 19.9 %collective-permute-start.25 = (bf16[192,768]{1,0:T(8,128)(2,1)S(1)}, bf16[192,768]{1,0:T(8,128)(2,1)S(1)}, u32[]{:S(2)}, u32[]{:S(2)}) collective-permute-start(bf16[192,768]{1,0:T(8,128)(2,1)S(1)} %shard_map.292.refs_0_), channel_id=1, source_target_pairs={{0,8},{8,0},{16,24},{24,16},{1,9},{9,1},{17,25},{25,17},{2,10},{10... | collective-permute-start | bytes 884744 | tf_op jit(solution)/shard_map/ppermute | solution.py:591
  129.7 8.2 %collective-permute-start.32 = (bf16[112,768]{1,0:T(8,128)(2,1)S(1)}, bf16[112,768]{1,0:T(8,128)(2,1)S(1)}, u32[]{:S(2)}, u32[]{:S(2)}) collective-permute-start(bf16[112,768]{1,0:T(8,128)(2,1)S(1)} %shard_map.297.refs_0_), channel_id=1, source_target_pairs={{0,8},{8,0},{16,24},{24,16},{1,9},{9,1},{17,25},{25,17},{2,10},{10... | collective-permute-start | bytes 516104 | tf_op jit(solution)/shard_map/ppermute | solution.py:591
  129.7 8.1 %collective-permute-start.33 = (bf16[96,768]{1,0:T(8,128)(2,1)S(1)}, bf16[96,768]{1,0:T(8,128)(2,1)S(1)}, u32[]{:S(2)}, u32[]{:S(2)}) collective-permute-start(bf16[96,768]{1,0:T(8,128)(2,1)S(1)} %shard_map.296.refs_4_), channel_id=1, source_target_pairs={{0,8},{8,0},{16,24},{24,16},{1,9},{9,1},{17,25},{25,17},{2,10},{10... | collective-permute-start | bytes 442376 | tf_op jit(solution)/shard_map/ppermute | solution.py:591
  131.8 10.8 %collective-permute-start.34 = (bf16[128,768]{1,0:T(8,128)(2,1)S(1)}, bf16[128,768]{1,0:T(8,128)(2,1)S(1)}, u32[]{:S(2)}, u32[]{:S(2)}) collective-permute-start(bf16[128,768]{1,0:T(8,128)(2,1)S(1)} %shard_map.295), channel_id=1, source_target_pairs={{0,4},{2,6},{4,0},{6,2},{1,5},{3,7},{5,1},{7,3},{8,12},{10,14},{12... | collective-permute-start | bytes 589832 | tf_op jit(solution)/shard_map/ppermute | solution.py:828
  133.3 7.2 %collective-permute-start.28 = (bf16[192,768]{1,0:T(8,128)(2,1)S(1)}, bf16[192,768]{1,0:T(8,128)(2,1)S(1)}, u32[]{:S(2)}, u32[]{:S(2)}) collective-permute-start(bf16[192,768]{1,0:T(8,128)(2,1)S(1)} %collective-permute-done.25.refs_1_), channel_id=1, source_target_pairs={{0,1},{1,0},{2,3},{3,2},{4,5},{5,4},{6,7},{7,6},{8,9},{9,8},{10,11... | collective-permute-start | bytes 884744 | tf_op jit(solution)/shard_map/ppermute | solution.py:601
  133.3 5.1 %collective-permute-start.29 = (bf16[192,768]{1,0:T(8,128)(2,1)S(1)}, bf16[192,768]{1,0:T(8,128)(2,1)S(1)}, u32[]{:S(2)}, u32[]{:S(2)}) collective-permute-start(bf16[192,768]{1,0:T(8,128)(2,1)S(1)} %collective-permute-done.26.refs_1_), channel_id=1, source_target_pairs={{0,1},{1,0},{2,3},{3,2},{4,5},{5,4},{6,7},{7,6},{8,9},{9,8},{10,11... | collective-permute-start | bytes 884744 | tf_op jit(solution)/shard_map/ppermute | solution.py:601
  137.8 5.6 %collective-permute-start.35 = (bf16[112,768]{1,0:T(8,128)(2,1)S(1)}, bf16[112,768]{1,0:T(8,128)(2,1)S(1)}, u32[]{:S(2)}, u32[]{:S(2)}) collective-permute-start(bf16[112,768]{1,0:T(8,128)(2,1)S(1)} %collective-permute-done.32.refs_1_), channel_id=1, source_target_pairs={{0,1},{1,0},{2,3},{3,2},{4,5},{5,4},{6,7},{7,6},{8,9},{9,8},{10,11... | collective-permute-start | bytes 516104 | tf_op jit(solution)/shard_map/ppermute | solution.py:601
  138.0 5.4 %collective-permute-start.36 = (bf16[96,768]{1,0:T(8,128)(2,1)S(1)}, bf16[96,768]{1,0:T(8,128)(2,1)S(1)}, u32[]{:S(2)}, u32[]{:S(2)}) collective-permute-start(bf16[96,768]{1,0:T(8,128)(2,1)S(1)} %collective-permute-done.33.refs_5_), channel_id=1, source_target_pairs={{0,1},{1,0},{2,3},{3,2},{4,5},{5,4},{6,7},{7,6},{8,9},{9,8},{10,11... | collective-permute-start | bytes 442376 | tf_op jit(solution)/shard_map/ppermute | solution.py:601

commit v4 on v3

--- a/solution.py
+++ b/solution.py
@@ -434,7 +434,8 @@
     out_ref[rows_at(2 * ctx + bit, size)] = own_ref[:size].astype(F32)
     out_ref[rows_at(2 * ctx + 1 - bit, size)] = other_ref[:size].astype(F32)
     out_ref[rows_at(2 - 2 * ctx + bit, size)] = peer_rows(ctx, own_pair)[:size].astype(F32)
-    out_ref[rows_at(3 - 2 * ctx - bit, size)] = other_peer[:size].astype(F32)
+    other = other_peer if other_peer.shape[0] < 2 * size else peer_rows(ctx, other_peer)
+    out_ref[rows_at(3 - 2 * ctx - bit, size)] = other[:size].astype(F32)
 
 
 def whole_kernel(meta_ref, *refs):
@@ -597,6 +598,9 @@
     def five(self):
         self.own_pair = self.order.pair(self.own)
 
+    def six_now(self):
+        self.got_peer = self.order.pair(self.got)
+
     def six(self):
         self.got_peer = lax.ppermute(self.got, "ctx", CTX)
 
@@ -604,7 +608,6 @@
         return [self.own, self.got, self.own_pair, self.got_peer]
 
     def whole(self):
-        self.six()
         rows, cols = self.own.shape
         return self.order.call(
             whole_kernel, [shape((4 * rows, cols), F32)], [self.meta, *self.parts()], smem=1
@@ -827,6 +830,8 @@
     (o_second,) = order.call(out_second_kernel, [block_low], [o2, o_first_got], at=0)
     o_second_got = lax.ppermute(o_second, "tensor", y_pairs)
     down_sum.got = order.step(down_sum.got)
+    down_sum.six_now()
+    down_grad = down_sum.whole()
     up_sum.got = order.step(up_sum.got)
     kv_sum.four()
     qo_sum.four()
@@ -834,7 +839,7 @@
     qo_sum.five()
     kv_sum.got = order.step(kv_sum.got)
     qo_sum.got = order.step(qo_sum.got)
-    down_grad = down_sum.whole()
+    up_sum.six()
     up_weight_grad = up_sum.whole()
     (output,) = order.call(
         output_kernel, [block_low], [o0, o_first_got, o_second_got, hidden, vectors], at=0

time: 146 us -> 145 us (level)
  waiting for transfers between devices: 34.1 us -> 31.2 us
  blocking collectives: 26.1 us -> 28.5 us
    ppermute x4, waiting for transfers between devices: 13.5 us -> 10.7 us  [four_send(): self.got = lax.ppermute(self.own, 'dp', NEAR)]
    all_gather x11 -> x12, blocking collectives: 26.1 us -> 28.5 us  [pair(): self.last = lax.all_gather(self.first(x), 'ctx', axis=0, tiled=True)]
  transfers between devices with their start and end apart: 37 -> 36, of which waited for: 13 -> 14; matrix products, arithmetic and copies ran while one was open for 1% -> 1% of each run, Pallas kernels for 19% -> 19%
where the time goes in v4:
time: 145 us
  starting transfers between devices  39.9 us (28%)
  Pallas kernels  36.3 us (25%)
  waiting for transfers between devices  31.2 us (22%)
  blocking collectives  28.5 us (20%)
  local copies, waits for them, and re-layouts  6.8 us (5%)
    pallas_call x31, Pallas kernels, call(): pl.pallas_call(kernel, out_shape=out_shape, in_specs=[pl.BlockSpec(memory...  36.3 us
    all_gather x12, blocking collectives, pair(): self.last = lax.all_gather(self.first(x), 'ctx', axis=0, tiled=True)  28.5 us
    ppermute x15, starting transfers between devices, to_peers(): lax.ppermute(b, 'tensor', xor_pairs(lax.axis_size('tensor'), r))  18.8 us
    ppermute x15, waiting for transfers between devices, to_peers(): lax.ppermute(b, 'tensor', xor_pairs(lax.axis_size('tensor'), r))  10.8 us
    ppermute x4, waiting for transfers between devices, four_send(): self.got = lax.ppermute(self.own, 'dp', NEAR)  10.7 us
    unnamed x34, local copies, waits for them, and re-layouts  6.77 us
    ppermute x4, starting transfers between devices, three(): self.got = lax.ppermute(self.own, 'dp', FAR)  5.72 us
    ppermute x2, waiting for transfers between devices, both(): lax.ppermute(send, 'dp', NEAR)  5.45 us
  transfers between devices with their start and end apart: 36, of which 14 were waited for; matrix products, arithmetic and copies ran while one was open for 1% of the time, Pallas kernels for 19%

profile of v4, /device:TPU:0, one launch (start us, length us, event | category | flops | bytes accessed | tf_op | source)
XLA Modules:
  0.0 144.6 jit_solution(13266345371385085343)
XLA Ops:
  0.6 4.0 %collective-permute-start.2 = (bf16[128,768]{1,0:T(8,128)(2,1)}, bf16[128,768]{1,0:T(8,128)(2,1)S(1)}, u32[]{:S(2)}, u32[]{:S(2)}) collective-permute-start(bf16[128,768]{1,0:T(8,128)(2,1)} %bitcast.18), channel_id=1, source_target_pairs={{0,6},{2,4},{4,2},{6,0},{1,7},{3,5},{5,3},{7,1},{8,14},{10,12},{12... | collective-permute-start | bytes 589832 | tf_op jit(solution)/shard_map/ppermute | solution.py:468
  5.2 0.7 pad_add_fusion.meta_ref
  6.0 1.0 copy-done.1
  6.9 0.9 copy-done.3
  7.9 1.2 copy-done.6
  9.0 0.9 copy-done.7
  10.0 0.7 copy-done.8
  10.7 0.7 copy-done.9
  11.3 0.7 copy-done.15
  12.0 0.7 copy-done.16
  14.2 1.5 %collective-permute-start.6 = (bf16[224,768]{1,0:T(8,128)(2,1)S(1)}, bf16[224,768]{1,0:T(8,128)(2,1)S(1)}, u32[]{:S(2)}, u32[]{:S(2)}) collective-permute-start(bf16[224,768]{1,0:T(8,128)(2,1)S(1)} %get-tuple-element.141), channel_id=1, source_target_pairs={{0,2},{2,0},{4,6},{6,4},{1,3},{3,1},{5,7},{7,5},{8,10},{10,8},{12,... | collective-permute-start | bytes 1032200 | tf_op jit(solution)/shard_map/ppermute | solution.py:468
  15.7 1.4 collective-permute-start.8
  17.7 2.1 %shard_map.272 = (bf16[512,768]{1,0:T(8,128)(2,1)S(1)}, bf16[512,768]{1,0:T(8,128)(2,1)S(1)}, bf16[512,192]{1,0:T(8,128)(2,1)S(1)}, bf16[512,384]{1,0:T(8,128)(2,1)S(1)}) custom-call(s32[7]{0:T(128)S(1)} %pad_add_fusion.meta_ref, bf16[128,768]{1,0:T(8,128)(2,1)S(1)} %get-tuple-element.131.x0.x_ref, bf16[128,768]{1,0:T(8,128)(2,1)S(1)} %collective-permute-done.x1, ...), custom_call_target="tpu_custom_call" | custom-call | tf_op jit(solution)/shard_map/pallas_call | solution.py:58
  19.8 2.4 %all_gather.36.kv_ref = bf16[1024,384]{1,0:T(8,128)(2,1)S(1)} all-gather(bf16[512,384]{1,0:T(8,128)(2,1)S(1)} %get-tuple-element.137), channel_id=1, replica_groups=mesh['dp'=4,'tensor'=4,'ctx'=2] {'ctx'}, dimensions={0}, use_global_device_ids=true | all-gather | bytes 1179648 | tf_op jit(solution)/shard_map/all_gather | solution.py:535
  22.2 4.5 %shard_map.273 = (bf16[192,512]{1,0:T(8,128)(2,1)S(1)}, f32[8,512]{1,0:T(8,128)S(1)}) custom-call(s32[7]{0:T(128)S(1)} %pad_add_fusion.meta_ref, bf16[512,192]{1,0:T(8,128)(2,1)S(1)} %get-tuple-element.171.q_ref, bf16[1024,384]{1,0:T(8,128)(2,1)S(1)} %all_gather.36.kv_ref), custom_call_target="tpu_custom_call" | custom-call | tf_op jit(solution)/shard_map/pallas_call | solution.py:58
  26.7 2.1 %collective-permute-start.5 = (bf16[192,512]{1,0:T(8,128)(2,1)S(1)}, bf16[192,512]{1,0:T(8,128)(2,1)S(1)}, u32[]{:S(2)}, u32[]{:S(2)}) collective-permute-start(bf16[192,512]{1,0:T(8,128)(2,1)S(1)} %get-tuple-element.139.m0.mix_ref), channel_id=1, source_target_pairs={{0,6},{2,4},{4,2},{6,0},{1,7},{3,5},{5,3},{7,1},{8,14},{10,12},{12... | collective-permute-start | bytes 589832 | tf_op jit(solution)/shard_map/ppermute | solution.py:468
  28.9 0.9 collective-permute-start.4
  30.3 2.3 %collective-permute-done.8.c3 = bf16[224,768]{1,0:T(8,128)(2,1)S(1)} collective-permute-done((bf16[224,768]{1,0:T(8,128)(2,1)S(1)}, bf16[224,768]{1,0:T(8,128)(2,1)S(1)}, u32[]{:S(2)}, u32[]{:S(2)}) %collective-permute-start.8) | collective-permute-done | bytes 344096 | tf_op jit(solution)/shard_map/ppermute | solution.py:468
  32.6 6.8 %collective-permute-done.7.c2 = bf16[224,768]{1,0:T(8,128)(2,1)S(1)} collective-permute-done((bf16[224,768]{1,0:T(8,128)(2,1)S(1)}, bf16[224,768]{1,0:T(8,128)(2,1)S(1)}, u32[]{:S(2)}, u32[]{:S(2)}) %collective-permute-start.7) | collective-permute-done | bytes 344096 | tf_op jit(solution)/shard_map/ppermute | solution.py:468
  39.5 2.6 %all_gather.37.wc_ref = bf16[576,768]{1,0:T(8,128)(2,1)S(1)} all-gather(bf16[288,768]{1,0:T(8,128)(2,1)S(1)} %pad_maximum_fusion), channel_id=1, replica_groups=mesh['dp'=4,'tensor'=4,'ctx'=2] {'ctx'}, dimensions={0}, use_global_device_ids=true | all-gather | bytes 1327104 | tf_op jit(solution)/shard_map/all_gather | solution.py:535
  42.4 4.4 %shard_map.275 = (bf16[512,768]{1,0:T(8,128)(2,1)S(1)}, bf16[512,768]{1,0:T(8,128)(2,1)S(1)}, bf16[512,768]{1,0:T(8,128)(2,1)S(1)}, bf16[512,768]{1,0:T(8,128)(2...) custom-call(s32[7]{0:T(128)S(1)} %pad_add_fusion.meta_ref, ...), custom_call_target="tpu_custom_call" | custom-call | tf_op jit(solution)/shard_map/pallas_call | solution.py:58
  47.1 1.7 %collective-permute-start.10 = (bf16[128,768]{1,0:T(8,128)(2,1)S(1)}, bf16[128,768]{1,0:T(8,128)(2,1)S(1)}, u32[]{:S(2)}, u32[]{:S(2)}) collective-permute-start(bf16[128,768]{1,0:T(8,128)(2,1)S(1)} %get-tuple-element.162), channel_id=1, source_target_pairs={{0,4},{2,6},{4,0},{6,2},{1,5},{3,7},{5,1},{7,3},{8,12},{10,14},{12... | collective-permute-start | bytes 589832 | tf_op jit(solution)/shard_map/ppermute | solution.py:468
  48.8 1.5 %collective-permute-start.11 = (bf16[128,768]{1,0:T(8,128)(2,1)S(1)}, bf16[128,768]{1,0:T(8,128)(2,1)S(1)}, u32[]{:S(2)}, u32[]{:S(2)}) collective-permute-start(bf16[128,768]{1,0:T(8,128)(2,1)S(1)} %get-tuple-element.163), channel_id=1, source_target_pairs={{0,6},{2,4},{4,2},{6,0},{1,7},{3,5},{5,3},{7,1},{8,14},{10,12},{12... | collective-permute-start | bytes 589832 | tf_op jit(solution)/shard_map/ppermute | solution.py:468
  50.3 1.4 shard_map.276
  51.8 2.2 %all_gather.38.pair_ref = bf16[384,768]{1,0:T(8,128)(2,1)S(1)} all-gather(bf16[192,768]{1,0:T(8,128)(2,1)S(1)} %get-tuple-element.154), channel_id=1, replica_groups=mesh['dp'=4,'tensor'=4,'ctx'=2] {'ctx'}, dimensions={0}, use_global_device_ids=true | all-gather | bytes 884736 | tf_op jit(solution)/shard_map/all_gather | solution.py:535
  54.6 1.7 %collective-permute-start.12 = (bf16[192,768]{1,0:T(8,128)(2,1)S(1)}, bf16[192,768]{1,0:T(8,128)(2,1)S(1)}, u32[]{:S(2)}, u32[]{:S(2)}) collective-permute-start(bf16[192,768]{1,0:T(8,128)(2,1)S(1)} %shard_map.277), channel_id=1, source_target_pairs={{0,8},{8,0},{16,24},{24,16},{1,9},{9,1},{17,25},{25,17},{2,10},{10... | collective-permute-start | bytes 884744 | tf_op jit(solution)/shard_map/ppermute | solution.py:562
  56.3 1.4 shard_map.278
  58.3 1.5 %collective-permute-start.16 = (bf16[128,768]{1,0:T(8,128)(2,1)S(1)}, bf16[128,768]{1,0:T(8,128)(2,1)S(1)}, u32[]{:S(2)}, u32[]{:S(2)}) collective-permute-start(bf16[128,768]{1,0:T(8,128)(2,1)S(1)} %get-tuple-element.173.b0), channel_id=1, source_target_pairs={{0,6},{2,4},{4,2},{6,0},{1,7},{3,5},{5,3},{7,1},{8,14},{10,12},{12... | collective-permute-start | bytes 589832 | tf_op jit(solution)/shard_map/ppermute | solution.py:468
  59.8 1.7 %collective-permute-start.15 = (bf16[128,768]{1,0:T(8,128)(2,1)S(1)}, bf16[128,768]{1,0:T(8,128)(2,1)S(1)}, u32[]{:S(2)}, u32[]{:S(2)}) collective-permute-start(bf16[128,768]{1,0:T(8,128)(2,1)S(1)} %get-tuple-element.173.b0), channel_id=1, source_target_pairs={{0,4},{2,6},{4,0},{6,2},{1,5},{3,7},{5,1},{7,3},{8,12},{10,14},{12... | collective-permute-start | bytes 589832 | tf_op jit(solution)/shard_map/ppermute | solution.py:468
  61.9 2.2 %all_gather.39.pair_ref = bf16[384,768]{1,0:T(8,128)(2,1)S(1)} all-gather(bf16[192,768]{1,0:T(8,128)(2,1)S(1)} %get-tuple-element.166), channel_id=1, replica_groups=mesh['dp'=4,'tensor'=4,'ctx'=2] {'ctx'}, dimensions={0}, use_global_device_ids=true | all-gather | bytes 884736 | tf_op jit(solution)/shard_map/all_gather | solution.py:535
  65.0 1.6 %collective-permute-start.17 = (bf16[192,768]{1,0:T(8,128)(2,1)S(1)}, bf16[192,768]{1,0:T(8,128)(2,1)S(1)}, u32[]{:S(2)}, u32[]{:S(2)}) collective-permute-start(bf16[192,768]{1,0:T(8,128)(2,1)S(1)} %shard_map.280), channel_id=1, source_target_pairs={{0,8},{8,0},{16,24},{24,16},{1,9},{9,1},{17,25},{25,17},{2,10},{10... | collective-permute-start | bytes 884744 | tf_op jit(solution)/shard_map/ppermute | solution.py:562
  67.1 2.6 %collective-permute-start.19 = (bf16[192,768]{1,0:T(8,128)(2,1)S(1)}, bf16[192,768]{1,0:T(8,128)(2,1)S(1)}, u32[]{:S(2)}, u32[]{:S(2)}) collective-permute-start(bf16[192,768]{1,0:T(8,128)(2,1)S(1)} %shard_map.281.refs_0_), channel_id=1, source_target_pairs={{0,16},{8,24},{16,0},{24,8},{1,17},{9,25},{17,1},{25,9},{2,18},{10... | collective-permute-start | bytes 884744 | tf_op jit(solution)/shard_map/ppermute | solution.py:580
  69.7 1.4 shard_map.282
  71.1 5.7 %shard_map.283 = (bf16[192,512]{1,0:T(8,128)(2,1)S(1)}, f32[512,384]{1,0:T(8,128)S(1)}, bf16[512,384]{1,0:T(8,128)(2,1)S(1)}, bf16[512,768]{1,0:T(8,128)(2,1)S(1)}) custom-call(s32[7]{0:T(128)S(1)} %pad_add_fusion.meta_ref, bf16[512,192]{1,0:T(8,128)(2,1)S(1)} %get-tuple-element.171.q_ref, bf16[1024,384]{1,0:T(8,128)(2,1)S(1)} %all_gather.36.kv_ref, ...), custom_call_target="tpu_custom_call" | custom-call | tf_op jit(solution)/shard_map/pallas_call | solution.py:58
  76.8 3.8 %all_gather.40.got_kv = bf16[1024,384]{1,0:T(8,128)(2,1)S(1)} all-gather(bf16[512,384]{1,0:T(8,128)(2,1)S(1)} %get-tuple-element.176), channel_id=1, replica_groups=mesh['dp'=4,'tensor'=4,'ctx'=2] {'ctx'}, dimensions={0}, use_global_device_ids=true | all-gather | bytes 1179648 | tf_op jit(solution)/shard_map/all_gather | solution.py:535
  80.7 2.3 %collective-permute-done.19.refs_1_ = bf16[192,768]{1,0:T(8,128)(2,1)S(1)} collective-permute-done((bf16[192,768]{1,0:T(8,128)(2,1)S(1)}, bf16[192,768]{1,0:T(8,128)(2,1)S(1)}, u32[]{:S(2)}, u32[]{:S(2)}) %collective-permute-start.19) | collective-permute-done | bytes 294944 | tf_op jit(solution)/shard_map/ppermute | solution.py:580
  83.1 2.0 %shard_map.286 = (bf16[96,768]{1,0:T(8,128)(2,1)S(1)}, bf16[96,768]{1,0:T(8,128)(2,1)S(1)}, bf16[192,768]{1,0:T(8,128)(2,1)S(1)}, f32[128,768]{1,0:T(8,128)S(1)}...) custom-call(s32[7]{0:T(128)S(1)} %pad_add_fusion.meta_ref, ...), custom_call_target="tpu_custom_call" | custom-call | tf_op jit(solution)/shard_map/pallas_call | solution.py:58
  85.0 1.7 %collective-permute-start.20 = (bf16[272,768]{1,0:T(8,128)(2,1)S(1)}, bf16[272,768]{1,0:T(8,128)(2,1)S(1)}, u32[]{:S(2)}, u32[]{:S(2)}) collective-permute-start(bf16[272,768]{1,0:T(8,128)(2,1)S(1)} %get-tuple-element.199), channel_id=1, source_target_pairs={{0,2},{2,0},{4,6},{6,4},{1,3},{3,1},{5,7},{7,5},{8,10},{10,8},{12,... | collective-permute-start | bytes 1253384 | tf_op jit(solution)/shard_map/ppermute | solution.py:793
  86.9 2.2 %all_gather.41.pair_ref = bf16[384,768]{1,0:T(8,128)(2,1)S(1)} all-gather(bf16[192,768]{1,0:T(8,128)(2,1)S(1)} %get-tuple-element.187), channel_id=1, replica_groups=mesh['dp'=4,'tensor'=4,'ctx'=2] {'ctx'}, dimensions={0}, use_global_device_ids=true | all-gather | bytes 884736 | tf_op jit(solution)/shard_map/all_gather | solution.py:535
  89.8 1.1 shard_map.288
  90.9 2.2 %all_gather.42.pair_ref = bf16[384,768]{1,0:T(8,128)(2,1)S(1)} all-gather(bf16[192,768]{1,0:T(8,128)(2,1)S(1)} %get-tuple-element.196), channel_id=1, replica_groups=mesh['dp'=4,'tensor'=4,'ctx'=2] {'ctx'}, dimensions={0}, use_global_device_ids=true | all-gather | bytes 884736 | tf_op jit(solution)/shard_map/all_gather | solution.py:535
  93.7 1.0 collective-permute-done.20.got.g1
  94.8 1.6 %collective-permute-start.23 = (bf16[144,768]{1,0:T(8,128)(2,1)S(1)}, bf16[144,768]{1,0:T(8,128)(2,1)S(1)}, u32[]{:S(2)}, u32[]{:S(2)}) collective-permute-start(bf16[144,768]{1,0:T(8,128)(2,1)S(1)} %get-tuple-element.201), channel_id=1, source_target_pairs={{0,4},{2,6},{4,0},{6,2},{1,5},{3,7},{5,1},{7,3},{8,12},{10,14},{12... | collective-permute-start | bytes 663560 | tf_op jit(solution)/shard_map/ppermute | solution.py:812
  96.4 1.8 %collective-permute-start.21 = (bf16[96,768]{1,0:T(8,128)(2,1)S(1)}, bf16[96,768]{1,0:T(8,128)(2,1)S(1)}, u32[]{:S(2)}, u32[]{:S(2)}) collective-permute-start(bf16[96,768]{1,0:T(8,128)(2,1)S(1)} %get-tuple-element.190), channel_id=1, source_target_pairs={{0,8},{8,0},{16,24},{24,16},{1,9},{9,1},{17,25},{25,17},{2,10},{10... | collective-permute-start | bytes 442376 | tf_op jit(solution)/shard_map/ppermute | solution.py:554
  98.4 5.4 %collective-permute-done.21.refs_1_ = bf16[96,768]{1,0:T(8,128)(2,1)S(1)} collective-permute-done((bf16[96,768]{1,0:T(8,128)(2,1)S(1)}, bf16[96,768]{1,0:T(8,128)(2,1)S(1)}, u32[]{:S(2)}, u32[]{:S(2)}) %collective-permute-start.21) | collective-permute-done | bytes 147488 | tf_op jit(solution)/shard_map/ppermute | solution.py:554
  104.0 1.1 shard_map.293
  105.5 1.7 %collective-permute-start.29 = (bf16[96,768]{1,0:T(8,128)(2,1)S(1)}, bf16[96,768]{1,0:T(8,128)(2,1)S(1)}, u32[]{:S(2)}, u32[]{:S(2)}) collective-permute-start(bf16[96,768]{1,0:T(8,128)(2,1)S(1)} %shard_map.291.refs_0_), channel_id=1, source_target_pairs={{0,16},{8,24},{16,0},{24,8},{1,17},{9,25},{17,1},{25,9},{2,18},{10... | collective-permute-start | bytes 442376 | tf_op jit(solution)/shard_map/ppermute | solution.py:580
  107.3 1.3 collective-permute-start.30
  108.6 1.1 collective-permute-start.26
  109.7 0.9 collective-permute-start.25
  110.6 2.2 %all_gather.43.refs_2_ = bf16[384,768]{1,0:T(8,128)(2,1)S(1)} all-gather(bf16[192,768]{1,0:T(8,128)(2,1)S(1)} %shard_map.285.refs_0_), channel_id=1, replica_groups=mesh['dp'=4,'tensor'=4,'ctx'=2] {'ctx'}, dimensions={0}, use_global_device_ids=true | all-gather | bytes 884736 | tf_op jit(solution)/shard_map/all_gather | solution.py:535
  112.8 2.2 %all_gather.44.refs_2_ = bf16[384,768]{1,0:T(8,128)(2,1)S(1)} all-gather(bf16[192,768]{1,0:T(8,128)(2,1)S(1)} %shard_map.292.refs_0_), channel_id=1, replica_groups=mesh['dp'=4,'tensor'=4,'ctx'=2] {'ctx'}, dimensions={0}, use_global_device_ids=true | all-gather | bytes 884736 | tf_op jit(solution)/shard_map/all_gather | solution.py:535
  115.0 0.9 collective-permute-done.27.got.g1
  116.0 8.9 %collective-permute-done.26.refs_1_ = bf16[192,768]{1,0:T(8,128)(2,1)S(1)} collective-permute-done((bf16[192,768]{1,0:T(8,128)(2,1)S(1)}, bf16[192,768]{1,0:T(8,128)(2,1)S(1)}, u32[]{:S(2)}, u32[]{:S(2)}) %collective-permute-start.26) | collective-permute-done | bytes 294944 | tf_op jit(solution)/shard_map/ppermute | solution.py:592
  124.9 2.2 %all_gather.45.refs_3_ = bf16[384,768]{1,0:T(8,128)(2,1)S(1)} all-gather(bf16[192,768]{1,0:T(8,128)(2,1)S(1)} %collective-permute-done.26.refs_1_), channel_id=1, replica_groups=mesh['dp'=4,'tensor'=4,'ctx'=2] {'ctx'}, dimensions={0}, use_global_device_ids=true | all-gather | bytes 884736 | tf_op jit(solution)/shard_map/all_gather | solution.py:535
  127.1 2.1 %shard_map.296 = f32[768,768]{1,0:T(8,128)} custom-call(s32[7]{0:T(128)S(1)} %pad_add_fusion.meta_ref, bf16[192,768]{1,0:T(8,128)(2,1)S(1)} %shard_map.285.refs_0_, bf16[192,768]{1,0:T(8,128)(2,1)S(1)} %collective-permute-done.26.refs_1_, bf16[384,768]{1,0:T(8,128)(2,1)S(1)} %all_gather.43.refs_2_, bf16[384,768]{1,0:T(8,128)(2,1)S(1)} %all_gather.45.refs_3_), custom_call_target="tpu_custom_call" | custom-call | tf_op jit(solution)/shard_map/pallas_call | solution.py:58
  129.7 1.6 %collective-permute-start.33 = (bf16[128,768]{1,0:T(8,128)(2,1)S(1)}, bf16[128,768]{1,0:T(8,128)(2,1)S(1)}, u32[]{:S(2)}, u32[]{:S(2)}) collective-permute-start(bf16[128,768]{1,0:T(8,128)(2,1)S(1)} %shard_map.295), channel_id=1, source_target_pairs={{0,4},{2,6},{4,0},{6,2},{1,5},{3,7},{5,1},{7,3},{8,12},{10,14},{12... | collective-permute-start | bytes 589832 | tf_op jit(solution)/shard_map/ppermute | solution.py:831
  131.3 1.9 %collective-permute-start.32 = (bf16[96,768]{1,0:T(8,128)(2,1)S(1)}, bf16[96,768]{1,0:T(8,128)(2,1)S(1)}, u32[]{:S(2)}, u32[]{:S(2)}) collective-permute-start(bf16[96,768]{1,0:T(8,128)(2,1)S(1)} %shard_map.297.refs_4_), channel_id=1, source_target_pairs={{0,8},{8,0},{16,24},{24,16},{1,9},{9,1},{17,25},{25,17},{2,10},{10... | collective-permute-start | bytes 442376 | tf_op jit(solution)/shard_map/ppermute | solution.py:592
  133.3 2.1 %all_gather.46.refs_6_ = bf16[192,768]{1,0:T(8,128)(2,1)S(1)} all-gather(bf16[96,768]{1,0:T(8,128)(2,1)S(1)} %shard_map.297.refs_4_), channel_id=1, replica_groups=mesh['dp'=4,'tensor'=4,'ctx'=2] {'ctx'}, dimensions={0}, use_global_device_ids=true | all-gather | bytes 442368 | tf_op jit(solution)/shard_map/all_gather | solution.py:535
  135.4 2.0 %all_gather.47.refs_2_ = bf16[224,768]{1,0:T(8,128)(2,1)S(1)} all-gather(bf16[112,768]{1,0:T(8,128)(2,1)S(1)} %shard_map.298.refs_0_), channel_id=1, replica_groups=mesh['dp'=4,'tensor'=4,'ctx'=2] {'ctx'}, dimensions={0}, use_global_device_ids=true | all-gather | bytes 516096 | tf_op jit(solution)/shard_map/all_gather | solution.py:535
  137.4 1.5 %collective-permute-done.32.refs_5_ = bf16[96,768]{1,0:T(8,128)(2,1)S(1)} collective-permute-done((bf16[96,768]{1,0:T(8,128)(2,1)S(1)}, bf16[96,768]{1,0:T(8,128)(2,1)S(1)}, u32[]{:S(2)}, u32[]{:S(2)}) %collective-permute-start.32) | collective-permute-done | bytes 147488 | tf_op jit(solution)/shard_map/ppermute | solution.py:592
  139.5 2.1 %shard_map.299 = f32[768,768]{1,0:T(8,128)} custom-call(s32[7]{0:T(128)S(1)} %pad_add_fusion.meta_ref, bf16[192,768]{1,0:T(8,128)(2,1)S(1)} %shard_map.292.refs_0_, bf16[192,768]{1,0:T(8,128)(2,1)S(1)} %collective-permute-done.25.refs_1_, bf16[384,768]{1,0:T(8,128)(2,1)S(1)} %all_gather.44.refs_2_, bf16[192,768]{1,0:T(8,128)(2,1)S(1)} %collective-permute-done.28.refs_3_), custom_call_target="tpu_custom_call" | custom-call | tf_op jit(solution)/shard_map/pallas_call | solution.py:58
  141.6 0.8 shard_map.300
  142.4 2.1 %shard_map.301 = (f32[576,768]{1,0:T(8,128)}, f32[192,768]{1,0:T(8,128)}, f32[768]{0:T(1024)}, f32[768]{0:T(1024)}, f32[768]{0:T(1024)}, /*index=5*/f32[768]{0:T...) custom-call(s32[7]{0:T(128)S(1)} %pad_add_fusion.meta_ref, ...), custom_call_target="tpu_custom_call" | custom-call | tf_op jit(solution)/shard_map/pallas_call | solution.py:58
  (90 shorter events, 10.5 us)
Async XLA Ops:
  0.6 12.7 %collective-permute-start.2 = (bf16[128,768]{1,0:T(8,128)(2,1)}, bf16[128,768]{1,0:T(8,128)(2,1)S(1)}, u32[]{:S(2)}, u32[]{:S(2)}) collective-permute-start(bf16[128,768]{1,0:T(8,128)(2,1)} %bitcast.18), channel_id=1, source_target_pairs={{0,6},{2,4},{4,2},{6,0},{1,7},{3,5},{5,3},{7,1},{8,14},{10,12},{12... | collective-permute-start | bytes 589832 | tf_op jit(solution)/shard_map/ppermute | solution.py:468
  4.6 9.3 %collective-permute-start.1 = (bf16[128,768]{1,0:T(8,128)(2,1)}, bf16[128,768]{1,0:T(8,128)(2,1)S(1)}, u32[]{:S(2)}, u32[]{:S(2)}) collective-permute-start(bf16[128,768]{1,0:T(8,128)(2,1)} %bitcast.19), channel_id=1, source_target_pairs={{0,4},{2,6},{4,0},{6,2},{1,5},{3,7},{5,1},{7,3},{8,12},{10,14},{12... | collective-permute-start | bytes 589832 | tf_op jit(solution)/shard_map/ppermute | solution.py:468
  5.1 9.1 %collective-permute-start = (bf16[128,768]{1,0:T(8,128)(2,1)}, bf16[128,768]{1,0:T(8,128)(2,1)S(1)}, u32[]{:S(2)}, u32[]{:S(2)}) collective-permute-start(bf16[128,768]{1,0:T(8,128)(2,1)} %bitcast.20), channel_id=1, source_target_pairs={{0,2},{2,0},{4,6},{6,4},{1,3},{3,1},{5,7},{7,5},{8,10},{10,8},{12,... | collective-permute-start | bytes 589832 | tf_op jit(solution)/shard_map/ppermute | solution.py:468
  6.0 1.0 copy-start.1
  6.9 0.9 copy-start.3
  7.9 1.2 copy-start.6
  9.0 0.9 copy-start.7
  10.0 0.7 copy-start.8
  10.7 0.7 copy-start.9
  11.3 0.7 copy-start.15
  12.0 0.7 copy-start.16
  14.2 15.5 %collective-permute-start.6 = (bf16[224,768]{1,0:T(8,128)(2,1)S(1)}, bf16[224,768]{1,0:T(8,128)(2,1)S(1)}, u32[]{:S(2)}, u32[]{:S(2)}) collective-permute-start(bf16[224,768]{1,0:T(8,128)(2,1)S(1)} %get-tuple-element.141), channel_id=1, source_target_pairs={{0,2},{2,0},{4,6},{6,4},{1,3},{3,1},{5,7},{7,5},{8,10},{10,8},{12,... | collective-permute-start | bytes 1032200 | tf_op jit(solution)/shard_map/ppermute | solution.py:468
  15.7 16.9 %collective-permute-start.8 = (bf16[224,768]{1,0:T(8,128)(2,1)S(1)}, bf16[224,768]{1,0:T(8,128)(2,1)S(1)}, u32[]{:S(2)}, u32[]{:S(2)}) collective-permute-start(bf16[224,768]{1,0:T(8,128)(2,1)S(1)} %get-tuple-element.141), channel_id=1, source_target_pairs={{0,6},{2,4},{4,2},{6,0},{1,7},{3,5},{5,3},{7,1},{8,14},{10,12},{12... | collective-permute-start | bytes 1032200 | tf_op jit(solution)/shard_map/ppermute | solution.py:468
  17.1 22.3 %collective-permute-start.7 = (bf16[224,768]{1,0:T(8,128)(2,1)S(1)}, bf16[224,768]{1,0:T(8,128)(2,1)S(1)}, u32[]{:S(2)}, u32[]{:S(2)}) collective-permute-start(bf16[224,768]{1,0:T(8,128)(2,1)S(1)} %get-tuple-element.141), channel_id=1, source_target_pairs={{0,4},{2,6},{4,0},{6,2},{1,5},{3,7},{5,1},{7,3},{8,12},{10,14},{12... | collective-permute-start | bytes 1032200 | tf_op jit(solution)/shard_map/ppermute | solution.py:468
  26.6 15.5 %copy-start.10 = (f32[768]{0:T(1024)S(1)}, f32[768]{0:T(1024)}, u32[]{:S(2)}) copy-start(f32[768]{0:T(1024)} %refs_0_.3) | copy-start | bytes 9220
  26.6 15.5 %copy-start.11 = (f32[768]{0:T(1024)S(1)}, f32[768]{0:T(1024)}, u32[]{:S(2)}) copy-start(f32[768]{0:T(1024)} %refs_1_.3) | copy-start | bytes 9220
  26.6 15.5 %copy-start.12 = (f32[768]{0:T(1024)S(1)}, f32[768]{0:T(1024)}, u32[]{:S(2)}) copy-start(f32[768]{0:T(1024)} %refs_2_.3) | copy-start | bytes 9220
  26.7 15.4 %copy-start.13 = (f32[768]{0:T(1024)S(1)}, f32[768]{0:T(1024)}, u32[]{:S(2)}) copy-start(f32[768]{0:T(1024)} %refs_3_.3) | copy-start | bytes 9220
  26.7 15.4 %copy-start.14 = (f32[768]{0:T(1024)S(1)}, f32[768]{0:T(1024)}, u32[]{:S(2)}) copy-start(f32[768]{0:T(1024)} %refs_4_) | copy-start | bytes 9220
  26.7 15.7 %copy-start = (bf16[768,768]{1,0:T(8,128)(2,1)S(1)}, bf16[768,768]{1,0:T(8,128)(2,1)}, u32[]{:S(2)}) copy-start(bf16[768,768]{1,0:T(8,128)(2,1)} %down_ref.3) | copy-start | bytes 3538948
  26.7 15.6 %copy-start.2 = (bf16[192,768]{1,0:T(8,128)(2,1)S(1)}, bf16[192,768]{1,0:T(8,128)(2,1)}, u32[]{:S(2)}) copy-start(bf16[192,768]{1,0:T(8,128)(2,1)} %w_ref.3) | copy-start | bytes 884740
  26.7 15.6 %copy-start.4 = (bf16[1,128,768]{2,1,0:T(8,128)(2,1)S(1)}, bf16[1,128,768]{2,1,0:T(8,128)(2,1)}, u32[]{:S(2)}) copy-start(bf16[1,128,768]{2,1,0:T(8,128)(2,1)} %param.31) | copy-start | bytes 589828
  26.7 15.6 %copy-start.5 = (bf16[768,768]{1,0:T(8,128)(2,1)S(1)}, bf16[768,768]{1,0:T(8,128)(2,1)}, u32[]{:S(2)}) copy-start(bf16[768,768]{1,0:T(8,128)(2,1)} %up_ref.1) | copy-start | bytes 3538948
  26.7 15.4 %collective-permute-start.5 = (bf16[192,512]{1,0:T(8,128)(2,1)S(1)}, bf16[192,512]{1,0:T(8,128)(2,1)S(1)}, u32[]{:S(2)}, u32[]{:S(2)}) collective-permute-start(bf16[192,512]{1,0:T(8,128)(2,1)S(1)} %get-tuple-element.139.m0.mix_ref), channel_id=1, source_target_pairs={{0,6},{2,4},{4,2},{6,0},{1,7},{3,5},{5,3},{7,1},{8,14},{10,12},{12... | collective-permute-start | bytes 589832 | tf_op jit(solution)/shard_map/ppermute | solution.py:468
  28.9 13.5 %collective-permute-start.4 = (bf16[192,512]{1,0:T(8,128)(2,1)S(1)}, bf16[192,512]{1,0:T(8,128)(2,1)S(1)}, u32[]{:S(2)}, u32[]{:S(2)}) collective-permute-start(bf16[192,512]{1,0:T(8,128)(2,1)S(1)} %get-tuple-element.139.m0.mix_ref), channel_id=1, source_target_pairs={{0,4},{2,6},{4,0},{6,2},{1,5},{3,7},{5,1},{7,3},{8,12},{10,14},{12... | collective-permute-start | bytes 589832 | tf_op jit(solution)/shard_map/ppermute | solution.py:468
  29.8 12.6 %collective-permute-start.3 = (bf16[192,512]{1,0:T(8,128)(2,1)S(1)}, bf16[192,512]{1,0:T(8,128)(2,1)S(1)}, u32[]{:S(2)}, u32[]{:S(2)}) collective-permute-start(bf16[192,512]{1,0:T(8,128)(2,1)S(1)} %get-tuple-element.139.m0.mix_ref), channel_id=1, source_target_pairs={{0,2},{2,0},{4,6},{6,4},{1,3},{3,1},{5,7},{7,5},{8,10},{10,8},{12,... | collective-permute-start | bytes 589832 | tf_op jit(solution)/shard_map/ppermute | solution.py:468
  46.8 11.0 %collective-permute-start.9 = (bf16[128,768]{1,0:T(8,128)(2,1)S(1)}, bf16[128,768]{1,0:T(8,128)(2,1)S(1)}, u32[]{:S(2)}, u32[]{:S(2)}) collective-permute-start(bf16[128,768]{1,0:T(8,128)(2,1)S(1)} %get-tuple-element.161), channel_id=1, source_target_pairs={{0,2},{2,0},{4,6},{6,4},{1,3},{3,1},{5,7},{7,5},{8,10},{10,8},{12,... | collective-permute-start | bytes 589832 | tf_op jit(solution)/shard_map/ppermute | solution.py:468
  47.1 10.8 %collective-permute-start.10 = (bf16[128,768]{1,0:T(8,128)(2,1)S(1)}, bf16[128,768]{1,0:T(8,128)(2,1)S(1)}, u32[]{:S(2)}, u32[]{:S(2)}) collective-permute-start(bf16[128,768]{1,0:T(8,128)(2,1)S(1)} %get-tuple-element.162), channel_id=1, source_target_pairs={{0,4},{2,6},{4,0},{6,2},{1,5},{3,7},{5,1},{7,3},{8,12},{10,14},{12... | collective-permute-start | bytes 589832 | tf_op jit(solution)/shard_map/ppermute | solution.py:468
  48.8 9.1 %collective-permute-start.11 = (bf16[128,768]{1,0:T(8,128)(2,1)S(1)}, bf16[128,768]{1,0:T(8,128)(2,1)S(1)}, u32[]{:S(2)}, u32[]{:S(2)}) collective-permute-start(bf16[128,768]{1,0:T(8,128)(2,1)S(1)} %get-tuple-element.163), channel_id=1, source_target_pairs={{0,6},{2,4},{4,2},{6,0},{1,7},{3,5},{5,3},{7,1},{8,14},{10,12},{12... | collective-permute-start | bytes 589832 | tf_op jit(solution)/shard_map/ppermute | solution.py:468
  54.6 10.1 %collective-permute-start.12 = (bf16[192,768]{1,0:T(8,128)(2,1)S(1)}, bf16[192,768]{1,0:T(8,128)(2,1)S(1)}, u32[]{:S(2)}, u32[]{:S(2)}) collective-permute-start(bf16[192,768]{1,0:T(8,128)(2,1)S(1)} %shard_map.277), channel_id=1, source_target_pairs={{0,8},{8,0},{16,24},{24,16},{1,9},{9,1},{17,25},{25,17},{2,10},{10... | collective-permute-start | bytes 884744 | tf_op jit(solution)/shard_map/ppermute | solution.py:562
  56.3 8.7 %collective-permute-start.13 = (bf16[192,768]{1,0:T(8,128)(2,1)S(1)}, bf16[192,768]{1,0:T(8,128)(2,1)S(1)}, u32[]{:S(2)}, u32[]{:S(2)}) collective-permute-start(bf16[192,768]{1,0:T(8,128)(2,1)S(1)} %get-tuple-element.168), channel_id=1, source_target_pairs={{0,1},{1,0},{2,3},{3,2},{4,5},{5,4},{6,7},{7,6},{8,9},{9,8},{10,11... | collective-permute-start | bytes 884744 | tf_op jit(solution)/shard_map/ppermute | solution.py:564
  58.3 8.7 %collective-permute-start.16 = (bf16[128,768]{1,0:T(8,128)(2,1)S(1)}, bf16[128,768]{1,0:T(8,128)(2,1)S(1)}, u32[]{:S(2)}, u32[]{:S(2)}) collective-permute-start(bf16[128,768]{1,0:T(8,128)(2,1)S(1)} %get-tuple-element.173.b0), channel_id=1, source_target_pairs={{0,6},{2,4},{4,2},{6,0},{1,7},{3,5},{5,3},{7,1},{8,14},{10,12},{12... | collective-permute-start | bytes 589832 | tf_op jit(solution)/shard_map/ppermute | solution.py:468
  59.8 11.2 %collective-permute-start.15 = (bf16[128,768]{1,0:T(8,128)(2,1)S(1)}, bf16[128,768]{1,0:T(8,128)(2,1)S(1)}, u32[]{:S(2)}, u32[]{:S(2)}) collective-permute-start(bf16[128,768]{1,0:T(8,128)(2,1)S(1)} %get-tuple-element.173.b0), channel_id=1, source_target_pairs={{0,4},{2,6},{4,0},{6,2},{1,5},{3,7},{5,1},{7,3},{8,12},{10,14},{12... | collective-permute-start | bytes 589832 | tf_op jit(solution)/shard_map/ppermute | solution.py:468
  61.5 9.5 %collective-permute-start.14 = (bf16[128,768]{1,0:T(8,128)(2,1)S(1)}, bf16[128,768]{1,0:T(8,128)(2,1)S(1)}, u32[]{:S(2)}, u32[]{:S(2)}) collective-permute-start(bf16[128,768]{1,0:T(8,128)(2,1)S(1)} %get-tuple-element.173.b0), channel_id=1, source_target_pairs={{0,2},{2,0},{4,6},{6,4},{1,3},{3,1},{5,7},{7,5},{8,10},{10,8},{12,... | collective-permute-start | bytes 589832 | tf_op jit(solution)/shard_map/ppermute | solution.py:468
  64.8 15.8 %collective-permute-start.18 = (bf16[192,768]{1,0:T(8,128)(2,1)S(1)}, bf16[192,768]{1,0:T(8,128)(2,1)S(1)}, u32[]{:S(2)}, u32[]{:S(2)}) collective-permute-start(bf16[192,768]{1,0:T(8,128)(2,1)S(1)} %get-tuple-element.178), channel_id=1, source_target_pairs={{0,1},{1,0},{2,3},{3,2},{4,5},{5,4},{6,7},{7,6},{8,9},{9,8},{10,11... | collective-permute-start | bytes 884744 | tf_op jit(solution)/shard_map/ppermute | solution.py:564
  65.0 15.6 %collective-permute-start.17 = (bf16[192,768]{1,0:T(8,128)(2,1)S(1)}, bf16[192,768]{1,0:T(8,128)(2,1)S(1)}, u32[]{:S(2)}, u32[]{:S(2)}) collective-permute-start(bf16[192,768]{1,0:T(8,128)(2,1)S(1)} %shard_map.280), channel_id=1, source_target_pairs={{0,8},{8,0},{16,24},{24,16},{1,9},{9,1},{17,25},{25,17},{2,10},{10... | collective-permute-start | bytes 884744 | tf_op jit(solution)/shard_map/ppermute | solution.py:562
  67.1 15.9 %collective-permute-start.19 = (bf16[192,768]{1,0:T(8,128)(2,1)S(1)}, bf16[192,768]{1,0:T(8,128)(2,1)S(1)}, u32[]{:S(2)}, u32[]{:S(2)}) collective-permute-start(bf16[192,768]{1,0:T(8,128)(2,1)S(1)} %shard_map.281.refs_0_), channel_id=1, source_target_pairs={{0,16},{8,24},{16,0},{24,8},{1,17},{9,25},{17,1},{25,9},{2,18},{10... | collective-permute-start | bytes 884744 | tf_op jit(solution)/shard_map/ppermute | solution.py:580
  85.0 9.7 %collective-permute-start.20 = (bf16[272,768]{1,0:T(8,128)(2,1)S(1)}, bf16[272,768]{1,0:T(8,128)(2,1)S(1)}, u32[]{:S(2)}, u32[]{:S(2)}) collective-permute-start(bf16[272,768]{1,0:T(8,128)(2,1)S(1)} %get-tuple-element.199), channel_id=1, source_target_pairs={{0,2},{2,0},{4,6},{6,4},{1,3},{3,1},{5,7},{7,5},{8,10},{10,8},{12,... | collective-permute-start | bytes 1253384 | tf_op jit(solution)/shard_map/ppermute | solution.py:793
  86.8 17.1 %collective-permute-start.22 = (bf16[192,768]{1,0:T(8,128)(2,1)S(1)}, bf16[192,768]{1,0:T(8,128)(2,1)S(1)}, u32[]{:S(2)}, u32[]{:S(2)}) collective-permute-start(bf16[192,768]{1,0:T(8,128)(2,1)S(1)} %shard_map.284.refs_0_), channel_id=1, source_target_pairs={{0,16},{8,24},{16,0},{24,8},{1,17},{9,25},{17,1},{25,9},{2,18},{10... | collective-permute-start | bytes 884744 | tf_op jit(solution)/shard_map/ppermute | solution.py:580
  94.8 9.2 %collective-permute-start.23 = (bf16[144,768]{1,0:T(8,128)(2,1)S(1)}, bf16[144,768]{1,0:T(8,128)(2,1)S(1)}, u32[]{:S(2)}, u32[]{:S(2)}) collective-permute-start(bf16[144,768]{1,0:T(8,128)(2,1)S(1)} %get-tuple-element.201), channel_id=1, source_target_pairs={{0,4},{2,6},{4,0},{6,2},{1,5},{3,7},{5,1},{7,3},{8,12},{10,14},{12... | collective-permute-start | bytes 663560 | tf_op jit(solution)/shard_map/ppermute | solution.py:812
  96.4 7.5 %collective-permute-start.21 = (bf16[96,768]{1,0:T(8,128)(2,1)S(1)}, bf16[96,768]{1,0:T(8,128)(2,1)S(1)}, u32[]{:S(2)}, u32[]{:S(2)}) collective-permute-start(bf16[96,768]{1,0:T(8,128)(2,1)S(1)} %get-tuple-element.190), channel_id=1, source_target_pairs={{0,8},{8,0},{16,24},{24,16},{1,9},{9,1},{17,25},{25,17},{2,10},{10... | collective-permute-start | bytes 442376 | tf_op jit(solution)/shard_map/ppermute | solution.py:554
  98.2 9.1 %collective-permute-start.24 = (bf16[96,768]{1,0:T(8,128)(2,1)S(1)}, bf16[96,768]{1,0:T(8,128)(2,1)S(1)}, u32[]{:S(2)}, u32[]{:S(2)}) collective-permute-start(bf16[96,768]{1,0:T(8,128)(2,1)S(1)} %get-tuple-element.197), channel_id=1, source_target_pairs={{0,8},{8,0},{16,24},{24,16},{1,9},{9,1},{17,25},{25,17},{2,10},{10... | collective-permute-start | bytes 442376 | tf_op jit(solution)/shard_map/ppermute | solution.py:554
  105.0 10.9 %collective-permute-start.27 = (bf16[256,768]{1,0:T(8,128)(2,1)S(1)}, bf16[256,768]{1,0:T(8,128)(2,1)S(1)}, u32[]{:S(2)}, u32[]{:S(2)}) collective-permute-start(bf16[256,768]{1,0:T(8,128)(2,1)S(1)} %get-tuple-element.223), channel_id=1, source_target_pairs={{0,2},{2,0},{4,6},{6,4},{1,3},{3,1},{5,7},{7,5},{8,10},{10,8},{12,... | collective-permute-start | bytes 1179656 | tf_op jit(solution)/shard_map/ppermute | solution.py:827
  105.5 24.0 %collective-permute-start.29 = (bf16[96,768]{1,0:T(8,128)(2,1)S(1)}, bf16[96,768]{1,0:T(8,128)(2,1)S(1)}, u32[]{:S(2)}, u32[]{:S(2)}) collective-permute-start(bf16[96,768]{1,0:T(8,128)(2,1)S(1)} %shard_map.291.refs_0_), channel_id=1, source_target_pairs={{0,16},{8,24},{16,0},{24,8},{1,17},{9,25},{17,1},{25,9},{2,18},{10... | collective-permute-start | bytes 442376 | tf_op jit(solution)/shard_map/ppermute | solution.py:580
  107.3 22.3 %collective-permute-start.30 = (bf16[112,768]{1,0:T(8,128)(2,1)S(1)}, bf16[112,768]{1,0:T(8,128)(2,1)S(1)}, u32[]{:S(2)}, u32[]{:S(2)}) collective-permute-start(bf16[112,768]{1,0:T(8,128)(2,1)S(1)} %shard_map.294.refs_0_), channel_id=1, source_target_pairs={{0,16},{8,24},{16,0},{24,8},{1,17},{9,25},{17,1},{25,9},{2,18},{10... | collective-permute-start | bytes 516104 | tf_op jit(solution)/shard_map/ppermute | solution.py:580
  108.6 16.3 %collective-permute-start.26 = (bf16[192,768]{1,0:T(8,128)(2,1)S(1)}, bf16[192,768]{1,0:T(8,128)(2,1)S(1)}, u32[]{:S(2)}, u32[]{:S(2)}) collective-permute-start(bf16[192,768]{1,0:T(8,128)(2,1)S(1)} %shard_map.285.refs_0_), channel_id=1, source_target_pairs={{0,8},{8,0},{16,24},{24,16},{1,9},{9,1},{17,25},{25,17},{2,10},{10... | collective-permute-start | bytes 884744 | tf_op jit(solution)/shard_map/ppermute | solution.py:592
  109.7 19.9 %collective-permute-start.25 = (bf16[192,768]{1,0:T(8,128)(2,1)S(1)}, bf16[192,768]{1,0:T(8,128)(2,1)S(1)}, u32[]{:S(2)}, u32[]{:S(2)}) collective-permute-start(bf16[192,768]{1,0:T(8,128)(2,1)S(1)} %shard_map.292.refs_0_), channel_id=1, source_target_pairs={{0,8},{8,0},{16,24},{24,16},{1,9},{9,1},{17,25},{25,17},{2,10},{10... | collective-permute-start | bytes 884744 | tf_op jit(solution)/shard_map/ppermute | solution.py:592
  129.7 9.3 %collective-permute-start.31 = (bf16[112,768]{1,0:T(8,128)(2,1)S(1)}, bf16[112,768]{1,0:T(8,128)(2,1)S(1)}, u32[]{:S(2)}, u32[]{:S(2)}) collective-permute-start(bf16[112,768]{1,0:T(8,128)(2,1)S(1)} %shard_map.298.refs_0_), channel_id=1, source_target_pairs={{0,8},{8,0},{16,24},{24,16},{1,9},{9,1},{17,25},{25,17},{2,10},{10... | collective-permute-start | bytes 516104 | tf_op jit(solution)/shard_map/ppermute | solution.py:592
  129.7 11.8 %collective-permute-start.33 = (bf16[128,768]{1,0:T(8,128)(2,1)S(1)}, bf16[128,768]{1,0:T(8,128)(2,1)S(1)}, u32[]{:S(2)}, u32[]{:S(2)}) collective-permute-start(bf16[128,768]{1,0:T(8,128)(2,1)S(1)} %shard_map.295), channel_id=1, source_target_pairs={{0,4},{2,6},{4,0},{6,2},{1,5},{3,7},{5,1},{7,3},{8,12},{10,14},{12... | collective-permute-start | bytes 589832 | tf_op jit(solution)/shard_map/ppermute | solution.py:831
  131.3 7.6 %collective-permute-start.32 = (bf16[96,768]{1,0:T(8,128)(2,1)S(1)}, bf16[96,768]{1,0:T(8,128)(2,1)S(1)}, u32[]{:S(2)}, u32[]{:S(2)}) collective-permute-start(bf16[96,768]{1,0:T(8,128)(2,1)S(1)} %shard_map.297.refs_4_), channel_id=1, source_target_pairs={{0,8},{8,0},{16,24},{24,16},{1,9},{9,1},{17,25},{25,17},{2,10},{10... | collective-permute-start | bytes 442376 | tf_op jit(solution)/shard_map/ppermute | solution.py:592
  133.3 6.2 %collective-permute-start.28 = (bf16[192,768]{1,0:T(8,128)(2,1)S(1)}, bf16[192,768]{1,0:T(8,128)(2,1)S(1)}, u32[]{:S(2)}, u32[]{:S(2)}) collective-permute-start(bf16[192,768]{1,0:T(8,128)(2,1)S(1)} %collective-permute-done.25.refs_1_), channel_id=1, source_target_pairs={{0,1},{1,0},{2,3},{3,2},{4,5},{5,4},{6,7},{7,6},{8,9},{9,8},{10,11... | collective-permute-start | bytes 884744 | tf_op jit(solution)/shard_map/ppermute | solution.py:605
  138.9 3.4 %collective-permute-start.34 = (bf16[112,768]{1,0:T(8,128)(2,1)S(1)}, bf16[112,768]{1,0:T(8,128)(2,1)S(1)}, u32[]{:S(2)}, u32[]{:S(2)}) collective-permute-start(bf16[112,768]{1,0:T(8,128)(2,1)S(1)} %collective-permute-done.31.refs_1_), channel_id=1, source_target_pairs={{0,1},{1,0},{2,3},{3,2},{4,5},{5,4},{6,7},{7,6},{8,9},{9,8},{10,11... | collective-permute-start | bytes 516104 | tf_op jit(solution)/shard_map/ppermute | solution.py:605
  139.0 3.4 %collective-permute-start.35 = (bf16[96,768]{1,0:T(8,128)(2,1)S(1)}, bf16[96,768]{1,0:T(8,128)(2,1)S(1)}, u32[]{:S(2)}, u32[]{:S(2)}) collective-permute-start(bf16[96,768]{1,0:T(8,128)(2,1)S(1)} %collective-permute-done.32.refs_5_), channel_id=1, source_target_pairs={{0,1},{1,0},{2,3},{3,2},{4,5},{5,4},{6,7},{7,6},{8,9},{9,8},{10,11... | collective-permute-start | bytes 442376 | tf_op jit(solution)/shard_map/ppermute | solution.py:605

commit v5 on v4

--- a/solution.py
+++ b/solution.py
@@ -837,10 +837,10 @@
     qo_sum.four()
     kv_sum.five()
     qo_sum.five()
+    up_sum.six()
+    up_weight_grad = up_sum.whole()
     kv_sum.got = order.step(kv_sum.got)
     qo_sum.got = order.step(qo_sum.got)
-    up_sum.six()
-    up_weight_grad = up_sum.whole()
     (output,) = order.call(
         output_kernel, [block_low], [o0, o_first_got, o_second_got, hidden, vectors], at=0
     )

time: 145 us -> 144 us (level)
  transfers between devices with their start and end apart: 36 -> 36, of which waited for: 14 -> 15; matrix products, arithmetic and copies ran while one was open for 1% -> 1% of each run, Pallas kernels for 19% -> 19%
where the time goes in v5:
time: 144 us
  starting transfers between devices  40 us (28%)
  Pallas kernels  36.3 us (25%)
  waiting for transfers between devices  30.2 us (21%)
  blocking collectives  28.3 us (20%)
  local copies, waits for them, and re-layouts  6.8 us (5%)
    pallas_call x31, Pallas kernels, call(): pl.pallas_call(kernel, out_shape=out_shape, in_specs=[pl.BlockSpec(memory...  36.3 us
    all_gather x12, blocking collectives, pair(): self.last = lax.all_gather(self.first(x), 'ctx', axis=0, tiled=True)  28.3 us
    ppermute x15, starting transfers between devices, to_peers(): lax.ppermute(b, 'tensor', xor_pairs(lax.axis_size('tensor'), r))  18.8 us
    ppermute x15, waiting for transfers between devices, to_peers(): lax.ppermute(b, 'tensor', xor_pairs(lax.axis_size('tensor'), r))  10.8 us
    ppermute x4, waiting for transfers between devices, four_send(): self.got = lax.ppermute(self.own, 'dp', NEAR)  9.4 us
    unnamed x34, local copies, waits for them, and re-layouts  6.77 us
    ppermute x4, starting transfers between devices, three(): self.got = lax.ppermute(self.own, 'dp', FAR)  5.72 us
    ppermute x2, waiting for transfers between devices, both(): lax.ppermute(send, 'dp', NEAR)  5.45 us
  transfers between devices with their start and end apart: 36, of which 15 were waited for; matrix products, arithmetic and copies ran while one was open for 1% of the time, Pallas kernels for 19%

profile of v5, /device:TPU:0, one launch (start us, length us, event | category | flops | bytes accessed | tf_op | source)
XLA Modules:
  0.0 143.6 jit_solution(6224780081394550614)
XLA Ops:
  0.6 4.0 %collective-permute-start.2 = (bf16[128,768]{1,0:T(8,128)(2,1)}, bf16[128,768]{1,0:T(8,128)(2,1)S(1)}, u32[]{:S(2)}, u32[]{:S(2)}) collective-permute-start(bf16[128,768]{1,0:T(8,128)(2,1)} %bitcast.18), channel_id=1, source_target_pairs={{0,6},{2,4},{4,2},{6,0},{1,7},{3,5},{5,3},{7,1},{8,14},{10,12},{12... | collective-permute-start | bytes 589832 | tf_op jit(solution)/shard_map/ppermute | solution.py:468
  5.2 0.7 pad_add_fusion.meta_ref
  6.0 1.0 copy-done.1
  6.9 0.9 copy-done.3
  7.9 1.2 copy-done.6
  9.0 0.9 copy-done.7
  10.0 0.7 copy-done.8
  10.7 0.7 copy-done.9
  11.3 0.7 copy-done.15
  12.0 0.7 copy-done.16
  12.7 0.6 shard_map.271
  14.2 1.5 %collective-permute-start.6 = (bf16[224,768]{1,0:T(8,128)(2,1)S(1)}, bf16[224,768]{1,0:T(8,128)(2,1)S(1)}, u32[]{:S(2)}, u32[]{:S(2)}) collective-permute-start(bf16[224,768]{1,0:T(8,128)(2,1)S(1)} %get-tuple-element.141), channel_id=1, source_target_pairs={{0,2},{2,0},{4,6},{6,4},{1,3},{3,1},{5,7},{7,5},{8,10},{10,8},{12,... | collective-permute-start | bytes 1032200 | tf_op jit(solution)/shard_map/ppermute | solution.py:468
  15.7 1.4 collective-permute-start.8
  17.7 2.1 %shard_map.272 = (bf16[512,768]{1,0:T(8,128)(2,1)S(1)}, bf16[512,768]{1,0:T(8,128)(2,1)S(1)}, bf16[512,192]{1,0:T(8,128)(2,1)S(1)}, bf16[512,384]{1,0:T(8,128)(2,1)S(1)}) custom-call(s32[7]{0:T(128)S(1)} %pad_add_fusion.meta_ref, bf16[128,768]{1,0:T(8,128)(2,1)S(1)} %get-tuple-element.131.x0.x_ref, bf16[128,768]{1,0:T(8,128)(2,1)S(1)} %collective-permute-done.x1, ...), custom_call_target="tpu_custom_call" | custom-call | tf_op jit(solution)/shard_map/pallas_call | solution.py:58
  19.8 2.4 %all_gather.36.kv_ref = bf16[1024,384]{1,0:T(8,128)(2,1)S(1)} all-gather(bf16[512,384]{1,0:T(8,128)(2,1)S(1)} %get-tuple-element.137), channel_id=1, replica_groups=mesh['dp'=4,'tensor'=4,'ctx'=2] {'ctx'}, dimensions={0}, use_global_device_ids=true | all-gather | bytes 1179648 | tf_op jit(solution)/shard_map/all_gather | solution.py:535
  22.2 4.5 %shard_map.273 = (bf16[192,512]{1,0:T(8,128)(2,1)S(1)}, f32[8,512]{1,0:T(8,128)S(1)}) custom-call(s32[7]{0:T(128)S(1)} %pad_add_fusion.meta_ref, bf16[512,192]{1,0:T(8,128)(2,1)S(1)} %get-tuple-element.171.q_ref, bf16[1024,384]{1,0:T(8,128)(2,1)S(1)} %all_gather.36.kv_ref), custom_call_target="tpu_custom_call" | custom-call | tf_op jit(solution)/shard_map/pallas_call | solution.py:58
  26.7 2.1 %collective-permute-start.5 = (bf16[192,512]{1,0:T(8,128)(2,1)S(1)}, bf16[192,512]{1,0:T(8,128)(2,1)S(1)}, u32[]{:S(2)}, u32[]{:S(2)}) collective-permute-start(bf16[192,512]{1,0:T(8,128)(2,1)S(1)} %get-tuple-element.139.m0.mix_ref), channel_id=1, source_target_pairs={{0,6},{2,4},{4,2},{6,0},{1,7},{3,5},{5,3},{7,1},{8,14},{10,12},{12... | collective-permute-start | bytes 589832 | tf_op jit(solution)/shard_map/ppermute | solution.py:468
  28.9 0.9 collective-permute-start.4
  30.3 2.3 %collective-permute-done.8.c3 = bf16[224,768]{1,0:T(8,128)(2,1)S(1)} collective-permute-done((bf16[224,768]{1,0:T(8,128)(2,1)S(1)}, bf16[224,768]{1,0:T(8,128)(2,1)S(1)}, u32[]{:S(2)}, u32[]{:S(2)}) %collective-permute-start.8) | collective-permute-done | bytes 344096 | tf_op jit(solution)/shard_map/ppermute | solution.py:468
  32.6 6.8 %collective-permute-done.7.c2 = bf16[224,768]{1,0:T(8,128)(2,1)S(1)} collective-permute-done((bf16[224,768]{1,0:T(8,128)(2,1)S(1)}, bf16[224,768]{1,0:T(8,128)(2,1)S(1)}, u32[]{:S(2)}, u32[]{:S(2)}) %collective-permute-start.7) | collective-permute-done | bytes 344096 | tf_op jit(solution)/shard_map/ppermute | solution.py:468
  39.5 2.6 %all_gather.37.wc_ref = bf16[576,768]{1,0:T(8,128)(2,1)S(1)} all-gather(bf16[288,768]{1,0:T(8,128)(2,1)S(1)} %pad_maximum_fusion), channel_id=1, replica_groups=mesh['dp'=4,'tensor'=4,'ctx'=2] {'ctx'}, dimensions={0}, use_global_device_ids=true | all-gather | bytes 1327104 | tf_op jit(solution)/shard_map/all_gather | solution.py:535
  42.4 4.4 %shard_map.275 = (bf16[512,768]{1,0:T(8,128)(2,1)S(1)}, bf16[512,768]{1,0:T(8,128)(2,1)S(1)}, bf16[512,768]{1,0:T(8,128)(2,1)S(1)}, bf16[512,768]{1,0:T(8,128)(2...) custom-call(s32[7]{0:T(128)S(1)} %pad_add_fusion.meta_ref, ...), custom_call_target="tpu_custom_call" | custom-call | tf_op jit(solution)/shard_map/pallas_call | solution.py:58
  47.1 1.7 %collective-permute-start.10 = (bf16[128,768]{1,0:T(8,128)(2,1)S(1)}, bf16[128,768]{1,0:T(8,128)(2,1)S(1)}, u32[]{:S(2)}, u32[]{:S(2)}) collective-permute-start(bf16[128,768]{1,0:T(8,128)(2,1)S(1)} %get-tuple-element.162), channel_id=1, source_target_pairs={{0,4},{2,6},{4,0},{6,2},{1,5},{3,7},{5,1},{7,3},{8,12},{10,14},{12... | collective-permute-start | bytes 589832 | tf_op jit(solution)/shard_map/ppermute | solution.py:468
  48.8 1.5 %collective-permute-start.11 = (bf16[128,768]{1,0:T(8,128)(2,1)S(1)}, bf16[128,768]{1,0:T(8,128)(2,1)S(1)}, u32[]{:S(2)}, u32[]{:S(2)}) collective-permute-start(bf16[128,768]{1,0:T(8,128)(2,1)S(1)} %get-tuple-element.163), channel_id=1, source_target_pairs={{0,6},{2,4},{4,2},{6,0},{1,7},{3,5},{5,3},{7,1},{8,14},{10,12},{12... | collective-permute-start | bytes 589832 | tf_op jit(solution)/shard_map/ppermute | solution.py:468
  50.3 1.4 %shard_map.276 = (bf16[192,768]{1,0:T(8,128)(2,1)S(1)}, bf16[192,768]{1,0:T(8,128)(2,1)S(1)}, bf16[192,768]{1,0:T(8,128)(2,1)S(1)}, bf16[192,768]{1,0:T(8,128)(2,1)S(1)}) custom-call(s32[7]{0:T(128)S(1)} %pad_add_fusion.meta_ref, bf16[512,768]{1,0:T(8,128)(2,1)S(1)} %get-tuple-element.169.a_ref.active_ref, bf16[512,768]{1,0:T(8,128)(2,1)S(1)} %get-tuple-element.149.b_ref), custom_call_target="tpu_custom_call" | custom-call | tf_op jit(solution)/shard_map/pallas_call | solution.py:58
  51.8 2.2 %all_gather.38.pair_ref = bf16[384,768]{1,0:T(8,128)(2,1)S(1)} all-gather(bf16[192,768]{1,0:T(8,128)(2,1)S(1)} %get-tuple-element.154), channel_id=1, replica_groups=mesh['dp'=4,'tensor'=4,'ctx'=2] {'ctx'}, dimensions={0}, use_global_device_ids=true | all-gather | bytes 884736 | tf_op jit(solution)/shard_map/all_gather | solution.py:535
  54.6 1.7 %collective-permute-start.12 = (bf16[192,768]{1,0:T(8,128)(2,1)S(1)}, bf16[192,768]{1,0:T(8,128)(2,1)S(1)}, u32[]{:S(2)}, u32[]{:S(2)}) collective-permute-start(bf16[192,768]{1,0:T(8,128)(2,1)S(1)} %shard_map.277), channel_id=1, source_target_pairs={{0,8},{8,0},{16,24},{24,16},{1,9},{9,1},{17,25},{25,17},{2,10},{10... | collective-permute-start | bytes 884744 | tf_op jit(solution)/shard_map/ppermute | solution.py:562
  56.3 1.4 %shard_map.278 = (bf16[192,768]{1,0:T(8,128)(2,1)S(1)}, bf16[192,768]{1,0:T(8,128)(2,1)S(1)}, bf16[192,768]{1,0:T(8,128)(2,1)S(1)}, bf16[192,768]{1,0:T(8,128)(2,1)S(1)}) custom-call(s32[7]{0:T(128)S(1)} %pad_add_fusion.meta_ref, bf16[512,768]{1,0:T(8,128)(2,1)S(1)} %get-tuple-element.148.a_ref, bf16[512,768]{1,0:T(8,128)(2,1)S(1)} %get-tuple-element.155.b_ref), custom_call_target="tpu_custom_call" | custom-call | tf_op jit(solution)/shard_map/pallas_call | solution.py:58
  58.3 1.5 %collective-permute-start.16 = (bf16[128,768]{1,0:T(8,128)(2,1)S(1)}, bf16[128,768]{1,0:T(8,128)(2,1)S(1)}, u32[]{:S(2)}, u32[]{:S(2)}) collective-permute-start(bf16[128,768]{1,0:T(8,128)(2,1)S(1)} %get-tuple-element.173.b0), channel_id=1, source_target_pairs={{0,6},{2,4},{4,2},{6,0},{1,7},{3,5},{5,3},{7,1},{8,14},{10,12},{12... | collective-permute-start | bytes 589832 | tf_op jit(solution)/shard_map/ppermute | solution.py:468
  59.8 1.7 %collective-permute-start.15 = (bf16[128,768]{1,0:T(8,128)(2,1)S(1)}, bf16[128,768]{1,0:T(8,128)(2,1)S(1)}, u32[]{:S(2)}, u32[]{:S(2)}) collective-permute-start(bf16[128,768]{1,0:T(8,128)(2,1)S(1)} %get-tuple-element.173.b0), channel_id=1, source_target_pairs={{0,4},{2,6},{4,0},{6,2},{1,5},{3,7},{5,1},{7,3},{8,12},{10,14},{12... | collective-permute-start | bytes 589832 | tf_op jit(solution)/shard_map/ppermute | solution.py:468
  61.9 2.2 %all_gather.39.pair_ref = bf16[384,768]{1,0:T(8,128)(2,1)S(1)} all-gather(bf16[192,768]{1,0:T(8,128)(2,1)S(1)} %get-tuple-element.166), channel_id=1, replica_groups=mesh['dp'=4,'tensor'=4,'ctx'=2] {'ctx'}, dimensions={0}, use_global_device_ids=true | all-gather | bytes 884736 | tf_op jit(solution)/shard_map/all_gather | solution.py:535
  65.0 1.6 %collective-permute-start.17 = (bf16[192,768]{1,0:T(8,128)(2,1)S(1)}, bf16[192,768]{1,0:T(8,128)(2,1)S(1)}, u32[]{:S(2)}, u32[]{:S(2)}) collective-permute-start(bf16[192,768]{1,0:T(8,128)(2,1)S(1)} %shard_map.280), channel_id=1, source_target_pairs={{0,8},{8,0},{16,24},{24,16},{1,9},{9,1},{17,25},{25,17},{2,10},{10... | collective-permute-start | bytes 884744 | tf_op jit(solution)/shard_map/ppermute | solution.py:562
  67.1 2.6 %collective-permute-start.19 = (bf16[192,768]{1,0:T(8,128)(2,1)S(1)}, bf16[192,768]{1,0:T(8,128)(2,1)S(1)}, u32[]{:S(2)}, u32[]{:S(2)}) collective-permute-start(bf16[192,768]{1,0:T(8,128)(2,1)S(1)} %shard_map.281.refs_0_), channel_id=1, source_target_pairs={{0,16},{8,24},{16,0},{24,8},{1,17},{9,25},{17,1},{25,9},{2,18},{10... | collective-permute-start | bytes 884744 | tf_op jit(solution)/shard_map/ppermute | solution.py:580
  69.7 1.4 shard_map.282
  71.1 5.7 %shard_map.283 = (bf16[192,512]{1,0:T(8,128)(2,1)S(1)}, f32[512,384]{1,0:T(8,128)S(1)}, bf16[512,384]{1,0:T(8,128)(2,1)S(1)}, bf16[512,768]{1,0:T(8,128)(2,1)S(1)}) custom-call(s32[7]{0:T(128)S(1)} %pad_add_fusion.meta_ref, bf16[512,192]{1,0:T(8,128)(2,1)S(1)} %get-tuple-element.171.q_ref, bf16[1024,384]{1,0:T(8,128)(2,1)S(1)} %all_gather.36.kv_ref, ...), custom_call_target="tpu_custom_call" | custom-call | tf_op jit(solution)/shard_map/pallas_call | solution.py:58
  76.8 3.8 %all_gather.40.got_kv = bf16[1024,384]{1,0:T(8,128)(2,1)S(1)} all-gather(bf16[512,384]{1,0:T(8,128)(2,1)S(1)} %get-tuple-element.176), channel_id=1, replica_groups=mesh['dp'=4,'tensor'=4,'ctx'=2] {'ctx'}, dimensions={0}, use_global_device_ids=true | all-gather | bytes 1179648 | tf_op jit(solution)/shard_map/all_gather | solution.py:535
  80.7 2.3 %collective-permute-done.19.refs_1_ = bf16[192,768]{1,0:T(8,128)(2,1)S(1)} collective-permute-done((bf16[192,768]{1,0:T(8,128)(2,1)S(1)}, bf16[192,768]{1,0:T(8,128)(2,1)S(1)}, u32[]{:S(2)}, u32[]{:S(2)}) %collective-permute-start.19) | collective-permute-done | bytes 294944 | tf_op jit(solution)/shard_map/ppermute | solution.py:580
  83.1 2.0 %shard_map.286 = (bf16[96,768]{1,0:T(8,128)(2,1)S(1)}, bf16[96,768]{1,0:T(8,128)(2,1)S(1)}, bf16[192,768]{1,0:T(8,128)(2,1)S(1)}, f32[128,768]{1,0:T(8,128)S(1)}...) custom-call(s32[7]{0:T(128)S(1)} %pad_add_fusion.meta_ref, ...), custom_call_target="tpu_custom_call" | custom-call | tf_op jit(solution)/shard_map/pallas_call | solution.py:58
  85.0 1.7 %collective-permute-start.20 = (bf16[272,768]{1,0:T(8,128)(2,1)S(1)}, bf16[272,768]{1,0:T(8,128)(2,1)S(1)}, u32[]{:S(2)}, u32[]{:S(2)}) collective-permute-start(bf16[272,768]{1,0:T(8,128)(2,1)S(1)} %get-tuple-element.201), channel_id=1, source_target_pairs={{0,2},{2,0},{4,6},{6,4},{1,3},{3,1},{5,7},{7,5},{8,10},{10,8},{12,... | collective-permute-start | bytes 1253384 | tf_op jit(solution)/shard_map/ppermute | solution.py:793
  86.9 2.2 %all_gather.41.pair_ref = bf16[384,768]{1,0:T(8,128)(2,1)S(1)} all-gather(bf16[192,768]{1,0:T(8,128)(2,1)S(1)} %get-tuple-element.187), channel_id=1, replica_groups=mesh['dp'=4,'tensor'=4,'ctx'=2] {'ctx'}, dimensions={0}, use_global_device_ids=true | all-gather | bytes 884736 | tf_op jit(solution)/shard_map/all_gather | solution.py:535
  89.8 1.1 shard_map.288
  90.9 2.2 %all_gather.42.pair_ref = bf16[384,768]{1,0:T(8,128)(2,1)S(1)} all-gather(bf16[192,768]{1,0:T(8,128)(2,1)S(1)} %get-tuple-element.194), channel_id=1, replica_groups=mesh['dp'=4,'tensor'=4,'ctx'=2] {'ctx'}, dimensions={0}, use_global_device_ids=true | all-gather | bytes 884736 | tf_op jit(solution)/shard_map/all_gather | solution.py:535
  93.7 1.0 collective-permute-done.20.got.g1
  94.8 1.6 %collective-permute-start.23 = (bf16[144,768]{1,0:T(8,128)(2,1)S(1)}, bf16[144,768]{1,0:T(8,128)(2,1)S(1)}, u32[]{:S(2)}, u32[]{:S(2)}) collective-permute-start(bf16[144,768]{1,0:T(8,128)(2,1)S(1)} %get-tuple-element.203), channel_id=1, source_target_pairs={{0,4},{2,6},{4,0},{6,2},{1,5},{3,7},{5,1},{7,3},{8,12},{10,14},{12... | collective-permute-start | bytes 663560 | tf_op jit(solution)/shard_map/ppermute | solution.py:812
  96.4 1.8 %collective-permute-start.21 = (bf16[96,768]{1,0:T(8,128)(2,1)S(1)}, bf16[96,768]{1,0:T(8,128)(2,1)S(1)}, u32[]{:S(2)}, u32[]{:S(2)}) collective-permute-start(bf16[96,768]{1,0:T(8,128)(2,1)S(1)} %get-tuple-element.188), channel_id=1, source_target_pairs={{0,8},{8,0},{16,24},{24,16},{1,9},{9,1},{17,25},{25,17},{2,10},{10... | collective-permute-start | bytes 442376 | tf_op jit(solution)/shard_map/ppermute | solution.py:554
  98.4 5.4 %collective-permute-done.21.refs_1_ = bf16[96,768]{1,0:T(8,128)(2,1)S(1)} collective-permute-done((bf16[96,768]{1,0:T(8,128)(2,1)S(1)}, bf16[96,768]{1,0:T(8,128)(2,1)S(1)}, u32[]{:S(2)}, u32[]{:S(2)}) %collective-permute-start.21) | collective-permute-done | bytes 147488 | tf_op jit(solution)/shard_map/ppermute | solution.py:554
  104.0 1.1 shard_map.293
  105.5 1.7 %collective-permute-start.28 = (bf16[96,768]{1,0:T(8,128)(2,1)S(1)}, bf16[96,768]{1,0:T(8,128)(2,1)S(1)}, u32[]{:S(2)}, u32[]{:S(2)}) collective-permute-start(bf16[96,768]{1,0:T(8,128)(2,1)S(1)} %shard_map.291.refs_0_), channel_id=1, source_target_pairs={{0,16},{8,24},{16,0},{24,8},{1,17},{9,25},{17,1},{25,9},{2,18},{10... | collective-permute-start | bytes 442376 | tf_op jit(solution)/shard_map/ppermute | solution.py:580
  107.3 1.3 collective-permute-start.29
  108.6 1.1 collective-permute-start.26
  109.7 0.9 collective-permute-start.25
  110.6 2.2 %all_gather.43.refs_2_ = bf16[384,768]{1,0:T(8,128)(2,1)S(1)} all-gather(bf16[192,768]{1,0:T(8,128)(2,1)S(1)} %shard_map.285.refs_0_), channel_id=1, replica_groups=mesh['dp'=4,'tensor'=4,'ctx'=2] {'ctx'}, dimensions={0}, use_global_device_ids=true | all-gather | bytes 884736 | tf_op jit(solution)/shard_map/all_gather | solution.py:535
  112.8 2.2 %all_gather.44.refs_2_ = bf16[384,768]{1,0:T(8,128)(2,1)S(1)} all-gather(bf16[192,768]{1,0:T(8,128)(2,1)S(1)} %shard_map.292.refs_0_), channel_id=1, replica_groups=mesh['dp'=4,'tensor'=4,'ctx'=2] {'ctx'}, dimensions={0}, use_global_device_ids=true | all-gather | bytes 884736 | tf_op jit(solution)/shard_map/all_gather | solution.py:535
  115.0 0.9 collective-permute-done.27.got.g1
  116.0 8.9 %collective-permute-done.26.refs_1_ = bf16[192,768]{1,0:T(8,128)(2,1)S(1)} collective-permute-done((bf16[192,768]{1,0:T(8,128)(2,1)S(1)}, bf16[192,768]{1,0:T(8,128)(2,1)S(1)}, u32[]{:S(2)}, u32[]{:S(2)}) %collective-permute-start.26) | collective-permute-done | bytes 294944 | tf_op jit(solution)/shard_map/ppermute | solution.py:592
  124.9 2.2 %all_gather.45.refs_3_ = bf16[384,768]{1,0:T(8,128)(2,1)S(1)} all-gather(bf16[192,768]{1,0:T(8,128)(2,1)S(1)} %collective-permute-done.26.refs_1_), channel_id=1, replica_groups=mesh['dp'=4,'tensor'=4,'ctx'=2] {'ctx'}, dimensions={0}, use_global_device_ids=true | all-gather | bytes 884736 | tf_op jit(solution)/shard_map/all_gather | solution.py:535
  127.1 2.1 %shard_map.296 = f32[768,768]{1,0:T(8,128)} custom-call(s32[7]{0:T(128)S(1)} %pad_add_fusion.meta_ref, bf16[192,768]{1,0:T(8,128)(2,1)S(1)} %shard_map.285.refs_0_, bf16[192,768]{1,0:T(8,128)(2,1)S(1)} %collective-permute-done.26.refs_1_, bf16[384,768]{1,0:T(8,128)(2,1)S(1)} %all_gather.43.refs_2_, bf16[384,768]{1,0:T(8,128)(2,1)S(1)} %all_gather.45.refs_3_), custom_call_target="tpu_custom_call" | custom-call | tf_op jit(solution)/shard_map/pallas_call | solution.py:58
  129.7 1.6 %collective-permute-start.33 = (bf16[128,768]{1,0:T(8,128)(2,1)S(1)}, bf16[128,768]{1,0:T(8,128)(2,1)S(1)}, u32[]{:S(2)}, u32[]{:S(2)}) collective-permute-start(bf16[128,768]{1,0:T(8,128)(2,1)S(1)} %shard_map.295), channel_id=1, source_target_pairs={{0,4},{2,6},{4,0},{6,2},{1,5},{3,7},{5,1},{7,3},{8,12},{10,14},{12... | collective-permute-start | bytes 589832 | tf_op jit(solution)/shard_map/ppermute | solution.py:831
  131.4 1.9 %collective-permute-start.31 = (bf16[96,768]{1,0:T(8,128)(2,1)S(1)}, bf16[96,768]{1,0:T(8,128)(2,1)S(1)}, u32[]{:S(2)}, u32[]{:S(2)}) collective-permute-start(bf16[96,768]{1,0:T(8,128)(2,1)S(1)} %shard_map.297.refs_4_), channel_id=1, source_target_pairs={{0,8},{8,0},{16,24},{24,16},{1,9},{9,1},{17,25},{25,17},{2,10},{10... | collective-permute-start | bytes 442376 | tf_op jit(solution)/shard_map/ppermute | solution.py:592
  133.3 2.0 %all_gather.46.refs_6_ = bf16[192,768]{1,0:T(8,128)(2,1)S(1)} all-gather(bf16[96,768]{1,0:T(8,128)(2,1)S(1)} %shard_map.297.refs_4_), channel_id=1, replica_groups=mesh['dp'=4,'tensor'=4,'ctx'=2] {'ctx'}, dimensions={0}, use_global_device_ids=true | all-gather | bytes 442368 | tf_op jit(solution)/shard_map/all_gather | solution.py:535
  135.4 2.0 %all_gather.47.refs_2_ = bf16[224,768]{1,0:T(8,128)(2,1)S(1)} all-gather(bf16[112,768]{1,0:T(8,128)(2,1)S(1)} %shard_map.298.refs_0_), channel_id=1, replica_groups=mesh['dp'=4,'tensor'=4,'ctx'=2] {'ctx'}, dimensions={0}, use_global_device_ids=true | all-gather | bytes 516096 | tf_op jit(solution)/shard_map/all_gather | solution.py:535
  137.4 2.1 %shard_map.299 = f32[768,768]{1,0:T(8,128)} custom-call(s32[7]{0:T(128)S(1)} %pad_add_fusion.meta_ref, bf16[192,768]{1,0:T(8,128)(2,1)S(1)} %shard_map.292.refs_0_, bf16[192,768]{1,0:T(8,128)(2,1)S(1)} %collective-permute-done.25.refs_1_, bf16[384,768]{1,0:T(8,128)(2,1)S(1)} %all_gather.44.refs_2_, bf16[192,768]{1,0:T(8,128)(2,1)S(1)} %collective-permute-done.32.refs_3_), custom_call_target="tpu_custom_call" | custom-call | tf_op jit(solution)/shard_map/pallas_call | solution.py:58
  140.2 0.8 shard_map.300
  141.3 2.1 %shard_map.301 = (f32[576,768]{1,0:T(8,128)}, f32[192,768]{1,0:T(8,128)}, f32[768]{0:T(1024)}, f32[768]{0:T(1024)}, f32[768]{0:T(1024)}, /*index=5*/f32[768]{0:T...) custom-call(s32[7]{0:T(128)S(1)} %pad_add_fusion.meta_ref, ...), custom_call_target="tpu_custom_call" | custom-call | tf_op jit(solution)/shard_map/pallas_call | solution.py:58
  (90 shorter events, 10.3 us)
Async XLA Ops:
  0.6 12.7 %collective-permute-start.2 = (bf16[128,768]{1,0:T(8,128)(2,1)}, bf16[128,768]{1,0:T(8,128)(2,1)S(1)}, u32[]{:S(2)}, u32[]{:S(2)}) collective-permute-start(bf16[128,768]{1,0:T(8,128)(2,1)} %bitcast.18), channel_id=1, source_target_pairs={{0,6},{2,4},{4,2},{6,0},{1,7},{3,5},{5,3},{7,1},{8,14},{10,12},{12... | collective-permute-start | bytes 589832 | tf_op jit(solution)/shard_map/ppermute | solution.py:468
  4.6 9.3 %collective-permute-start.1 = (bf16[128,768]{1,0:T(8,128)(2,1)}, bf16[128,768]{1,0:T(8,128)(2,1)S(1)}, u32[]{:S(2)}, u32[]{:S(2)}) collective-permute-start(bf16[128,768]{1,0:T(8,128)(2,1)} %bitcast.19), channel_id=1, source_target_pairs={{0,4},{2,6},{4,0},{6,2},{1,5},{3,7},{5,1},{7,3},{8,12},{10,14},{12... | collective-permute-start | bytes 589832 | tf_op jit(solution)/shard_map/ppermute | solution.py:468
  5.1 9.1 %collective-permute-start = (bf16[128,768]{1,0:T(8,128)(2,1)}, bf16[128,768]{1,0:T(8,128)(2,1)S(1)}, u32[]{:S(2)}, u32[]{:S(2)}) collective-permute-start(bf16[128,768]{1,0:T(8,128)(2,1)} %bitcast.20), channel_id=1, source_target_pairs={{0,2},{2,0},{4,6},{6,4},{1,3},{3,1},{5,7},{7,5},{8,10},{10,8},{12,... | collective-permute-start | bytes 589832 | tf_op jit(solution)/shard_map/ppermute | solution.py:468
  6.0 1.0 copy-start.1
  6.9 0.9 copy-start.3
  7.9 1.2 copy-start.6
  9.0 0.9 copy-start.7
  10.0 0.7 copy-start.8
  10.7 0.7 copy-start.9
  11.3 0.7 copy-start.15
  12.0 0.7 copy-start.16
  14.2 15.5 %collective-permute-start.6 = (bf16[224,768]{1,0:T(8,128)(2,1)S(1)}, bf16[224,768]{1,0:T(8,128)(2,1)S(1)}, u32[]{:S(2)}, u32[]{:S(2)}) collective-permute-start(bf16[224,768]{1,0:T(8,128)(2,1)S(1)} %get-tuple-element.141), channel_id=1, source_target_pairs={{0,2},{2,0},{4,6},{6,4},{1,3},{3,1},{5,7},{7,5},{8,10},{10,8},{12,... | collective-permute-start | bytes 1032200 | tf_op jit(solution)/shard_map/ppermute | solution.py:468
  15.7 16.9 %collective-permute-start.8 = (bf16[224,768]{1,0:T(8,128)(2,1)S(1)}, bf16[224,768]{1,0:T(8,128)(2,1)S(1)}, u32[]{:S(2)}, u32[]{:S(2)}) collective-permute-start(bf16[224,768]{1,0:T(8,128)(2,1)S(1)} %get-tuple-element.141), channel_id=1, source_target_pairs={{0,6},{2,4},{4,2},{6,0},{1,7},{3,5},{5,3},{7,1},{8,14},{10,12},{12... | collective-permute-start | bytes 1032200 | tf_op jit(solution)/shard_map/ppermute | solution.py:468
  17.1 22.3 %collective-permute-start.7 = (bf16[224,768]{1,0:T(8,128)(2,1)S(1)}, bf16[224,768]{1,0:T(8,128)(2,1)S(1)}, u32[]{:S(2)}, u32[]{:S(2)}) collective-permute-start(bf16[224,768]{1,0:T(8,128)(2,1)S(1)} %get-tuple-element.141), channel_id=1, source_target_pairs={{0,4},{2,6},{4,0},{6,2},{1,5},{3,7},{5,1},{7,3},{8,12},{10,14},{12... | collective-permute-start | bytes 1032200 | tf_op jit(solution)/shard_map/ppermute | solution.py:468
  26.6 15.5 %copy-start.10 = (f32[768]{0:T(1024)S(1)}, f32[768]{0:T(1024)}, u32[]{:S(2)}) copy-start(f32[768]{0:T(1024)} %refs_0_.3) | copy-start | bytes 9220
  26.6 15.5 %copy-start.11 = (f32[768]{0:T(1024)S(1)}, f32[768]{0:T(1024)}, u32[]{:S(2)}) copy-start(f32[768]{0:T(1024)} %refs_1_.3) | copy-start | bytes 9220
  26.6 15.5 %copy-start.12 = (f32[768]{0:T(1024)S(1)}, f32[768]{0:T(1024)}, u32[]{:S(2)}) copy-start(f32[768]{0:T(1024)} %refs_2_.3) | copy-start | bytes 9220
  26.7 15.4 %copy-start.13 = (f32[768]{0:T(1024)S(1)}, f32[768]{0:T(1024)}, u32[]{:S(2)}) copy-start(f32[768]{0:T(1024)} %refs_3_.3) | copy-start | bytes 9220
  26.7 15.4 %copy-start.14 = (f32[768]{0:T(1024)S(1)}, f32[768]{0:T(1024)}, u32[]{:S(2)}) copy-start(f32[768]{0:T(1024)} %refs_4_) | copy-start | bytes 9220
  26.7 15.7 %copy-start = (bf16[768,768]{1,0:T(8,128)(2,1)S(1)}, bf16[768,768]{1,0:T(8,128)(2,1)}, u32[]{:S(2)}) copy-start(bf16[768,768]{1,0:T(8,128)(2,1)} %down_ref.3) | copy-start | bytes 3538948
  26.7 15.6 %copy-start.2 = (bf16[192,768]{1,0:T(8,128)(2,1)S(1)}, bf16[192,768]{1,0:T(8,128)(2,1)}, u32[]{:S(2)}) copy-start(bf16[192,768]{1,0:T(8,128)(2,1)} %w_ref.3) | copy-start | bytes 884740
  26.7 15.6 %copy-start.4 = (bf16[1,128,768]{2,1,0:T(8,128)(2,1)S(1)}, bf16[1,128,768]{2,1,0:T(8,128)(2,1)}, u32[]{:S(2)}) copy-start(bf16[1,128,768]{2,1,0:T(8,128)(2,1)} %param.31) | copy-start | bytes 589828
  26.7 15.6 %copy-start.5 = (bf16[768,768]{1,0:T(8,128)(2,1)S(1)}, bf16[768,768]{1,0:T(8,128)(2,1)}, u32[]{:S(2)}) copy-start(bf16[768,768]{1,0:T(8,128)(2,1)} %up_ref.1) | copy-start | bytes 3538948
  26.7 15.4 %collective-permute-start.5 = (bf16[192,512]{1,0:T(8,128)(2,1)S(1)}, bf16[192,512]{1,0:T(8,128)(2,1)S(1)}, u32[]{:S(2)}, u32[]{:S(2)}) collective-permute-start(bf16[192,512]{1,0:T(8,128)(2,1)S(1)} %get-tuple-element.139.m0.mix_ref), channel_id=1, source_target_pairs={{0,6},{2,4},{4,2},{6,0},{1,7},{3,5},{5,3},{7,1},{8,14},{10,12},{12... | collective-permute-start | bytes 589832 | tf_op jit(solution)/shard_map/ppermute | solution.py:468
  28.9 13.5 %collective-permute-start.4 = (bf16[192,512]{1,0:T(8,128)(2,1)S(1)}, bf16[192,512]{1,0:T(8,128)(2,1)S(1)}, u32[]{:S(2)}, u32[]{:S(2)}) collective-permute-start(bf16[192,512]{1,0:T(8,128)(2,1)S(1)} %get-tuple-element.139.m0.mix_ref), channel_id=1, source_target_pairs={{0,4},{2,6},{4,0},{6,2},{1,5},{3,7},{5,1},{7,3},{8,12},{10,14},{12... | collective-permute-start | bytes 589832 | tf_op jit(solution)/shard_map/ppermute | solution.py:468
  29.8 12.6 %collective-permute-start.3 = (bf16[192,512]{1,0:T(8,128)(2,1)S(1)}, bf16[192,512]{1,0:T(8,128)(2,1)S(1)}, u32[]{:S(2)}, u32[]{:S(2)}) collective-permute-start(bf16[192,512]{1,0:T(8,128)(2,1)S(1)} %get-tuple-element.139.m0.mix_ref), channel_id=1, source_target_pairs={{0,2},{2,0},{4,6},{6,4},{1,3},{3,1},{5,7},{7,5},{8,10},{10,8},{12,... | collective-permute-start | bytes 589832 | tf_op jit(solution)/shard_map/ppermute | solution.py:468
  46.8 11.0 %collective-permute-start.9 = (bf16[128,768]{1,0:T(8,128)(2,1)S(1)}, bf16[128,768]{1,0:T(8,128)(2,1)S(1)}, u32[]{:S(2)}, u32[]{:S(2)}) collective-permute-start(bf16[128,768]{1,0:T(8,128)(2,1)S(1)} %get-tuple-element.161), channel_id=1, source_target_pairs={{0,2},{2,0},{4,6},{6,4},{1,3},{3,1},{5,7},{7,5},{8,10},{10,8},{12,... | collective-permute-start | bytes 589832 | tf_op jit(solution)/shard_map/ppermute | solution.py:468
  47.1 10.8 %collective-permute-start.10 = (bf16[128,768]{1,0:T(8,128)(2,1)S(1)}, bf16[128,768]{1,0:T(8,128)(2,1)S(1)}, u32[]{:S(2)}, u32[]{:S(2)}) collective-permute-start(bf16[128,768]{1,0:T(8,128)(2,1)S(1)} %get-tuple-element.162), channel_id=1, source_target_pairs={{0,4},{2,6},{4,0},{6,2},{1,5},{3,7},{5,1},{7,3},{8,12},{10,14},{12... | collective-permute-start | bytes 589832 | tf_op jit(solution)/shard_map/ppermute | solution.py:468
  48.8 9.1 %collective-permute-start.11 = (bf16[128,768]{1,0:T(8,128)(2,1)S(1)}, bf16[128,768]{1,0:T(8,128)(2,1)S(1)}, u32[]{:S(2)}, u32[]{:S(2)}) collective-permute-start(bf16[128,768]{1,0:T(8,128)(2,1)S(1)} %get-tuple-element.163), channel_id=1, source_target_pairs={{0,6},{2,4},{4,2},{6,0},{1,7},{3,5},{5,3},{7,1},{8,14},{10,12},{12... | collective-permute-start | bytes 589832 | tf_op jit(solution)/shard_map/ppermute | solution.py:468
  54.6 10.1 %collective-permute-start.12 = (bf16[192,768]{1,0:T(8,128)(2,1)S(1)}, bf16[192,768]{1,0:T(8,128)(2,1)S(1)}, u32[]{:S(2)}, u32[]{:S(2)}) collective-permute-start(bf16[192,768]{1,0:T(8,128)(2,1)S(1)} %shard_map.277), channel_id=1, source_target_pairs={{0,8},{8,0},{16,24},{24,16},{1,9},{9,1},{17,25},{25,17},{2,10},{10... | collective-permute-start | bytes 884744 | tf_op jit(solution)/shard_map/ppermute | solution.py:562
  56.3 8.7 %collective-permute-start.13 = (bf16[192,768]{1,0:T(8,128)(2,1)S(1)}, bf16[192,768]{1,0:T(8,128)(2,1)S(1)}, u32[]{:S(2)}, u32[]{:S(2)}) collective-permute-start(bf16[192,768]{1,0:T(8,128)(2,1)S(1)} %get-tuple-element.168), channel_id=1, source_target_pairs={{0,1},{1,0},{2,3},{3,2},{4,5},{5,4},{6,7},{7,6},{8,9},{9,8},{10,11... | collective-permute-start | bytes 884744 | tf_op jit(solution)/shard_map/ppermute | solution.py:564
  58.3 8.7 %collective-permute-start.16 = (bf16[128,768]{1,0:T(8,128)(2,1)S(1)}, bf16[128,768]{1,0:T(8,128)(2,1)S(1)}, u32[]{:S(2)}, u32[]{:S(2)}) collective-permute-start(bf16[128,768]{1,0:T(8,128)(2,1)S(1)} %get-tuple-element.173.b0), channel_id=1, source_target_pairs={{0,6},{2,4},{4,2},{6,0},{1,7},{3,5},{5,3},{7,1},{8,14},{10,12},{12... | collective-permute-start | bytes 589832 | tf_op jit(solution)/shard_map/ppermute | solution.py:468
  59.8 11.2 %collective-permute-start.15 = (bf16[128,768]{1,0:T(8,128)(2,1)S(1)}, bf16[128,768]{1,0:T(8,128)(2,1)S(1)}, u32[]{:S(2)}, u32[]{:S(2)}) collective-permute-start(bf16[128,768]{1,0:T(8,128)(2,1)S(1)} %get-tuple-element.173.b0), channel_id=1, source_target_pairs={{0,4},{2,6},{4,0},{6,2},{1,5},{3,7},{5,1},{7,3},{8,12},{10,14},{12... | collective-permute-start | bytes 589832 | tf_op jit(solution)/shard_map/ppermute | solution.py:468
  61.5 9.5 %collective-permute-start.14 = (bf16[128,768]{1,0:T(8,128)(2,1)S(1)}, bf16[128,768]{1,0:T(8,128)(2,1)S(1)}, u32[]{:S(2)}, u32[]{:S(2)}) collective-permute-start(bf16[128,768]{1,0:T(8,128)(2,1)S(1)} %get-tuple-element.173.b0), channel_id=1, source_target_pairs={{0,2},{2,0},{4,6},{6,4},{1,3},{3,1},{5,7},{7,5},{8,10},{10,8},{12,... | collective-permute-start | bytes 589832 | tf_op jit(solution)/shard_map/ppermute | solution.py:468
  64.8 15.8 %collective-permute-start.18 = (bf16[192,768]{1,0:T(8,128)(2,1)S(1)}, bf16[192,768]{1,0:T(8,128)(2,1)S(1)}, u32[]{:S(2)}, u32[]{:S(2)}) collective-permute-start(bf16[192,768]{1,0:T(8,128)(2,1)S(1)} %get-tuple-element.178), channel_id=1, source_target_pairs={{0,1},{1,0},{2,3},{3,2},{4,5},{5,4},{6,7},{7,6},{8,9},{9,8},{10,11... | collective-permute-start | bytes 884744 | tf_op jit(solution)/shard_map/ppermute | solution.py:564
  65.0 15.6 %collective-permute-start.17 = (bf16[192,768]{1,0:T(8,128)(2,1)S(1)}, bf16[192,768]{1,0:T(8,128)(2,1)S(1)}, u32[]{:S(2)}, u32[]{:S(2)}) collective-permute-start(bf16[192,768]{1,0:T(8,128)(2,1)S(1)} %shard_map.280), channel_id=1, source_target_pairs={{0,8},{8,0},{16,24},{24,16},{1,9},{9,1},{17,25},{25,17},{2,10},{10... | collective-permute-start | bytes 884744 | tf_op jit(solution)/shard_map/ppermute | solution.py:562
  67.1 15.9 %collective-permute-start.19 = (bf16[192,768]{1,0:T(8,128)(2,1)S(1)}, bf16[192,768]{1,0:T(8,128)(2,1)S(1)}, u32[]{:S(2)}, u32[]{:S(2)}) collective-permute-start(bf16[192,768]{1,0:T(8,128)(2,1)S(1)} %shard_map.281.refs_0_), channel_id=1, source_target_pairs={{0,16},{8,24},{16,0},{24,8},{1,17},{9,25},{17,1},{25,9},{2,18},{10... | collective-permute-start | bytes 884744 | tf_op jit(solution)/shard_map/ppermute | solution.py:580
  85.0 9.7 %collective-permute-start.20 = (bf16[272,768]{1,0:T(8,128)(2,1)S(1)}, bf16[272,768]{1,0:T(8,128)(2,1)S(1)}, u32[]{:S(2)}, u32[]{:S(2)}) collective-permute-start(bf16[272,768]{1,0:T(8,128)(2,1)S(1)} %get-tuple-element.201), channel_id=1, source_target_pairs={{0,2},{2,0},{4,6},{6,4},{1,3},{3,1},{5,7},{7,5},{8,10},{10,8},{12,... | collective-permute-start | bytes 1253384 | tf_op jit(solution)/shard_map/ppermute | solution.py:793
  86.8 17.1 %collective-permute-start.22 = (bf16[192,768]{1,0:T(8,128)(2,1)S(1)}, bf16[192,768]{1,0:T(8,128)(2,1)S(1)}, u32[]{:S(2)}, u32[]{:S(2)}) collective-permute-start(bf16[192,768]{1,0:T(8,128)(2,1)S(1)} %shard_map.284.refs_0_), channel_id=1, source_target_pairs={{0,16},{8,24},{16,0},{24,8},{1,17},{9,25},{17,1},{25,9},{2,18},{10... | collective-permute-start | bytes 884744 | tf_op jit(solution)/shard_map/ppermute | solution.py:580
  94.8 9.2 %collective-permute-start.23 = (bf16[144,768]{1,0:T(8,128)(2,1)S(1)}, bf16[144,768]{1,0:T(8,128)(2,1)S(1)}, u32[]{:S(2)}, u32[]{:S(2)}) collective-permute-start(bf16[144,768]{1,0:T(8,128)(2,1)S(1)} %get-tuple-element.203), channel_id=1, source_target_pairs={{0,4},{2,6},{4,0},{6,2},{1,5},{3,7},{5,1},{7,3},{8,12},{10,14},{12... | collective-permute-start | bytes 663560 | tf_op jit(solution)/shard_map/ppermute | solution.py:812
  96.4 7.5 %collective-permute-start.21 = (bf16[96,768]{1,0:T(8,128)(2,1)S(1)}, bf16[96,768]{1,0:T(8,128)(2,1)S(1)}, u32[]{:S(2)}, u32[]{:S(2)}) collective-permute-start(bf16[96,768]{1,0:T(8,128)(2,1)S(1)} %get-tuple-element.188), channel_id=1, source_target_pairs={{0,8},{8,0},{16,24},{24,16},{1,9},{9,1},{17,25},{25,17},{2,10},{10... | collective-permute-start | bytes 442376 | tf_op jit(solution)/shard_map/ppermute | solution.py:554
  98.2 9.1 %collective-permute-start.24 = (bf16[96,768]{1,0:T(8,128)(2,1)S(1)}, bf16[96,768]{1,0:T(8,128)(2,1)S(1)}, u32[]{:S(2)}, u32[]{:S(2)}) collective-permute-start(bf16[96,768]{1,0:T(8,128)(2,1)S(1)} %get-tuple-element.199), channel_id=1, source_target_pairs={{0,8},{8,0},{16,24},{24,16},{1,9},{9,1},{17,25},{25,17},{2,10},{10... | collective-permute-start | bytes 442376 | tf_op jit(solution)/shard_map/ppermute | solution.py:554
  105.0 10.9 %collective-permute-start.27 = (bf16[256,768]{1,0:T(8,128)(2,1)S(1)}, bf16[256,768]{1,0:T(8,128)(2,1)S(1)}, u32[]{:S(2)}, u32[]{:S(2)}) collective-permute-start(bf16[256,768]{1,0:T(8,128)(2,1)S(1)} %get-tuple-element.223), channel_id=1, source_target_pairs={{0,2},{2,0},{4,6},{6,4},{1,3},{3,1},{5,7},{7,5},{8,10},{10,8},{12,... | collective-permute-start | bytes 1179656 | tf_op jit(solution)/shard_map/ppermute | solution.py:827
  105.5 24.0 %collective-permute-start.28 = (bf16[96,768]{1,0:T(8,128)(2,1)S(1)}, bf16[96,768]{1,0:T(8,128)(2,1)S(1)}, u32[]{:S(2)}, u32[]{:S(2)}) collective-permute-start(bf16[96,768]{1,0:T(8,128)(2,1)S(1)} %shard_map.291.refs_0_), channel_id=1, source_target_pairs={{0,16},{8,24},{16,0},{24,8},{1,17},{9,25},{17,1},{25,9},{2,18},{10... | collective-permute-start | bytes 442376 | tf_op jit(solution)/shard_map/ppermute | solution.py:580
  107.3 22.3 %collective-permute-start.29 = (bf16[112,768]{1,0:T(8,128)(2,1)S(1)}, bf16[112,768]{1,0:T(8,128)(2,1)S(1)}, u32[]{:S(2)}, u32[]{:S(2)}) collective-permute-start(bf16[112,768]{1,0:T(8,128)(2,1)S(1)} %shard_map.294.refs_0_), channel_id=1, source_target_pairs={{0,16},{8,24},{16,0},{24,8},{1,17},{9,25},{17,1},{25,9},{2,18},{10... | collective-permute-start | bytes 516104 | tf_op jit(solution)/shard_map/ppermute | solution.py:580
  108.6 16.3 %collective-permute-start.26 = (bf16[192,768]{1,0:T(8,128)(2,1)S(1)}, bf16[192,768]{1,0:T(8,128)(2,1)S(1)}, u32[]{:S(2)}, u32[]{:S(2)}) collective-permute-start(bf16[192,768]{1,0:T(8,128)(2,1)S(1)} %shard_map.285.refs_0_), channel_id=1, source_target_pairs={{0,8},{8,0},{16,24},{24,16},{1,9},{9,1},{17,25},{25,17},{2,10},{10... | collective-permute-start | bytes 884744 | tf_op jit(solution)/shard_map/ppermute | solution.py:592
  109.7 19.9 %collective-permute-start.25 = (bf16[192,768]{1,0:T(8,128)(2,1)S(1)}, bf16[192,768]{1,0:T(8,128)(2,1)S(1)}, u32[]{:S(2)}, u32[]{:S(2)}) collective-permute-start(bf16[192,768]{1,0:T(8,128)(2,1)S(1)} %shard_map.292.refs_0_), channel_id=1, source_target_pairs={{0,8},{8,0},{16,24},{24,16},{1,9},{9,1},{17,25},{25,17},{2,10},{10... | collective-permute-start | bytes 884744 | tf_op jit(solution)/shard_map/ppermute | solution.py:592
  129.6 7.8 %collective-permute-start.32 = (bf16[192,768]{1,0:T(8,128)(2,1)S(1)}, bf16[192,768]{1,0:T(8,128)(2,1)S(1)}, u32[]{:S(2)}, u32[]{:S(2)}) collective-permute-start(bf16[192,768]{1,0:T(8,128)(2,1)S(1)} %collective-permute-done.25.refs_1_), channel_id=1, source_target_pairs={{0,1},{1,0},{2,3},{3,2},{4,5},{5,4},{6,7},{7,6},{8,9},{9,8},{10,11... | collective-permute-start | bytes 884744 | tf_op jit(solution)/shard_map/ppermute | solution.py:605
  129.7 10.0 %collective-permute-start.30 = (bf16[112,768]{1,0:T(8,128)(2,1)S(1)}, bf16[112,768]{1,0:T(8,128)(2,1)S(1)}, u32[]{:S(2)}, u32[]{:S(2)}) collective-permute-start(bf16[112,768]{1,0:T(8,128)(2,1)S(1)} %shard_map.298.refs_0_), channel_id=1, source_target_pairs={{0,8},{8,0},{16,24},{24,16},{1,9},{9,1},{17,25},{25,17},{2,10},{10... | collective-permute-start | bytes 516104 | tf_op jit(solution)/shard_map/ppermute | solution.py:592
  129.7 10.5 %collective-permute-start.33 = (bf16[128,768]{1,0:T(8,128)(2,1)S(1)}, bf16[128,768]{1,0:T(8,128)(2,1)S(1)}, u32[]{:S(2)}, u32[]{:S(2)}) collective-permute-start(bf16[128,768]{1,0:T(8,128)(2,1)S(1)} %shard_map.295), channel_id=1, source_target_pairs={{0,4},{2,6},{4,0},{6,2},{1,5},{3,7},{5,1},{7,3},{8,12},{10,14},{12... | collective-permute-start | bytes 589832 | tf_op jit(solution)/shard_map/ppermute | solution.py:831
  131.4 8.3 %collective-permute-start.31 = (bf16[96,768]{1,0:T(8,128)(2,1)S(1)}, bf16[96,768]{1,0:T(8,128)(2,1)S(1)}, u32[]{:S(2)}, u32[]{:S(2)}) collective-permute-start(bf16[96,768]{1,0:T(8,128)(2,1)S(1)} %shard_map.297.refs_4_), channel_id=1, source_target_pairs={{0,8},{8,0},{16,24},{24,16},{1,9},{9,1},{17,25},{25,17},{2,10},{10... | collective-permute-start | bytes 442376 | tf_op jit(solution)/shard_map/ppermute | solution.py:592
  139.7 1.6 %collective-permute-start.34 = (bf16[112,768]{1,0:T(8,128)(2,1)S(1)}, bf16[112,768]{1,0:T(8,128)(2,1)S(1)}, u32[]{:S(2)}, u32[]{:S(2)}) collective-permute-start(bf16[112,768]{1,0:T(8,128)(2,1)S(1)} %collective-permute-done.30.refs_1_), channel_id=1, source_target_pairs={{0,1},{1,0},{2,3},{3,2},{4,5},{5,4},{6,7},{7,6},{8,9},{9,8},{10,11... | collective-permute-start | bytes 516104 | tf_op jit(solution)/shard_map/ppermute | solution.py:605
  139.7 1.6 %collective-permute-start.35 = (bf16[96,768]{1,0:T(8,128)(2,1)S(1)}, bf16[96,768]{1,0:T(8,128)(2,1)S(1)}, u32[]{:S(2)}, u32[]{:S(2)}) collective-permute-start(bf16[96,768]{1,0:T(8,128)(2,1)S(1)} %collective-permute-done.31.refs_5_), channel_id=1, source_target_pairs={{0,1},{1,0},{2,3},{3,2},{4,5},{5,4},{6,7},{7,6},{8,9},{9,8},{10,11... | collective-permute-start | bytes 442376 | tf_op jit(solution)/shard_map/ppermute | solution.py:605
